TPU v7x, 32 devices: a whole 2x2x4 slice. The times are simulated.
32 devices in a mesh: groups: 2 (over y), wide: 4 (over z), narrow: 4 (over x, core).
Axes of the slice: x: 2, y: 2, z: 4, core: 2. Of those that a mesh axis runs over, the one named last changes fastest.
Arguments:
- tokens: bfloat16 [512, 4096], P(('groups', 'wide'), 'narrow'), parts along dimension 0, may hold values from -6 to 6
- routes: int32 [512, 8], P(('groups', 'wide')), parts along dimension 0, may hold values from 0 to 15, all different within a row; in each aligned block of 64 rows (0 to 63, 64 to 127, ...) at most 40 rows name the same one
- gate_weights: float32 [512, 8], P(('groups', 'wide')), parts along dimension 0, may hold values from 0.05 to 1
- delta_of: int32 [16], replicated, may hold values from 0 to 15, each once
- base_gate: bfloat16 [4096, 1536], P('wide', 'narrow'), may hold values from -0.09375 to 0.09375
- base_up: bfloat16 [4096, 1536], P('wide', 'narrow'), may hold values from -0.09375 to 0.09375
- base_down: bfloat16 [1536, 4096], P('wide', 'narrow'), may hold values from -0.15625 to 0.15625
- gate_left: bfloat16 [16, 4096, 32], P('wide', 'narrow'), may hold values from -0.09375 to 0.09375
- gate_right: bfloat16 [16, 32, 1536], P('wide', None, 'narrow'), may hold values from -0.5 to 0.5
- up_left: bfloat16 [16, 4096, 32], P('wide', 'narrow'), may hold values from -0.09375 to 0.09375
- up_right: bfloat16 [16, 32, 1536], P('wide', None, 'narrow'), may hold values from -0.5 to 0.5
- down_left: bfloat16 [16, 1536, 32], P('wide', 'narrow'), may hold values from -0.15625 to 0.15625
- down_right: bfloat16 [16, 32, 4096], P('wide', None, 'narrow'), may hold values from -0.5 to 0.5
Outputs:
- mixed_out: bfloat16 [512, 4096], P(('groups', 'wide'), 'narrow'), parts along dimension 0
There are 2 independent parts, one for each index of `groups`. A program takes and returns all parts, laid end to end along the dimension named above; an argument that names none is the same for every part. Nothing has to cross between parts.
Inputs may be any that keep to these rules, and one draw needn't show every extreme that they name: `routes`: in each aligned block of 64 rows (the rows of one index of wide) no expert is named by more than 40 rows, and in some block some expert is named by exactly 40 rows.
All inputs are finite; a program needn't handle non-finite values.
Results may differ from a plain program's by a relative error of at most 0.0053.
Values may be sent and summed in bfloat16 or wider, within the bound.
No kernel may reach another device: no remote copies, remote signals or barrier semaphores. Data moves between devices by JAX's collectives and lax.ppermute only.
A program may use at most 64 MiB of HBM per device.

v0:
```python
import jax
import jax.numpy as jnp
from jax import lax
from jax.sharding import PartitionSpec as P


def with_zero_row(rows):
    return jnp.concatenate([rows, jnp.zeros((1, rows.shape[1]), rows.dtype)], axis=0)


def rebuild(base_rows, left_rows, right_factor):
    product = jnp.einsum(
        "ecr,erf->ecf", left_rows, right_factor, preferred_element_type=jnp.float32
    )
    return (base_rows.astype(jnp.float32)[None] + product).astype(jnp.bfloat16)


def shards(
    tokens,
    routes,
    gate_weights,
    delta_of,
    base_gate,
    base_up,
    base_down,
    gate_left,
    gate_right,
    up_left,
    up_right,
    down_left,
    down_right,
):
    block_rows, top_count = routes.shape
    feature_part = tokens.shape[1]
    exp_here = gate_left.shape[0]
    wide_count = lax.axis_size("wide")
    experts = wide_count * exp_here
    capacity = max(2, block_rows * top_count * 5 // (4 * experts))
    slot_total = experts * capacity
    expert_ids = lax.broadcasted_iota(jnp.int32, (1, 1, experts), 2)
    onehot = (routes[:, :, None] == expert_ids).astype(jnp.float32)
    routed = jnp.sum(onehot, axis=1)
    row_index = lax.broadcasted_iota(jnp.int32, (block_rows, block_rows), 0)
    col_index = lax.broadcasted_iota(jnp.int32, (block_rows, block_rows), 1)
    earlier_mask = (col_index < row_index).astype(jnp.float32)
    before = jnp.dot(
        earlier_mask, routed, preferred_element_type=jnp.float32, precision=lax.Precision.HIGHEST
    )
    place_in = jnp.sum(onehot * before[:, None, :], axis=2).astype(jnp.int32)
    delta_ids = jnp.sum(onehot * delta_of.astype(jnp.float32)[None, None, :], axis=2).astype(
        jnp.int32
    )
    position = delta_ids * capacity + place_in
    every_row = lax.all_gather(tokens, "wide", axis=0, tiled=True)
    every_place = lax.all_gather(position, "wide", axis=0, tiled=True)
    own_first = lax.axis_index("wide") * (exp_here * capacity)
    local_place = every_place - own_first
    owned = (local_place >= 0) & (local_place < exp_here * capacity)
    block_ids = lax.broadcasted_iota(jnp.int32, every_place.shape, 0) // block_rows
    target = jnp.where(owned, block_ids * (exp_here * capacity) + local_place, slot_total)
    every_token = lax.broadcasted_iota(jnp.int32, every_place.shape, 0)
    picked_rows = (
        jnp.full((slot_total,), every_row.shape[0], jnp.int32)
        .at[target.reshape(-1)]
        .set(every_token.reshape(-1), mode="drop")
    )
    local_rows = jnp.take(with_zero_row(every_row), picked_rows, axis=0).reshape(
        wide_count, exp_here, capacity, feature_part
    )
    slot_rows = lax.all_gather(local_rows, "narrow", axis=3, tiled=True)
    left_gate, left_up, left_down = (
        lax.all_gather(gate_left, "narrow", axis=1, tiled=True),
        lax.all_gather(up_left, "narrow", axis=1, tiled=True),
        lax.all_gather(down_left, "narrow", axis=1, tiled=True),
    )
    base_rows_gate = lax.all_gather(base_gate, "wide", axis=0, tiled=True)
    base_rows_up = lax.all_gather(base_up, "wide", axis=0, tiled=True)
    columns = slot_rows
    dense_gate = rebuild(base_rows_gate, left_gate, gate_right)
    dense_up = rebuild(base_rows_up, left_up, up_right)
    gate_sum = jnp.einsum("secd,edf->secf", columns, dense_gate, preferred_element_type=jnp.float32)
    up_sum = jnp.einsum("secd,edf->secf", columns, dense_up, preferred_element_type=jnp.float32)
    hidden = (jax.nn.silu(gate_sum) * up_sum).astype(jnp.bfloat16)
    hidden_all = lax.all_gather(hidden, "narrow", axis=3, tiled=True)
    dense_down = rebuild(
        lax.all_gather(base_down, "wide", axis=0, tiled=True), left_down, down_right
    )
    columns = hidden_all
    expert_out = jnp.einsum(
        "secf,efd->secd", columns, dense_down, preferred_element_type=jnp.float32
    ).astype(jnp.bfloat16)
    returned = lax.all_to_all(expert_out, "wide", split_axis=0, concat_axis=0, tiled=True).reshape(
        slot_total, feature_part
    )
    picked = jnp.take(returned, position.reshape(-1), axis=0).reshape(
        block_rows, top_count, feature_part
    )
    mixed_out = jnp.sum(gate_weights[:, :, None] * picked.astype(jnp.float32), axis=1)
    return mixed_out.astype(jnp.bfloat16)


def solution(mesh):
    return jax.shard_map(
        shards,
        mesh=mesh,
        in_specs=(
            P(("groups", "wide"), "narrow"),
            P(("groups", "wide"), None),
            P(("groups", "wide"), None),
            P(),
            P("wide", "narrow"),
            P("wide", "narrow"),
            P("wide", "narrow"),
            P("wide", "narrow", None),
            P("wide", None, "narrow"),
            P("wide", "narrow", None),
            P("wide", None, "narrow"),
            P("wide", "narrow", None),
            P("wide", None, "narrow"),
        ),
        out_specs=P(("groups", "wide"), "narrow"),
        check_vma=False,
    )
```

profile of v0, /device:TPU:0, one launch (start us, length us, event | category | flops | bytes accessed | tf_op | source)
XLA Modules:
  0.0 368.1 jit_solution(3245689724304477766)
XLA Ops:
  6.5 0.0 copy-start
  6.5 0.0 all-gather.11.cloned.1.call-start
  6.5 0.7 all-gather.11.cloned.1.call-update
  7.3 0.0 all-gather.17.cloned.1.call-start
  7.3 0.7 all-gather.17.cloned.1.call-update
  8.0 0.0 all-gather.13.cloned.1.call-start
  8.1 0.7 all-gather.13.cloned.1.call-update
  8.7 0.0 all-gather.15.cloned.1.call-start
  8.8 0.7 convert_reduce_fusion
  9.5 0.1 fusion.32
  9.6 0.7 convert_element_type.70
  10.3 0.8 select_reduce_fusion.1
  11.1 14.8 %all-gather = s32[4,64,8]{1,2,0:T(8,128)S(1)} all-gather(s32[1,64,8]{1,2,0:T(8,128)S(1)} %bitcast.60), channel_id=1, replica_groups=mesh['groups'=2,'wide'=4,'narrow'=4] {'wide'}, dimensions={0}, use_global_device_ids=true | all-gather | bytes 10240 | tf_op jit(solution)/shard_map/all_gather | solution.py:55
  26.0 0.1 reshape.144
  26.1 0.1 copy.44
  26.2 0.1 reshape.113
  26.4 0.1 reshape.136
  26.5 8.0 %scatter_custom_fusion = s32[640]{0:T(1024)S(1)} fusion(s32[2048]{0:T(1024)S(1)} %bitcast.62, s32[2048]{0:T(1024)S(1)} %reshape.136, s32[]{:T(128)} %constant.61.clone.1), kind=kCustom, calls=%fused_computation.45 | custom fusion | bytes 2564 | tf_op jit(solution)/shard_map/scatter | solution.py:65
  34.6 0.1 broadcast_in_dim.43
  34.7 23.0 %all_gather.35 = bf16[256,1024]{1,0:T(8,128)(2,1)S(1)} all-gather(bf16[64,1024]{1,0:T(8,128)(2,1)} %param.13), channel_id=1, replica_groups=mesh['groups'=2,'wide'=4,'narrow'=4] {'wide'}, dimensions={0}, use_global_device_ids=true | all-gather | bytes 655360 | tf_op jit(solution)/shard_map/all_gather | solution.py:54
  57.8 2.8 gather_fusion
  60.6 1.4 copy_select_fusion
  62.0 0.0 all-gather.15.cloned.1.call-update
  62.0 0.0 all-gather.19.cloned.1.call-start
  62.0 0.5 all-gather.19.cloned.1.call-update
  62.6 0.0 all-gather.9.cloned.1.call-start
  62.6 0.5 all-gather.9.cloned.1.call-update
  63.2 0.0 all-gather.21.cloned.1.call-start
  63.2 20.3 %all-gather.11.cloned.1.call-done = bf16[4096,384]{1,0:T(8,128)(2,1)} async-done(((bf16[1024,384]{1,0:T(8,128)(2,1)}), bf16[4096,384]{1,0:T(8,128)(2,1)}) %all-gather.11.cloned.1.call-update) | async-done | bytes 3145744 | tf_op jit(solution)/shard_map/all_gather | solution.py:76
  83.5 4.9 %convert_element_type.76 = f32[4096,384]{1,0:T(8,128)} convert(bf16[4096,384]{1,0:T(8,128)(2,1)} %all-gather.11.cloned.1.call-done) | non-fusion elementwise | flops 1572864 | bytes 9437184 | tf_op jit(solution)/shard_map/convert_element_type | solution.py:15
  88.4 0.0 copy-start.3
  88.4 58.8 %all-gather.17.cloned.1.call-done = bf16[4096,384]{1,0:T(8,128)(2,1)} async-done(((bf16[1024,384]{1,0:T(8,128)(2,1)}), bf16[4096,384]{1,0:T(8,128)(2,1)}) %all-gather.17.cloned.1.call-update) | async-done | bytes 3145744 | tf_op jit(solution)/shard_map/all_gather | solution.py:77
  147.2 5.0 %convert_element_type.78 = f32[4096,384]{1,0:T(8,128)} convert(bf16[4096,384]{1,0:T(8,128)(2,1)} %all-gather.17.cloned.1.call-done) | non-fusion elementwise | flops 1572864 | bytes 9437184 | tf_op jit(solution)/shard_map/convert_element_type | solution.py:15
  152.2 0.0 copy-start.4
  152.2 12.0 %all-gather.13.cloned.1.call-done = bf16[4,4096,32]{1,2,0:T(8,128)(2,1)} async-done(((bf16[4,1024,32]{1,2,0:T(8,128)(2,1)}), bf16[4,4096,32]{1,2,0:T(8,128)(2,1)}) %all-gather.13.cloned.1.call-update) | async-done | bytes 1048592 | tf_op jit(solution)/shard_map/all_gather | solution.py:72
  164.2 41.9 %all-gather.15.cloned.1.call-done = bf16[4,4,40,4096]{3,2,0,1:T(8,128)(2,1)} async-done(((bf16[4,4,40,1024]{3,2,0,1:T(8,128)(2,1)}), bf16[4,4,40,4096]{3,2,0,1:T(8,128)(2,1)}) %all-gather.15.cloned.1.call-update) | async-done | bytes 5242896 | tf_op jit(solution)/shard_map/all_gather | solution.py:70
  206.1 0.0 copy-done.3
  206.1 10.2 %fusion.23 = f32[4,4,40,384]{3,2,0,1:T(8,128)S(1)} fusion(bf16[4,4,40,4096]{3,2,0,1:T(8,128)(2,1)} %all-gather.15.cloned.1.call-done, f32[4096,384]{1,0:T(8,128)} %convert_element_type.76, bf16[4,4096,32]{1,2,0:T(8,128)(2,1)} %all-gather.13.cloned.1.call-done, bf16[4,32,384]{2,1,0:T(8,128)(2,1)S(1)} %copy-done.3), kind=kOutput, calls=%fused_computation.20 | convolution fusion | flops 2428502016 | bytes 13664256 | tf_op jit(solution)/shard_map/secd,edf->secf/dot_general | solution.py:81
  216.3 0.0 copy-start.1
  216.3 8.0 %all-gather.19.cloned.1.call-done = bf16[4,4096,32]{1,2,0:T(8,128)(2,1)} async-done(((bf16[4,1024,32]{1,2,0:T(8,128)(2,1)}), bf16[4,4096,32]{1,2,0:T(8,128)(2,1)}) %all-gather.19.cloned.1.call-update) | async-done | bytes 1048592 | tf_op jit(solution)/shard_map/all_gather | solution.py:73
  224.2 0.0 copy-done.4
  224.2 10.9 %fusion.29 = bf16[4,4,40,384]{3,2,0,1:T(8,128)(2,1)} fusion(bf16[4,4,40,4096]{3,2,0,1:T(8,128)(2,1)} %all-gather.15.cloned.1.call-done, f32[4096,384]{1,0:T(8,128)} %convert_element_type.78, bf16[4,4096,32]{1,2,0:T(8,128)(2,1)} %all-gather.19.cloned.1.call-done, bf16[4,32,384]{2,1,0:T(8,128)(2,1)S(1)} %copy-done.4, f32[4,4,40,384]{3,2,0,1:T(8,128)S(1)} %fusion.23), kind=kOutput, calls=%fused_computation.23 | convolution fusion | flops 2429976576 | bytes 14155776 | tf_op jit(solution)/shard_map/secd,edf->secf/dot_general | solution.py:82
  235.2 0.0 all-gather.21.cloned.1.call-update
  235.2 0.0 copy-done.1
  235.2 6.6 %all_gather.31 = bf16[4,1536,32]{1,2,0:T(8,128)(2,1)S(1)} all-gather(bf16[4,384,32]{1,2,0:T(8,128)(2,1)S(1)} %copy-done.1), channel_id=1, replica_groups=mesh['groups'=2,'wide'=4,'narrow'=4] {'narrow'}, dimensions={1}, use_global_device_ids=true | all-gather | bytes 491520 | tf_op jit(solution)/shard_map/all_gather | solution.py:74
  241.8 47.4 %all-gather.9.cloned.1.call-done = bf16[1536,1024]{1,0:T(8,128)(2,1)} async-done(((bf16[384,1024]{1,0:T(8,128)(2,1)}), bf16[1536,1024]{1,0:T(8,128)(2,1)}) %all-gather.9.cloned.1.call-update) | async-done | bytes 3145744 | tf_op jit(solution)/shard_map/all_gather | solution.py:86
  289.2 5.3 %convert_element_type.74 = f32[1536,1024]{1,0:T(8,128)} convert(bf16[1536,1024]{1,0:T(8,128)(2,1)} %all-gather.9.cloned.1.call-done) | non-fusion elementwise | flops 1572864 | bytes 9437184 | tf_op jit(solution)/shard_map/convert_element_type | solution.py:15
  294.5 16.7 %all-gather.21.cloned.1.call-done = bf16[4,4,40,1536]{3,2,0,1:T(8,128)(2,1)} async-done(((bf16[4,4,40,384]{3,2,0,1:T(8,128)(2,1)}), bf16[4,4,40,1536]{3,2,0,1:T(8,128)(2,1)}) %all-gather.21.cloned.1.call-update) | async-done | bytes 1966096 | tf_op jit(solution)/shard_map/all_gather | solution.py:84
  311.3 0.0 copy-done
  311.3 8.9 %fusion.17 = bf16[4,4,40,1024]{3,2,0,1:T(8,128)(2,1)S(1)} fusion(bf16[4,4,40,1536]{3,2,0,1:T(8,128)(2,1)} %all-gather.21.cloned.1.call-done, bf16[4,1536,32]{1,2,0:T(8,128)(2,1)S(1)} %all_gather.31, bf16[4,32,1024]{2,1,0:T(8,128)(2,1)S(1)} %copy-done, f32[1536,1024]{1,0:T(8,128)} %convert_element_type.74), kind=kOutput, calls=%fused_computation.18 | convolution fusion | flops 2429157376 | bytes 10223616 | tf_op jit(solution)/shard_map/secf,efd->secd/dot_general | solution.py:89
  320.1 0.0 copy-start.2
  320.2 1.2 copy.47
  321.4 4.6 %all-to-all-start = ((bf16[4,4,40,1024]{3,2,1,0:T(8,128)(2,1)}), bf16[4,4,40,1024]{3,2,1,0:T(8,128)(2,1)S(1)}, u32[]{:S(2)}, u32[]{:S(2)}) async-start(bf16[4,4,40,1024]{3,2,1,0:T(8,128)(2,1)} %copy.47), calls=%async_computation | async-start | bytes 2621440 | tf_op jit(solution)/shard_map/all_to_all | solution.py:92
  326.0 0.1 copy.48
  326.1 0.1 add.110
  326.1 0.1 copy.42
  326.2 0.0 copy-done.2
  326.3 0.1 copy.41
  326.4 31.4 %all-to-all-done = bf16[4,4,40,1024]{3,2,1,0:T(8,128)(2,1)S(1)} async-done(((bf16[4,4,40,1024]{3,2,1,0:T(8,128)(2,1)}), bf16[4,4,40,1024]{3,2,1,0:T(8,128)(2,1)S(1)}, u32[]{:S(2)}, u32[]{:S(2)}) %all-to-all-start) | async-done | bytes 1310752 | tf_op jit(solution)/shard_map/all_to_all | solution.py:92
  357.7 2.0 gather_fusion.1
  359.8 1.5 multiply_reduce_fusion
  (15 shorter events, 0.1 us)
Async XLA Ops:
  6.5 304.7 %copy-start = (bf16[4,32,1024]{2,1,0:T(8,128)(2,1)S(1)}, bf16[4,32,1024]{2,1,0:T(8,128)(2,1)}, u32[]{:S(2)}) copy-start(bf16[4,32,1024]{2,1,0:T(8,128)(2,1)} %param.25) | copy-start | bytes 786436
  6.5 76.9 %all-gather.11.cloned.1.call-start = ((), (), s32[]{:S(2)}) async-start(), calls=%async_computation.2 | async-start | bytes 3932160 | tf_op jit(solution)/shard_map/all_gather | solution.py:76
  7.3 139.9 %all-gather.17.cloned.1.call-start = ((), (), s32[]{:S(2)}) async-start(), calls=%async_computation.5 | async-start | bytes 3932160 | tf_op jit(solution)/shard_map/all_gather | solution.py:77
  8.0 156.2 %all-gather.13.cloned.1.call-start = ((), (), s32[]{:S(2)}) async-start(), calls=%async_computation.3 | async-start | bytes 1310720 | tf_op jit(solution)/shard_map/all_gather | solution.py:72
  8.7 197.3 %all-gather.15.cloned.1.call-start = ((), (), s32[]{:S(2)}) async-start(), calls=%async_computation.4 | async-start | bytes 6553600 | tf_op jit(solution)/shard_map/all_gather | solution.py:70
  62.0 162.2 %all-gather.19.cloned.1.call-start = ((), (), s32[]{:S(2)}) async-start(), calls=%async_computation.6 | async-start | bytes 1310720 | tf_op jit(solution)/shard_map/all_gather | solution.py:73
  62.6 226.6 %all-gather.9.cloned.1.call-start = ((), (), s32[]{:S(2)}) async-start(), calls=%async_computation.1 | async-start | bytes 3932160 | tf_op jit(solution)/shard_map/all_gather | solution.py:86
  63.2 248.1 %all-gather.21.cloned.1.call-start = ((), (), s32[]{:S(2)}) async-start(), calls=%async_computation.7 | async-start | bytes 2457600 | tf_op jit(solution)/shard_map/all_gather | solution.py:84
  88.4 117.7 %copy-start.3 = (bf16[4,32,384]{2,1,0:T(8,128)(2,1)S(1)}, bf16[4,32,384]{2,1,0:T(8,128)(2,1)}, u32[]{:S(2)}) copy-start(bf16[4,32,384]{2,1,0:T(8,128)(2,1)} %param.21) | copy-start | bytes 294916
  152.2 72.1 %copy-start.4 = (bf16[4,32,384]{2,1,0:T(8,128)(2,1)S(1)}, bf16[4,32,384]{2,1,0:T(8,128)(2,1)}, u32[]{:S(2)}) copy-start(bf16[4,32,384]{2,1,0:T(8,128)(2,1)} %param.23) | copy-start | bytes 294916
  216.3 18.9 %copy-start.1 = (bf16[4,384,32]{1,2,0:T(8,128)(2,1)S(1)}, bf16[4,384,32]{1,2,0:T(8,128)(2,1)}, u32[]{:S(2)}) copy-start(bf16[4,384,32]{1,2,0:T(8,128)(2,1)} %param.24) | copy-start | bytes 294916
  320.1 6.1 %copy-start.2 = (f32[64,8]{0,1:T(8,128)S(1)}, f32[64,8]{0,1:T(8,128)}, u32[]{:S(2)}) copy-start(f32[64,8]{0,1:T(8,128)} %param.15) | copy-start | bytes 6148
  321.4 36.3 %all-to-all-start = ((bf16[4,4,40,1024]{3,2,1,0:T(8,128)(2,1)}), bf16[4,4,40,1024]{3,2,1,0:T(8,128)(2,1)S(1)}, u32[]{:S(2)}, u32[]{:S(2)}) async-start(bf16[4,4,40,1024]{3,2,1,0:T(8,128)(2,1)} %copy.47), calls=%async_computation | async-start | bytes 2621440 | tf_op jit(solution)/shard_map/all_to_all | solution.py:92
Sparse Core Ops, SparseCore 0:
  8.9 74.5 all-gather.10
  85.0 62.1 all-gather.16
  148.8 15.3 all-gather.12
  165.6 40.4 all-gather.14
  207.5 16.7 all-gather.18
  225.7 63.5 all-gather.8
  290.8 20.4 all-gather.20
where the time goes:
time: 368 us
  waiting for transfers between devices  240 us (65%)
  blocking collectives  44.5 us (12%)
  matrix products  30.1 us (8%)
  other arithmetic  20.3 us (6%)
  local copies, waits for them, and re-layouts  15.1 us (4%)
  between operations  13.7 us (4%)
  starting transfers between devices  4.84 us (1%)
    all_gather x1, waiting for transfers between devices, shards(): base_rows_up = lax.all_gather(base_up, 'wide', axis=0, tiled=True)  58.8 us
    all_gather x1, waiting for transfers between devices, shards(): lax.all_gather(base_down, 'wide', axis=0, tiled=True)  47.4 us
    all_gather x1, waiting for transfers between devices, shards(): slot_rows = lax.all_gather(local_rows, 'narrow', axis=3, tiled=True)  41.9 us
    all_to_all x1, waiting for transfers between devices, shards(): lax.all_to_all(expert_out, 'wide', split_axis=0, concat_axis=0, tiled=True)  31.4 us
    all_gather x1, blocking collectives, shards(): every_row = lax.all_gather(tokens, 'wide', axis=0, tiled=True)  23 us
    all_gather x1, waiting for transfers between devices, shards(): base_rows_gate = lax.all_gather(base_gate, 'wide', axis=0, tiled=True)  20.3 us
    all_gather x1, waiting for transfers between devices, shards(): hidden_all = lax.all_gather(hidden, 'narrow', axis=3, tiled=True)  16.7 us
    convert_element_type x3, other arithmetic, rebuild(): return (base_rows.astype(jnp.float32)[None] + product).astype(jnp.bfloat16)  15.2 us
  transfers between devices with their start and end apart: 8, of which 8 were waited for; matrix products, arithmetic and copies ran while one was open for 14% of the time, Pallas kernels for 0%

commit v1 on v0

--- a/solution.py
+++ b/solution.py
@@ -1,7 +1,14 @@
+import functools
+
 import jax
 import jax.numpy as jnp
 from jax import lax
+from jax.experimental import pallas as pl
+from jax.experimental.pallas import tpu as pltpu
 from jax.sharding import PartitionSpec as P
+
+F32 = jnp.float32
+BF16 = jnp.bfloat16
 
 
 def with_zero_row(rows):
@@ -15,7 +22,7 @@
     return (base_rows.astype(jnp.float32)[None] + product).astype(jnp.bfloat16)
 
 
-def shards(
+def gathered_shards(
     tokens,
     routes,
     gate_weights,
@@ -99,9 +106,192 @@
     return mixed_out.astype(jnp.bfloat16)
 
 
+def dot_rows(a, b):
+    return lax.dot_general(a, b, (((1,), (1,)), ((), ())), preferred_element_type=F32)
+
+
+def left_kernel(count, *refs):
+    xs, (lg, lu), outs = refs[:count], refs[count : count + 2], refs[count + 2 :]
+    cols = lg.shape[0]
+    for x, out in zip(xs, outs):
+        out[:, :cols] = dot_rows(x[...], lg[...]).astype(BF16)
+        out[:, cols:] = dot_rows(x[...], lu[...]).astype(BF16)
+
+
+def base_kernel(count, place, x, wg, wu, *refs):
+    outs, total = refs[:count], refs[count]
+    cols = wg.shape[1]
+    total[:, :cols] = jnp.dot(x[...], wg[...], preferred_element_type=F32)
+    total[:, cols:] = jnp.dot(x[...], wu[...], preferred_element_type=F32)
+    rows = outs[0].shape[0]
+    for k in range(count):
+        start = pl.multiple_of(lax.rem(place[0] + k, count) * rows, rows)
+        outs[k][...] = total[pl.ds(start, rows), :].astype(BF16)
+
+
+def hidden_kernel(count, held, *refs):
+    gs, (pls, weight), rs = refs[:count], refs[count : count + 2], refs[count + 2 : 2 * count + 2]
+    hsum, hl, *_ = refs[2 * count + 2 :]
+    rows, both = gs[0].shape
+    cols = both // 2
+    rank_cols = rs[0].shape[1]
+    rank = rank_cols // held
+    base = sum(g[...].astype(F32) for g in gs)
+    gate, up = base[:, :cols], base[:, cols:]
+    low = sum(pls[pl.ds(n * rows, rows), :].astype(F32) for n in range(pls.shape[0] // rows)).astype(BF16)
+    owner = lax.broadcasted_iota(jnp.int32, (rows, rank_cols), 1) // rank
+    acc = jnp.zeros((rows, cols), F32)
+    for k in range(count):
+        here = low[:, k * 2 * rank_cols : (k + 1) * 2 * rank_cols]
+        low_gate, low_up = here[:, :rank_cols], here[:, rank_cols:]
+        zero = jnp.zeros_like(low_gate)
+        lhs_gate = jnp.concatenate([jnp.where(owner == i, low_gate, zero) for i in range(held)], axis=0)
+        lhs_up = jnp.concatenate([jnp.where(owner == i, low_up, zero) for i in range(held)], axis=0)
+        g = jnp.dot(lhs_gate, rs[k][0], preferred_element_type=F32)
+        u = jnp.dot(lhs_up, rs[k][1], preferred_element_type=F32)
+        parts = []
+        for i in range(held):
+            gi = gate + g[i * rows : (i + 1) * rows]
+            ui = up + u[i * rows : (i + 1) * rows]
+            h = (gi / (1.0 + jnp.exp(-gi))) * ui
+            slot = k * held + i
+            hw = h * weight[:, slot : slot + 1]
+            acc += hw
+            parts.append(hw.astype(BF16))
+        back = dot_rows(jnp.concatenate(parts, axis=0), rs[k][2])
+        block = jnp.zeros((rows, rank_cols), F32)
+        for i in range(held):
+            block += jnp.where(owner == i, back[i * rows : (i + 1) * rows], 0.0)
+        hl[k] = block.astype(BF16)
+    hsum[...] = acc.astype(BF16)
+
+
+def down_kernel(count, place, hs, w, rd, *refs):
+    outs, total = refs[:count], refs[count]
+    rows = outs[0].shape[0]
+    inner = w.shape[0]
+    rank_cols = rd.shape[0]
+    low = sum(hs[pl.ds(n * rows, rows), inner:].astype(F32) for n in range(hs.shape[0] // rows)).astype(BF16)
+    total[...] = jnp.dot(hs[:, :inner], w[...], preferred_element_type=F32)
+    low_rows = jnp.concatenate(
+        [low[:, j * rank_cols : (j + 1) * rank_cols] for j in ((count - k) % count for k in range(count))], axis=0
+    )
+    added = jnp.dot(low_rows, rd[...], preferred_element_type=F32)
+    for k in range(count):
+        start = pl.multiple_of(lax.rem(place[0] + k, count) * rows, rows)
+        outs[k][...] = (total[pl.ds(start, rows), :] + added[k * rows : (k + 1) * rows]).astype(BF16)
+
+
+VMEM = pl.BlockSpec(memory_space=pltpu.VMEM)
+SMEM = pl.BlockSpec(memory_space=pltpu.SMEM)
+PARAMS = pltpu.CompilerParams(vmem_limit_bytes=24 * 2**20)
+
+
+def along(axis, count, step):
+    return lambda a: lax.ppermute(a, axis, [(i, (i + step) % count) for i in range(count)])
+
+
+def stationary_shards(
+    tokens,
+    routes,
+    gate_weights,
+    delta_of,
+    base_gate,
+    base_up,
+    base_down,
+    gate_left,
+    gate_right,
+    up_left,
+    up_right,
+    down_left,
+    down_right,
+):
+    count = lax.axis_size("wide")
+    rows, top_count = routes.shape
+    held, rank = gate_left.shape[0], gate_left.shape[2]
+    experts = held * count
+    rank_cols = held * rank
+    inner = base_gate.shape[1]
+    features = base_down.shape[1]
+    place = lax.axis_index("wide")
+    place_arr = place[None].astype(jnp.int32)
+
+    def swap(a):
+        return lax.ppermute(
+            a, ("wide", "narrow"), [(i * count + j, j * count + i) for i in range(count) for j in range(count)]
+        )
+
+    def spread(parts, sign):
+        return [parts[0]] + [along("wide", count, sign * k)(parts[k]) for k in range(1, count)]
+
+    own_features = lax.all_gather(swap(tokens), "narrow", axis=0, tiled=True)
+    blocks = spread([tokens] * count, 1)
+
+    packed = jnp.stack(
+        [
+            gate_right.reshape(rank_cols, inner),
+            up_right.reshape(rank_cols, inner),
+            jnp.swapaxes(down_left, 1, 2).reshape(rank_cols, inner),
+        ]
+    )
+    factors = spread([packed] * count, -1)
+
+    expert_ids = lax.broadcasted_iota(jnp.int32, (1, 1, experts), 2)
+    named = routes[:, :, None] == expert_ids
+    delta_ids = jnp.sum(jnp.where(named, delta_of[None, None, :], 0), axis=2)
+    slots = lax.rem(delta_ids - place * held + experts, experts)
+    weight = jnp.sum(jnp.where(slots[:, :, None] == expert_ids, gate_weights[:, :, None], 0.0), axis=1)
+
+    left_t = [jnp.swapaxes(a, 1, 2).reshape(rank_cols, a.shape[1]) for a in (gate_left, up_left)]
+    low = pl.pallas_call(
+        functools.partial(left_kernel, count),
+        out_shape=[jax.ShapeDtypeStruct((rows, 2 * rank_cols), BF16)] * count,
+        in_specs=[VMEM] * (count + 2),
+        out_specs=[VMEM] * count,
+        compiler_params=PARAMS,
+    )(*blocks, *left_t)
+    low = jnp.concatenate(spread(low, -1), axis=1)
+    low = lax.all_gather(low, "narrow", axis=0, tiled=True)
+
+    sums = pl.pallas_call(
+        functools.partial(base_kernel, count),
+        out_shape=[jax.ShapeDtypeStruct((rows, 2 * inner), BF16)] * count,
+        in_specs=[SMEM] + [VMEM] * 3,
+        out_specs=[VMEM] * count,
+        scratch_shapes=[pltpu.VMEM((count * rows, 2 * inner), F32)],
+        compiler_params=PARAMS,
+    )(place_arr, own_features, base_gate, base_up)
+    sums = spread(sums, 1)
+
+    hsum, hl = pl.pallas_call(
+        functools.partial(hidden_kernel, count, held),
+        out_shape=[
+            jax.ShapeDtypeStruct((rows, inner), BF16),
+            jax.ShapeDtypeStruct((count, rows, rank_cols), BF16),
+        ],
+        in_specs=[VMEM] * (2 * count + 2),
+        out_specs=[VMEM] * 2,
+        compiler_params=PARAMS,
+    )(*sums, low, weight, *factors)
+
+    hs = jnp.concatenate([swap(hsum)] + spread([hl[k] for k in range(count)], 1), axis=1)
+    hs = lax.all_gather(hs, "narrow", axis=0, tiled=True)
+    outs = pl.pallas_call(
+        functools.partial(down_kernel, count),
+        out_shape=[jax.ShapeDtypeStruct((rows, features), BF16)] * count,
+        in_specs=[SMEM] + [VMEM] * 3,
+        out_specs=[VMEM] * count,
+        scratch_shapes=[pltpu.VMEM((count * rows, features), F32)],
+        compiler_params=PARAMS,
+    )(place_arr, hs, base_down, down_right.reshape(rank_cols, features))
+    outs = spread(outs, 1)
+    return sum(o.astype(F32) for o in outs).astype(BF16)
+
+
 def solution(mesh):
+    square = mesh.shape["wide"] == mesh.shape["narrow"]
     return jax.shard_map(
-        shards,
+        stationary_shards if square else gathered_shards,
         mesh=mesh,
         in_specs=(
             P(("groups", "wide"), "narrow"),

time: 368 us -> 99.1 us (0.27)
  waiting for transfers between devices: 240 us -> 20.8 us
  starting transfers between devices: 4.84 us -> 47.7 us
  matrix products: 30.1 us -> 0 us
  blocking collectives: 44.5 us -> 22.6 us
  other arithmetic: 20.3 us -> 3.34 us
  local copies, waits for them, and re-layouts: 15.1 us -> 0.17 us
  between operations: 13.7 us -> 0.17 us
    all_gather x7 -> x0, waiting for transfers between devices: 205 us -> none  [the longest x1 58.8 us: shards(): base_rows_up = lax.all_gather(base_up, 'wide', axis=0, tiled=True)]
    ppermute x0 -> x20, starting transfers between devices: none -> 47.7 us  [the longest x18 45.4 us: along(): lax.ppermute(a, axis, [(i, (i + step) % count) for i in range(count)])]
    all_to_all x1 -> x0, waiting for transfers between devices: 31.4 us -> none  [shards(): lax.all_to_all(expert_out, 'wide', split_axis=0, concat_axis=0, tiled=True)]
    dot_general x4 -> x0, matrix products: 30.1 us -> none  [the longest x1 10.9 us: shards(): jnp.einsum('secd,edf->secf', columns, dense_up, preferred_element_type=jn...]
    all_gather x3, blocking collectives: 44.5 us -> 22.6 us  [the longest x1 9.77 us: stationary_shards(): own_features = lax.all_gather(swap(tokens), 'narrow', axis=0, tiled=True)]
    ppermute x0 -> x20, waiting for transfers between devices: none -> 20.8 us  [the longest x18 20.8 us: along(): lax.ppermute(a, axis, [(i, (i + step) % count) for i in range(count)])]
    convert_element_type x4 -> x1, other arithmetic: 15.9 us -> 0.73 us  [stationary_shards(): return sum((o.astype(F32) for o in outs)).astype(BF16)]
    scatter x1 -> x0, local copies, waits for them, and re-layouts: 8.04 us -> none  [shards(): picked_rows = jnp.full((slot_total,), every_row.shape[0], jnp.int32).at[t...]
  transfers between devices with their start and end apart: 8 -> 20, of which waited for: 8 -> 6; matrix products, arithmetic and copies ran while one was open for 14% -> 3% of each run, Pallas kernels for 0% -> 2%
where the time goes in v1:
time: 99.1 us; the launch traced here: 98.4 us
  starting transfers between devices  47.7 us (48%)
  blocking collectives  22.6 us (23%)
  waiting for transfers between devices  20.8 us (21%)
  Pallas kernels  3.53 us (4%)
  other arithmetic  3.34 us (3%)
    ppermute x18, starting transfers between devices, along(): lax.ppermute(a, axis, [(i, (i + step) % count) for i in range(count)])  45.4 us
    ppermute x18, waiting for transfers between devices, along(): lax.ppermute(a, axis, [(i, (i + step) % count) for i in range(count)])  20.8 us
    all_gather x1, blocking collectives, stationary_shards(): own_features = lax.all_gather(swap(tokens), 'narrow', axis=0, tiled=True)  9.77 us
    all_gather x1, blocking collectives, stationary_shards(): low = lax.all_gather(low, 'narrow', axis=0, tiled=True)  6.5 us
    all_gather x1, blocking collectives, stationary_shards(): hs = lax.all_gather(hs, 'narrow', axis=0, tiled=True)  6.31 us
    ppermute x2, starting transfers between devices, swap(): lax.ppermute(a, ('wide', 'narrow'), [(i * count + j, j * count + i) for i...  2.35 us
  transfers between devices with their start and end apart: 20, of which 6 were waited for; matrix products, arithmetic and copies ran while one was open for 3% of the time, Pallas kernels for 2%

profile of v1, /device:TPU:0, one launch (start us, length us, event | category | flops | bytes accessed | tf_op | source)
XLA Modules:
  0.0 98.4 jit_solution(18191993517461912863)
XLA Ops:
  0.0 3.0 %collective-permute-start.4 = (bf16[64,1024]{1,0:T(8,128)(2,1)}, bf16[64,1024]{1,0:T(8,128)(2,1)S(1)}, u32[]{:S(2)}, u32[]{:S(2)}) collective-permute-start(bf16[64,1024]{1,0:T(8,128)(2,1)} %refs_0_.1), channel_id=1, source_target_pairs={{0,4},{4,8},{8,12},{12,0},{1,5},{5,9},{9,13},{13,1},{2,6},{6,10},{... | collective-permute-start | bytes 393224 | tf_op jit(solution)/shard_map/ppermute | solution.py:191
  3.0 2.6 %collective-permute-start.5 = (bf16[64,1024]{1,0:T(8,128)(2,1)}, bf16[64,1024]{1,0:T(8,128)(2,1)S(1)}, u32[]{:S(2)}, u32[]{:S(2)}) collective-permute-start(bf16[64,1024]{1,0:T(8,128)(2,1)} %refs_0_.1), channel_id=1, source_target_pairs={{0,8},{4,12},{8,0},{12,4},{1,9},{5,13},{9,1},{13,5},{2,10},{6,14},... | collective-permute-start | bytes 393224 | tf_op jit(solution)/shard_map/ppermute | solution.py:191
  5.6 1.3 %collective-permute-start.6 = (bf16[64,1024]{1,0:T(8,128)(2,1)}, bf16[64,1024]{1,0:T(8,128)(2,1)S(1)}, u32[]{:S(2)}, u32[]{:S(2)}) collective-permute-start(bf16[64,1024]{1,0:T(8,128)(2,1)} %refs_0_.1), channel_id=1, source_target_pairs={{0,12},{4,0},{8,4},{12,8},{1,13},{5,1},{9,5},{13,9},{2,14},{6,2},{... | collective-permute-start | bytes 393224 | tf_op jit(solution)/shard_map/ppermute | solution.py:191
  7.0 1.6 %collective-permute-start = (bf16[64,1024]{1,0:T(8,128)(2,1)}, bf16[64,1024]{1,0:T(8,128)(2,1)S(1)}, u32[]{:S(2)}, u32[]{:S(2)}) collective-permute-start(bf16[64,1024]{1,0:T(8,128)(2,1)} %refs_0_.1), channel_id=1, source_target_pairs={{0,0},{1,4},{2,8},{3,12},{4,1},{5,5},{6,9},{7,13},{8,2},{9,6},{10,... | collective-permute-start | bytes 393224 | tf_op jit(solution)/shard_map/ppermute | solution.py:220
  8.5 0.0 copy-start.3
  8.5 1.1 %pad_maximum_fusion.refs_6_ = bf16[3,128,384]{2,1,0:T(8,128)(2,1)S(1)} fusion(bf16[1,128,384]{2,1,0:T(8,128)(2,1)} %bitcast.24, bf16[1,128,384]{2,1,0:T(8,128)(2,1)} %bitcast.25, bf16[1,128,384]{2,1,0:T(8,128)(2,1)} %bitcast.26), kind=kLoop, calls=%fused_computation | loop fusion | flops 294912 | bytes 589824 | tf_op jit(solution)/shard_map/stack | solution.py:230
  9.6 3.8 %collective-permute-start.10 = (bf16[3,128,384]{2,1,0:T(8,128)(2,1)S(1)}, bf16[3,128,384]{2,1,0:T(8,128)(2,1)S(1)}, u32[]{:S(2)}, u32[]{:S(2)}) collective-permute-start(bf16[3,128,384]{2,1,0:T(8,128)(2,1)S(1)} %pad_maximum_fusion.refs_6_), channel_id=1, source_target_pairs={{0,12},{4,0},{8,4},{12,8},{1,13},{5,1},{9,5},{13,9},{2,14},{6,2},{... | collective-permute-start | bytes 884744 | tf_op jit(solution)/shard_map/ppermute | solution.py:191
  13.4 0.8 select_reduce_fusion.1
  14.2 0.7 select_reduce_fusion
  14.9 0.1 copy.16.refs_5_
  15.0 0.0 collective-permute-done.4.refs_1_
  15.0 1.3 %collective-permute-start.11 = (bf16[3,128,384]{2,1,0:T(8,128)(2,1)S(1)}, bf16[3,128,384]{2,1,0:T(8,128)(2,1)S(1)}, u32[]{:S(2)}, u32[]{:S(2)}) collective-permute-start(bf16[3,128,384]{2,1,0:T(8,128)(2,1)S(1)} %pad_maximum_fusion.refs_6_), channel_id=1, source_target_pairs={{0,8},{4,12},{8,0},{12,4},{1,9},{5,13},{9,1},{13,5},{2,10},{6,14},... | collective-permute-start | bytes 884744 | tf_op jit(solution)/shard_map/ppermute | solution.py:191
  16.2 0.0 collective-permute-done.5.refs_2_
  16.3 0.0 collective-permute-done.6.refs_3_
  16.3 0.0 copy-done.3
  16.3 0.0 copy-done.4
  16.3 0.0 copy-done.6
  16.3 0.0 copy-start
  16.3 0.0 copy-start.1
  16.3 0.8 shard_map.128
  17.1 16.4 %collective-permute-start.7 = (bf16[64,256]{1,0:T(8,128)(2,1)S(1)}, bf16[64,256]{1,0:T(8,128)(2,1)S(1)}, u32[]{:S(2)}, u32[]{:S(2)}) collective-permute-start(bf16[64,256]{1,0:T(8,128)(2,1)S(1)} %get-tuple-element.24), channel_id=1, source_target_pairs={{0,12},{4,0},{8,4},{12,8},{1,13},{5,1},{9,5},{13,9},{2,14},{6,2},{... | collective-permute-start | bytes 98312 | tf_op jit(solution)/shard_map/ppermute | solution.py:191
  33.5 0.0 collective-permute-start.8
  33.5 0.0 collective-permute-done
  33.5 0.6 collective-permute-start.9
  34.2 9.8 %all_gather.9.x = bf16[256,1024]{1,0:T(8,128)(2,1)S(1)} all-gather(bf16[64,1024]{1,0:T(8,128)(2,1)S(1)} %collective-permute-done), channel_id=1, replica_groups=mesh['groups'=2,'wide'=4,'narrow'=4] {'narrow'}, dimensions={0}, use_global_device_ids=true | all-gather | bytes 655360 | tf_op jit(solution)/shard_map/all_gather | solution.py:227
  44.0 0.0 copy-done
  44.0 0.0 copy-done.1
  44.0 0.8 shard_map.127
  44.8 0.0 collective-permute-done.7
  44.8 1.4 %collective-permute-start.12 = (bf16[3,128,384]{2,1,0:T(8,128)(2,1)S(1)}, bf16[3,128,384]{2,1,0:T(8,128)(2,1)S(1)}, u32[]{:S(2)}, u32[]{:S(2)}) collective-permute-start(bf16[3,128,384]{2,1,0:T(8,128)(2,1)S(1)} %pad_maximum_fusion.refs_6_), channel_id=1, source_target_pairs={{0,4},{4,8},{8,12},{12,0},{1,5},{5,9},{9,13},{13,1},{2,6},{6,10},{... | collective-permute-start | bytes 884744 | tf_op jit(solution)/shard_map/ppermute | solution.py:191
  46.1 0.0 collective-permute-done.8
  46.1 0.1 collective-permute-start.1
  46.2 0.0 collective-permute-done.9
  46.2 3.0 %collective-permute-start.2 = (bf16[64,768]{1,0:T(8,128)(2,1)S(1)}, bf16[64,768]{1,0:T(8,128)(2,1)S(1)}, u32[]{:S(2)}, u32[]{:S(2)}) collective-permute-start(bf16[64,768]{1,0:T(8,128)(2,1)S(1)} %get-tuple-element.21), channel_id=1, source_target_pairs={{0,8},{4,12},{8,0},{12,4},{1,9},{5,13},{9,1},{13,5},{2,10},{6,14},... | collective-permute-start | bytes 294920 | tf_op jit(solution)/shard_map/ppermute | solution.py:191
  49.2 9.4 %collective-permute-done.1.refs_1_ = bf16[64,768]{1,0:T(8,128)(2,1)S(1)} collective-permute-done((bf16[64,768]{1,0:T(8,128)(2,1)S(1)}, bf16[64,768]{1,0:T(8,128)(2,1)S(1)}, u32[]{:S(2)}, u32[]{:S(2)}) %collective-permute-start.1) | collective-permute-done | bytes 98336 | tf_op jit(solution)/shard_map/ppermute | solution.py:191
  58.6 0.0 collective-permute-start.3
  58.6 6.5 %all_gather.10.refs_4_ = bf16[256,1024]{1,0:T(8,128)(2,1)S(1)} all-gather(bf16[64,1024]{1,0:T(8,128)(2,1)S(1)} %pad_maximum_fusion.1), channel_id=1, replica_groups=mesh['groups'=2,'wide'=4,'narrow'=4] {'narrow'}, dimensions={0}, use_global_device_ids=true | all-gather | bytes 655360 | tf_op jit(solution)/shard_map/all_gather | solution.py:254
  65.1 0.0 collective-permute-done.2.refs_2_
  65.1 0.0 collective-permute-done.3.refs_3_
  65.2 0.0 collective-permute-done.10.refs_7_
  65.2 0.0 collective-permute-done.11.refs_8_
  65.2 0.0 collective-permute-done.12.refs_9_
  65.2 0.0 copy-start.5
  65.2 1.3 %shard_map.129 = (bf16[64,384]{1,0:T(8,128)(2,1)S(1)}, bf16[4,64,128]{2,1,0:T(8,128)(2,1)S(1)}) custom-call(bf16[64,768]{1,0:T(8,128)(2,1)S(1)} %get-tuple-element.19.refs_0_, bf16[64,768]{1,0:T(8,128)(2,1)S(1)} %collective-permute-done.1.refs_1_, bf16[64,768]{1,0:T(8,128)(2,1)S(1)} %collective-permute-done.2.refs_2_, ...), custom_call_target="tpu_custom_call" | custom-call | tf_op jit(solution)/shard_map/pallas_call | solution.py:266
  66.5 0.0 copy-start.2
  66.6 0.8 collective-permute-start.13
  67.4 3.3 %collective-permute-start.14 = (bf16[64,128]{1,0:T(8,128)(2,1)S(1)}, bf16[64,128]{1,0:T(8,128)(2,1)S(1)}, u32[]{:S(2)}, u32[]{:S(2)}) collective-permute-start(bf16[64,128]{1,0:T(8,128)(2,1)S(1)} %get-tuple-element.35), channel_id=1, source_target_pairs={{0,4},{4,8},{8,12},{12,0},{1,5},{5,9},{9,13},{13,1},{2,6},{6,10},{... | collective-permute-start | bytes 49160 | tf_op jit(solution)/shard_map/ppermute | solution.py:191
  70.7 3.0 %collective-permute-start.15 = (bf16[64,128]{1,0:T(8,128)(2,1)S(1)}, bf16[64,128]{1,0:T(8,128)(2,1)S(1)}, u32[]{:S(2)}, u32[]{:S(2)}) collective-permute-start(bf16[64,128]{1,0:T(8,128)(2,1)S(1)} %get-tuple-element.34), channel_id=1, source_target_pairs={{0,8},{4,12},{8,0},{12,4},{1,9},{5,13},{9,1},{13,5},{2,10},{6,14},... | collective-permute-start | bytes 49160 | tf_op jit(solution)/shard_map/ppermute | solution.py:191
  73.7 1.5 %collective-permute-start.16 = (bf16[64,128]{1,0:T(8,128)(2,1)S(1)}, bf16[64,128]{1,0:T(8,128)(2,1)S(1)}, u32[]{:S(2)}, u32[]{:S(2)}) collective-permute-start(bf16[64,128]{1,0:T(8,128)(2,1)S(1)} %get-tuple-element.33), channel_id=1, source_target_pairs={{0,12},{4,0},{8,4},{12,8},{1,13},{5,1},{9,5},{13,9},{2,14},{6,2},{... | collective-permute-start | bytes 49160 | tf_op jit(solution)/shard_map/ppermute | solution.py:191
  75.2 0.0 collective-permute-done.13
  75.2 0.8 collective-permute-done.14
  76.0 0.6 collective-permute-done.15
  76.7 0.7 collective-permute-done.16
  77.4 6.3 %all_gather.11.hs = bf16[256,896]{1,0:T(8,128)(2,1)S(1)} all-gather(bf16[64,896]{1,0:T(8,128)(2,1)S(1)} %constant_dynamic-update-slice_fusion), channel_id=1, replica_groups=mesh['groups'=2,'wide'=4,'narrow'=4] {'narrow'}, dimensions={0}, use_global_device_ids=true | all-gather | bytes 573440 | tf_op jit(solution)/shard_map/all_gather | solution.py:278
  83.7 0.0 copy-done.5
  83.7 0.0 copy-done.2
  83.8 0.6 shard_map.130
  84.3 1.7 %collective-permute-start.17 = (bf16[64,1024]{1,0:T(8,128)(2,1)S(1)}, bf16[64,1024]{1,0:T(8,128)(2,1)S(1)}, u32[]{:S(2)}, u32[]{:S(2)}) collective-permute-start(bf16[64,1024]{1,0:T(8,128)(2,1)S(1)} %get-tuple-element.30), channel_id=1, source_target_pairs={{0,4},{4,8},{8,12},{12,0},{1,5},{5,9},{9,13},{13,1},{2,6},{6,10},{... | collective-permute-start | bytes 393224 | tf_op jit(solution)/shard_map/ppermute | solution.py:191
  86.0 2.3 %collective-permute-start.18 = (bf16[64,1024]{1,0:T(8,128)(2,1)S(1)}, bf16[64,1024]{1,0:T(8,128)(2,1)S(1)}, u32[]{:S(2)}, u32[]{:S(2)}) collective-permute-start(bf16[64,1024]{1,0:T(8,128)(2,1)S(1)} %get-tuple-element.31), channel_id=1, source_target_pairs={{0,8},{4,12},{8,0},{12,4},{1,9},{5,13},{9,1},{13,5},{2,10},{6,14},... | collective-permute-start | bytes 393224 | tf_op jit(solution)/shard_map/ppermute | solution.py:191
  88.3 0.2 collective-permute-start.19
  88.4 4.2 %collective-permute-done.17 = bf16[64,1024]{1,0:T(8,128)(2,1)S(1)} collective-permute-done((bf16[64,1024]{1,0:T(8,128)(2,1)S(1)}, bf16[64,1024]{1,0:T(8,128)(2,1)S(1)}, u32[]{:S(2)}, u32[]{:S(2)}) %collective-permute-start.17) | collective-permute-done | bytes 131104 | tf_op jit(solution)/shard_map/ppermute | solution.py:191
  92.6 5.0 %collective-permute-done.18 = bf16[64,1024]{1,0:T(8,128)(2,1)S(1)} collective-permute-done((bf16[64,1024]{1,0:T(8,128)(2,1)S(1)}, bf16[64,1024]{1,0:T(8,128)(2,1)S(1)}, u32[]{:S(2)}, u32[]{:S(2)}) %collective-permute-start.18) | collective-permute-done | bytes 131104 | tf_op jit(solution)/shard_map/ppermute | solution.py:191
  97.6 0.0 collective-permute-done.19
  97.6 0.7 add_convert_fusion
  (10 shorter events, 0.1 us)
Async XLA Ops:
  0.0 15.0 %collective-permute-start.4 = (bf16[64,1024]{1,0:T(8,128)(2,1)}, bf16[64,1024]{1,0:T(8,128)(2,1)S(1)}, u32[]{:S(2)}, u32[]{:S(2)}) collective-permute-start(bf16[64,1024]{1,0:T(8,128)(2,1)} %refs_0_.1), channel_id=1, source_target_pairs={{0,4},{4,8},{8,12},{12,0},{1,5},{5,9},{9,13},{13,1},{2,6},{6,10},{... | collective-permute-start | bytes 393224 | tf_op jit(solution)/shard_map/ppermute | solution.py:191
  3.0 13.2 %collective-permute-start.5 = (bf16[64,1024]{1,0:T(8,128)(2,1)}, bf16[64,1024]{1,0:T(8,128)(2,1)S(1)}, u32[]{:S(2)}, u32[]{:S(2)}) collective-permute-start(bf16[64,1024]{1,0:T(8,128)(2,1)} %refs_0_.1), channel_id=1, source_target_pairs={{0,8},{4,12},{8,0},{12,4},{1,9},{5,13},{9,1},{13,5},{2,10},{6,14},... | collective-permute-start | bytes 393224 | tf_op jit(solution)/shard_map/ppermute | solution.py:191
  5.6 10.6 %collective-permute-start.6 = (bf16[64,1024]{1,0:T(8,128)(2,1)}, bf16[64,1024]{1,0:T(8,128)(2,1)S(1)}, u32[]{:S(2)}, u32[]{:S(2)}) collective-permute-start(bf16[64,1024]{1,0:T(8,128)(2,1)} %refs_0_.1), channel_id=1, source_target_pairs={{0,12},{4,0},{8,4},{12,8},{1,13},{5,1},{9,5},{13,9},{2,14},{6,2},{... | collective-permute-start | bytes 393224 | tf_op jit(solution)/shard_map/ppermute | solution.py:191
  7.0 26.6 %collective-permute-start = (bf16[64,1024]{1,0:T(8,128)(2,1)}, bf16[64,1024]{1,0:T(8,128)(2,1)S(1)}, u32[]{:S(2)}, u32[]{:S(2)}) collective-permute-start(bf16[64,1024]{1,0:T(8,128)(2,1)} %refs_0_.1), channel_id=1, source_target_pairs={{0,0},{1,4},{2,8},{3,12},{4,1},{5,5},{6,9},{7,13},{8,2},{9,6},{10,... | collective-permute-start | bytes 393224 | tf_op jit(solution)/shard_map/ppermute | solution.py:220
  8.5 7.7 %copy-start.3 = (bf16[4,1024,32]{1,2,0:T(8,128)(2,1)S(1)}, bf16[4,1024,32]{1,2,0:T(8,128)(2,1)}, u32[]{:S(2)}) copy-start(bf16[4,1024,32]{1,2,0:T(8,128)(2,1)} %param.20) | copy-start | bytes 786436
  8.5 7.7 %copy-start.4 = (bf16[4,1024,32]{1,2,0:T(8,128)(2,1)S(1)}, bf16[4,1024,32]{1,2,0:T(8,128)(2,1)}, u32[]{:S(2)}) copy-start(bf16[4,1024,32]{1,2,0:T(8,128)(2,1)} %param.22) | copy-start | bytes 786436
  8.5 7.8 %copy-start.6 = (bf16[64,1024]{1,0:T(8,128)(2,1)S(1)}, bf16[64,1024]{1,0:T(8,128)(2,1)}, u32[]{:S(2)}) copy-start(bf16[64,1024]{1,0:T(8,128)(2,1)} %refs_0_.1) | copy-start | bytes 393220
  9.6 55.5 %collective-permute-start.10 = (bf16[3,128,384]{2,1,0:T(8,128)(2,1)S(1)}, bf16[3,128,384]{2,1,0:T(8,128)(2,1)S(1)}, u32[]{:S(2)}, u32[]{:S(2)}) collective-permute-start(bf16[3,128,384]{2,1,0:T(8,128)(2,1)S(1)} %pad_maximum_fusion.refs_6_), channel_id=1, source_target_pairs={{0,12},{4,0},{8,4},{12,8},{1,13},{5,1},{9,5},{13,9},{2,14},{6,2},{... | collective-permute-start | bytes 884744 | tf_op jit(solution)/shard_map/ppermute | solution.py:191
  15.0 50.2 %collective-permute-start.11 = (bf16[3,128,384]{2,1,0:T(8,128)(2,1)S(1)}, bf16[3,128,384]{2,1,0:T(8,128)(2,1)S(1)}, u32[]{:S(2)}, u32[]{:S(2)}) collective-permute-start(bf16[3,128,384]{2,1,0:T(8,128)(2,1)S(1)} %pad_maximum_fusion.refs_6_), channel_id=1, source_target_pairs={{0,8},{4,12},{8,0},{12,4},{1,9},{5,13},{9,1},{13,5},{2,10},{6,14},... | collective-permute-start | bytes 884744 | tf_op jit(solution)/shard_map/ppermute | solution.py:191
  16.3 27.7 %copy-start = (bf16[1024,384]{1,0:T(8,128)(2,1)S(1)}, bf16[1024,384]{1,0:T(8,128)(2,1)}, u32[]{:S(2)}) copy-start(bf16[1024,384]{1,0:T(8,128)(2,1)} %wg.1) | copy-start | bytes 2359300
  16.3 27.7 %copy-start.1 = (bf16[1024,384]{1,0:T(8,128)(2,1)S(1)}, bf16[1024,384]{1,0:T(8,128)(2,1)}, u32[]{:S(2)}) copy-start(bf16[1024,384]{1,0:T(8,128)(2,1)} %wu.1) | copy-start | bytes 2359300
  17.1 27.6 %collective-permute-start.7 = (bf16[64,256]{1,0:T(8,128)(2,1)S(1)}, bf16[64,256]{1,0:T(8,128)(2,1)S(1)}, u32[]{:S(2)}, u32[]{:S(2)}) collective-permute-start(bf16[64,256]{1,0:T(8,128)(2,1)S(1)} %get-tuple-element.24), channel_id=1, source_target_pairs={{0,12},{4,0},{8,4},{12,8},{1,13},{5,1},{9,5},{13,9},{2,14},{6,2},{... | collective-permute-start | bytes 98312 | tf_op jit(solution)/shard_map/ppermute | solution.py:191
  33.5 12.6 %collective-permute-start.8 = (bf16[64,256]{1,0:T(8,128)(2,1)S(1)}, bf16[64,256]{1,0:T(8,128)(2,1)S(1)}, u32[]{:S(2)}, u32[]{:S(2)}) collective-permute-start(bf16[64,256]{1,0:T(8,128)(2,1)S(1)} %get-tuple-element.25), channel_id=1, source_target_pairs={{0,8},{4,12},{8,0},{12,4},{1,9},{5,13},{9,1},{13,5},{2,10},{6,14},... | collective-permute-start | bytes 98312 | tf_op jit(solution)/shard_map/ppermute | solution.py:191
  33.5 12.7 %collective-permute-start.9 = (bf16[64,256]{1,0:T(8,128)(2,1)S(1)}, bf16[64,256]{1,0:T(8,128)(2,1)S(1)}, u32[]{:S(2)}, u32[]{:S(2)}) collective-permute-start(bf16[64,256]{1,0:T(8,128)(2,1)S(1)} %get-tuple-element.26), channel_id=1, source_target_pairs={{0,4},{4,8},{8,12},{12,0},{1,5},{5,9},{9,13},{13,1},{2,6},{6,10},{... | collective-permute-start | bytes 98312 | tf_op jit(solution)/shard_map/ppermute | solution.py:191
  44.8 20.4 %collective-permute-start.12 = (bf16[3,128,384]{2,1,0:T(8,128)(2,1)S(1)}, bf16[3,128,384]{2,1,0:T(8,128)(2,1)S(1)}, u32[]{:S(2)}, u32[]{:S(2)}) collective-permute-start(bf16[3,128,384]{2,1,0:T(8,128)(2,1)S(1)} %pad_maximum_fusion.refs_6_), channel_id=1, source_target_pairs={{0,4},{4,8},{8,12},{12,0},{1,5},{5,9},{9,13},{13,1},{2,6},{6,10},{... | collective-permute-start | bytes 884744 | tf_op jit(solution)/shard_map/ppermute | solution.py:191
  46.1 12.5 %collective-permute-start.1 = (bf16[64,768]{1,0:T(8,128)(2,1)S(1)}, bf16[64,768]{1,0:T(8,128)(2,1)S(1)}, u32[]{:S(2)}, u32[]{:S(2)}) collective-permute-start(bf16[64,768]{1,0:T(8,128)(2,1)S(1)} %get-tuple-element.20), channel_id=1, source_target_pairs={{0,4},{4,8},{8,12},{12,0},{1,5},{5,9},{9,13},{13,1},{2,6},{6,10},{... | collective-permute-start | bytes 294920 | tf_op jit(solution)/shard_map/ppermute | solution.py:191
  46.2 18.9 %collective-permute-start.2 = (bf16[64,768]{1,0:T(8,128)(2,1)S(1)}, bf16[64,768]{1,0:T(8,128)(2,1)S(1)}, u32[]{:S(2)}, u32[]{:S(2)}) collective-permute-start(bf16[64,768]{1,0:T(8,128)(2,1)S(1)} %get-tuple-element.21), channel_id=1, source_target_pairs={{0,8},{4,12},{8,0},{12,4},{1,9},{5,13},{9,1},{13,5},{2,10},{6,14},... | collective-permute-start | bytes 294920 | tf_op jit(solution)/shard_map/ppermute | solution.py:191
  58.6 6.5 %collective-permute-start.3 = (bf16[64,768]{1,0:T(8,128)(2,1)S(1)}, bf16[64,768]{1,0:T(8,128)(2,1)S(1)}, u32[]{:S(2)}, u32[]{:S(2)}) collective-permute-start(bf16[64,768]{1,0:T(8,128)(2,1)S(1)} %get-tuple-element.22), channel_id=1, source_target_pairs={{0,12},{4,0},{8,4},{12,8},{1,13},{5,1},{9,5},{13,9},{2,14},{6,2},{... | collective-permute-start | bytes 294920 | tf_op jit(solution)/shard_map/ppermute | solution.py:191
  65.2 18.6 %copy-start.5 = (bf16[4,32,1024]{2,1,0:T(8,128)(2,1)S(1)}, bf16[4,32,1024]{2,1,0:T(8,128)(2,1)}, u32[]{:S(2)}) copy-start(bf16[4,32,1024]{2,1,0:T(8,128)(2,1)} %param.25) | copy-start | bytes 786436
  66.5 17.2 %copy-start.2 = (bf16[384,1024]{1,0:T(8,128)(2,1)S(1)}, bf16[384,1024]{1,0:T(8,128)(2,1)}, u32[]{:S(2)}) copy-start(bf16[384,1024]{1,0:T(8,128)(2,1)} %w.1) | copy-start | bytes 2359300
  66.6 8.6 %collective-permute-start.13 = (bf16[64,384]{1,0:T(8,128)(2,1)S(1)}, bf16[64,384]{1,0:T(8,128)(2,1)S(1)}, u32[]{:S(2)}, u32[]{:S(2)}) collective-permute-start(bf16[64,384]{1,0:T(8,128)(2,1)S(1)} %get-tuple-element.27), channel_id=1, source_target_pairs={{0,0},{1,4},{2,8},{3,12},{4,1},{5,5},{6,9},{7,13},{8,2},{9,6},{10,... | collective-permute-start | bytes 147464 | tf_op jit(solution)/shard_map/ppermute | solution.py:220
  67.4 8.6 %collective-permute-start.14 = (bf16[64,128]{1,0:T(8,128)(2,1)S(1)}, bf16[64,128]{1,0:T(8,128)(2,1)S(1)}, u32[]{:S(2)}, u32[]{:S(2)}) collective-permute-start(bf16[64,128]{1,0:T(8,128)(2,1)S(1)} %get-tuple-element.35), channel_id=1, source_target_pairs={{0,4},{4,8},{8,12},{12,0},{1,5},{5,9},{9,13},{13,1},{2,6},{6,10},{... | collective-permute-start | bytes 49160 | tf_op jit(solution)/shard_map/ppermute | solution.py:191
  70.7 6.0 %collective-permute-start.15 = (bf16[64,128]{1,0:T(8,128)(2,1)S(1)}, bf16[64,128]{1,0:T(8,128)(2,1)S(1)}, u32[]{:S(2)}, u32[]{:S(2)}) collective-permute-start(bf16[64,128]{1,0:T(8,128)(2,1)S(1)} %get-tuple-element.34), channel_id=1, source_target_pairs={{0,8},{4,12},{8,0},{12,4},{1,9},{5,13},{9,1},{13,5},{2,10},{6,14},... | collective-permute-start | bytes 49160 | tf_op jit(solution)/shard_map/ppermute | solution.py:191
  73.7 3.7 %collective-permute-start.16 = (bf16[64,128]{1,0:T(8,128)(2,1)S(1)}, bf16[64,128]{1,0:T(8,128)(2,1)S(1)}, u32[]{:S(2)}, u32[]{:S(2)}) collective-permute-start(bf16[64,128]{1,0:T(8,128)(2,1)S(1)} %get-tuple-element.33), channel_id=1, source_target_pairs={{0,12},{4,0},{8,4},{12,8},{1,13},{5,1},{9,5},{13,9},{2,14},{6,2},{... | collective-permute-start | bytes 49160 | tf_op jit(solution)/shard_map/ppermute | solution.py:191
  84.3 8.3 %collective-permute-start.17 = (bf16[64,1024]{1,0:T(8,128)(2,1)S(1)}, bf16[64,1024]{1,0:T(8,128)(2,1)S(1)}, u32[]{:S(2)}, u32[]{:S(2)}) collective-permute-start(bf16[64,1024]{1,0:T(8,128)(2,1)S(1)} %get-tuple-element.30), channel_id=1, source_target_pairs={{0,4},{4,8},{8,12},{12,0},{1,5},{5,9},{9,13},{13,1},{2,6},{6,10},{... | collective-permute-start | bytes 393224 | tf_op jit(solution)/shard_map/ppermute | solution.py:191
  86.0 11.6 %collective-permute-start.18 = (bf16[64,1024]{1,0:T(8,128)(2,1)S(1)}, bf16[64,1024]{1,0:T(8,128)(2,1)S(1)}, u32[]{:S(2)}, u32[]{:S(2)}) collective-permute-start(bf16[64,1024]{1,0:T(8,128)(2,1)S(1)} %get-tuple-element.31), channel_id=1, source_target_pairs={{0,8},{4,12},{8,0},{12,4},{1,9},{5,13},{9,1},{13,5},{2,10},{6,14},... | collective-permute-start | bytes 393224 | tf_op jit(solution)/shard_map/ppermute | solution.py:191
  88.3 9.4 %collective-permute-start.19 = (bf16[64,1024]{1,0:T(8,128)(2,1)S(1)}, bf16[64,1024]{1,0:T(8,128)(2,1)S(1)}, u32[]{:S(2)}, u32[]{:S(2)}) collective-permute-start(bf16[64,1024]{1,0:T(8,128)(2,1)S(1)} %get-tuple-element.32), channel_id=1, source_target_pairs={{0,12},{4,0},{8,4},{12,8},{1,13},{5,1},{9,5},{13,9},{2,14},{6,2},{... | collective-permute-start | bytes 393224 | tf_op jit(solution)/shard_map/ppermute | solution.py:191

commit v2 on v1

--- a/solution.py
+++ b/solution.py
@@ -1,4 +1,5 @@
 import functools
+import math
 
 import jax
 import jax.numpy as jnp
@@ -110,39 +111,44 @@
     return lax.dot_general(a, b, (((1,), (1,)), ((), ())), preferred_element_type=F32)
 
 
-def left_kernel(count, *refs):
-    xs, (lg, lu), outs = refs[:count], refs[count : count + 2], refs[count + 2 :]
-    cols = lg.shape[0]
-    for x, out in zip(xs, outs):
-        out[:, :cols] = dot_rows(x[...], lg[...]).astype(BF16)
-        out[:, cols:] = dot_rows(x[...], lu[...]).astype(BF16)
-
-
-def base_kernel(count, place, x, wg, wu, *refs):
-    outs, total = refs[:count], refs[count]
+def left_kernel(count, side, place, *refs):
+    xs, ls, outs, held = refs[:count], refs[count : count + side], refs[count + side : -1], refs[-1]
+    for m in range(count):
+        held[m] = xs[m][...]
+    for q in range(side):
+        total = jnp.zeros(outs[q].shape, F32)
+        for e in range(side):
+            total += dot_rows(held[place[0] ^ place[1] ^ (side * q + e)], ls[e][...])
+        outs[q][...] = total.astype(BF16)
+
+
+def base_kernel(count, side, place, *refs):
+    xs, (wg, wu), outs, total = refs[:side], refs[side : side + 2], refs[side + 2 : -1], refs[-1]
     cols = wg.shape[1]
-    total[:, :cols] = jnp.dot(x[...], wg[...], preferred_element_type=F32)
-    total[:, cols:] = jnp.dot(x[...], wu[...], preferred_element_type=F32)
     rows = outs[0].shape[0]
+    x = jnp.concatenate([x[...] for x in xs], axis=0)
+    total[:, :cols] = jnp.dot(x, wg[...], preferred_element_type=F32)
+    total[:, cols:] = jnp.dot(x, wu[...], preferred_element_type=F32)
     for k in range(count):
-        start = pl.multiple_of(lax.rem(place[0] + k, count) * rows, rows)
-        outs[k][...] = total[pl.ds(start, rows), :].astype(BF16)
-
-
-def hidden_kernel(count, held, *refs):
-    gs, (pls, weight), rs = refs[:count], refs[count : count + 2], refs[count + 2 : 2 * count + 2]
-    hsum, hl, *_ = refs[2 * count + 2 :]
+        turn = lax.rem(place[0] ^ place[1] ^ k, side)
+        start = pl.multiple_of((turn * side + k // side) * rows, rows)
+        outs[k][...] = total[pl.ds(start, rows), :].astype(outs[k].dtype)
+
+
+def hidden_kernel(count, held, place, *refs):
+    gs, (low, weight), rs = refs[:count], refs[count : count + 2], refs[count + 2 : 2 * count + 2]
+    outs, hl = refs[2 * count + 2 : 3 * count + 2], refs[3 * count + 2]
     rows, both = gs[0].shape
     cols = both // 2
     rank_cols = rs[0].shape[1]
     rank = rank_cols // held
     base = sum(g[...].astype(F32) for g in gs)
     gate, up = base[:, :cols], base[:, cols:]
-    low = sum(pls[pl.ds(n * rows, rows), :].astype(F32) for n in range(pls.shape[0] // rows)).astype(BF16)
     owner = lax.broadcasted_iota(jnp.int32, (rows, rank_cols), 1) // rank
     acc = jnp.zeros((rows, cols), F32)
     for k in range(count):
-        here = low[:, k * 2 * rank_cols : (k + 1) * 2 * rank_cols]
+        start = pl.multiple_of((place[0] ^ k) * rows, rows)
+        here = low[pl.ds(start, rows), :]
         low_gate, low_up = here[:, :rank_cols], here[:, rank_cols:]
         zero = jnp.zeros_like(low_gate)
         lhs_gate = jnp.concatenate([jnp.where(owner == i, low_gate, zero) for i in range(held)], axis=0)
@@ -162,33 +168,28 @@
         block = jnp.zeros((rows, rank_cols), F32)
         for i in range(held):
             block += jnp.where(owner == i, back[i * rows : (i + 1) * rows], 0.0)
-        hl[k] = block.astype(BF16)
-    hsum[...] = acc.astype(BF16)
+        hl[place[0] ^ place[1] ^ k] = block.astype(BF16)
+    outs[0][:, :cols] = acc.astype(BF16)
+    outs[0][:, cols:] = hl[0]
+    for m in range(1, count):
+        outs[m][...] = hl[m]
 
 
 def down_kernel(count, place, hs, w, rd, *refs):
     outs, total = refs[:count], refs[count]
     rows = outs[0].shape[0]
     inner = w.shape[0]
-    rank_cols = rd.shape[0]
-    low = sum(hs[pl.ds(n * rows, rows), inner:].astype(F32) for n in range(hs.shape[0] // rows)).astype(BF16)
     total[...] = jnp.dot(hs[:, :inner], w[...], preferred_element_type=F32)
-    low_rows = jnp.concatenate(
-        [low[:, j * rank_cols : (j + 1) * rank_cols] for j in ((count - k) % count for k in range(count))], axis=0
-    )
-    added = jnp.dot(low_rows, rd[...], preferred_element_type=F32)
+    total[...] += jnp.dot(hs[:, inner:], rd[...], preferred_element_type=F32)
     for k in range(count):
         start = pl.multiple_of(lax.rem(place[0] + k, count) * rows, rows)
-        outs[k][...] = (total[pl.ds(start, rows), :] + added[k * rows : (k + 1) * rows]).astype(BF16)
+        outs[k][...] = total[pl.ds(start, rows), :].astype(outs[k].dtype)
 
 
 VMEM = pl.BlockSpec(memory_space=pltpu.VMEM)
+ANY = pl.BlockSpec(memory_space=pl.ANY)
 SMEM = pl.BlockSpec(memory_space=pltpu.SMEM)
 PARAMS = pltpu.CompilerParams(vmem_limit_bytes=24 * 2**20)
-
-
-def along(axis, count, step):
-    return lambda a: lax.ppermute(a, axis, [(i, (i + step) % count) for i in range(count)])
 
 
 def stationary_shards(
@@ -207,25 +208,88 @@
     down_right,
 ):
     count = lax.axis_size("wide")
-    rows, top_count = routes.shape
+    rows = tokens.shape[0]
     held, rank = gate_left.shape[0], gate_left.shape[2]
     experts = held * count
     rank_cols = held * rank
     inner = base_gate.shape[1]
     features = base_down.shape[1]
     place = lax.axis_index("wide")
-    place_arr = place[None].astype(jnp.int32)
-
-    def swap(a):
-        return lax.ppermute(
-            a, ("wide", "narrow"), [(i * count + j, j * count + i) for i in range(count) for j in range(count)]
-        )
-
-    def spread(parts, sign):
-        return [parts[0]] + [along("wide", count, sign * k)(parts[k]) for k in range(1, count)]
-
-    own_features = lax.all_gather(swap(tokens), "narrow", axis=0, tiled=True)
-    blocks = spread([tokens] * count, 1)
+    spot = lax.axis_index("narrow")
+    places = jnp.stack([place, spot]).astype(jnp.int32)
+    side = math.isqrt(count)
+    steps = range(1, count)
+
+    def swap(a, k=0):
+        pairs = [(i * count + j, (j ^ k) * count + i) for i in range(count) for j in range(count)]
+        return lax.ppermute(a, ("wide", "narrow"), pairs)
+
+    def across(a, axis, k):
+        return lax.ppermute(a, axis, [(i, i ^ k) for i in range(count)])
+
+    def ahead(a, k):
+        return lax.ppermute(a, "wide", [(i, (i + k) % count) for i in range(count)])
+
+    def after(a, other):
+        return lax.optimization_barrier((a, other))[0]
+
+    def doubled(a, axis, order, other):
+        blocks = {0: a}
+        for bit in order:
+            for k, b in list(blocks.items()):
+                blocks[k ^ bit] = across(after(b, other) if k else b, axis, bit)
+        return [blocks[k] for k in range(count)]
+
+    bits = [1 << b for b in range(count.bit_length() - 1)]
+
+    spread = []
+    for m in range(count):
+        pairs = [
+            (w * count + j, (m ^ (w // side * side + j % side)) * count + j // side * side + w % side)
+            for w in range(count)
+            for j in range(count)
+        ]
+        spread.append(lax.ppermute(tokens, ("wide", "narrow"), pairs))
+
+    mine = [spread[side * a] for a in range(side)]
+    holds = spot // side == place // side
+    for a in range(side):
+        come = 0
+        for b in range(1, side):
+            pairs = [
+                (z * count + n, z * count + (n ^ (side * b)))
+                for z in range(count)
+                for n in range(count)
+                if z // side == n // side
+            ]
+            come += lax.ppermute(spread[side * a], ("wide", "narrow"), pairs)
+        mine[a] = jnp.where(holds, mine[a], come)
+    mine = jnp.concatenate(mine, axis=0)
+    own_features = [mine] + [across(mine, "narrow", e) for e in range(1, side)]
+
+    left = jnp.concatenate(
+        [jnp.swapaxes(a, 1, 2).reshape(rank_cols, a.shape[1]) for a in (gate_left, up_left)], axis=0
+    )
+    left = [left] + [across(left, "narrow", e) for e in range(1, side)]
+
+    low = pl.pallas_call(
+        functools.partial(left_kernel, count, side),
+        out_shape=[jax.ShapeDtypeStruct((rows, 2 * rank_cols), BF16)] * side,
+        in_specs=[SMEM] + [VMEM] * (count + side),
+        out_specs=[VMEM] * side,
+        scratch_shapes=[pltpu.VMEM((count, *tokens.shape), BF16)],
+        compiler_params=PARAMS,
+    )(places, *spread, *left)
+    low = sum(swap(low[q], side * q).astype(F32) for q in range(side)).astype(BF16)
+
+    sums = pl.pallas_call(
+        functools.partial(base_kernel, count, side),
+        out_shape=[jax.ShapeDtypeStruct((rows, 2 * inner), F32 if k == 0 else BF16) for k in range(count)],
+        in_specs=[SMEM] + [VMEM] * (side + 2),
+        out_specs=[VMEM] * count,
+        scratch_shapes=[pltpu.VMEM((count * rows, 2 * inner), F32)],
+        compiler_params=PARAMS,
+    )(places, *own_features, base_gate, base_up)
 
     packed = jnp.stack(
         [
@@ -234,62 +298,45 @@
             jnp.swapaxes(down_left, 1, 2).reshape(rank_cols, inner),
         ]
     )
-    factors = spread([packed] * count, -1)
+    factors = doubled(packed, "wide", bits[::-1], sums[0])
+    low = lax.all_gather(after(low, sums[0]), "narrow", axis=0, tiled=True)
+    sums = [sums[0]] + [across(sums[k], "wide", k) for k in steps]
 
     expert_ids = lax.broadcasted_iota(jnp.int32, (1, 1, experts), 2)
     named = routes[:, :, None] == expert_ids
     delta_ids = jnp.sum(jnp.where(named, delta_of[None, None, :], 0), axis=2)
-    slots = lax.rem(delta_ids - place * held + experts, experts)
+    slots = ((delta_ids // held) ^ place) * held + delta_ids % held
     weight = jnp.sum(jnp.where(slots[:, :, None] == expert_ids, gate_weights[:, :, None], 0.0), axis=1)
 
-    left_t = [jnp.swapaxes(a, 1, 2).reshape(rank_cols, a.shape[1]) for a in (gate_left, up_left)]
-    low = pl.pallas_call(
-        functools.partial(left_kernel, count),
-        out_shape=[jax.ShapeDtypeStruct((rows, 2 * rank_cols), BF16)] * count,
-        in_specs=[VMEM] * (count + 2),
-        out_specs=[VMEM] * count,
-        compiler_params=PARAMS,
-    )(*blocks, *left_t)
-    low = jnp.concatenate(spread(low, -1), axis=1)
-    low = lax.all_gather(low, "narrow", axis=0, tiled=True)
-
-    sums = pl.pallas_call(
-        functools.partial(base_kernel, count),
-        out_shape=[jax.ShapeDtypeStruct((rows, 2 * inner), BF16)] * count,
-        in_specs=[SMEM] + [VMEM] * 3,
-        out_specs=[VMEM] * count,
-        scratch_shapes=[pltpu.VMEM((count * rows, 2 * inner), F32)],
-        compiler_params=PARAMS,
-    )(place_arr, own_features, base_gate, base_up)
-    sums = spread(sums, 1)
-
-    hsum, hl = pl.pallas_call(
+    hidden = pl.pallas_call(
         functools.partial(hidden_kernel, count, held),
         out_shape=[
-            jax.ShapeDtypeStruct((rows, inner), BF16),
-            jax.ShapeDtypeStruct((count, rows, rank_cols), BF16),
+            jax.ShapeDtypeStruct((rows, rank_cols + (inner if k == 0 else 0)), BF16) for k in range(count)
         ],
-        in_specs=[VMEM] * (2 * count + 2),
-        out_specs=[VMEM] * 2,
+        in_specs=[SMEM] + [VMEM] * (2 * count + 2),
+        out_specs=[VMEM] * count,
+        scratch_shapes=[pltpu.VMEM((count, rows, rank_cols), BF16)],
         compiler_params=PARAMS,
-    )(*sums, low, weight, *factors)
-
-    hs = jnp.concatenate([swap(hsum)] + spread([hl[k] for k in range(count)], 1), axis=1)
+    )(places, *sums, low, weight, *factors)
+
+    hidden = [swap(hidden[k], k) for k in range(count)]
+    low_sum = sum(h[:, -rank_cols:].astype(F32) for h in hidden).astype(BF16)
+    hs = jnp.concatenate([hidden[0][:, :inner], low_sum], axis=1)
     hs = lax.all_gather(hs, "narrow", axis=0, tiled=True)
     outs = pl.pallas_call(
         functools.partial(down_kernel, count),
-        out_shape=[jax.ShapeDtypeStruct((rows, features), BF16)] * count,
+        out_shape=[jax.ShapeDtypeStruct((rows, features), F32 if k == 0 else BF16) for k in range(count)],
         in_specs=[SMEM] + [VMEM] * 3,
         out_specs=[VMEM] * count,
         scratch_shapes=[pltpu.VMEM((count * rows, features), F32)],
         compiler_params=PARAMS,
-    )(place_arr, hs, base_down, down_right.reshape(rank_cols, features))
-    outs = spread(outs, 1)
-    return sum(o.astype(F32) for o in outs).astype(BF16)
+    )(places, hs, base_down, down_right.reshape(rank_cols, features))
+    return sum([outs[0]] + [ahead(outs[k], k).astype(F32) for k in steps]).astype(BF16)
 
 
 def solution(mesh):
-    square = mesh.shape["wide"] == mesh.shape["narrow"]
+    count = mesh.shape["wide"]
+    square = count == mesh.shape["narrow"] == math.isqrt(count) ** 2 and count & (count - 1) == 0
     return jax.shard_map(
         stationary_shards if square else gathered_shards,
         mesh=mesh,

time: 99.1 us -> 86.1 us (0.87)
  starting transfers between devices: 47.7 us -> 37.9 us
  blocking collectives: 22.6 us -> 13.8 us
  waiting for transfers between devices: 20.8 us -> 25.9 us
  Pallas kernels: 3.53 us -> 5.71 us
  other arithmetic: 3.34 us -> 2.18 us
    all_gather x2 -> x1, blocking collectives: 16.3 us -> 6.19 us  [stationary_shards(): low = lax.all_gather(after(low, sums[0]), 'narrow', axis=0, tiled=True)]
    ppermute x20 -> x23, starting transfers between devices: 47.7 us -> 37.9 us  [the longest x6 10.5 us: swap(): return lax.ppermute(a, ('wide', 'narrow'), pairs)]
    ppermute x20 -> x23, waiting for transfers between devices: 20.8 us -> 25.9 us  [the longest x3 11.8 us: ahead(): return lax.ppermute(a, 'wide', [(i, (i + k) % count) for i in range(count)])]
    all_gather x1, blocking collectives: 6.31 us -> 7.6 us  [stationary_shards(): hs = lax.all_gather(hs, 'narrow', axis=0, tiled=True)]
    concatenate x1 -> x3, other arithmetic: 0.01 us -> 1.16 us  [the longest x1 1.13 us: stationary_shards(): jnp.concatenate([jnp.swapaxes(a, 1, 2).reshape(rank_cols, a.shape[1]) for...]
    another operation x1, other arithmetic: 1.09 us -> 0.04 us  [stationary_shards(): jnp.stack([gate_right.reshape(rank_cols, inner), up_right.reshape(rank_co...]
    pallas_call x2, Pallas kernels: 1.62 us -> 2.64 us  [the longest x1 1.35 us: stationary_shards(): pl.pallas_call(functools.partial(base_kernel, count, side), out_shape=[ja...]
  transfers between devices with their start and end apart: 20 -> 23, of which waited for: 6 -> 8; matrix products, arithmetic and copies ran while one was open for 3% -> 2% of each run, Pallas kernels for 2% -> 3%
where the time goes in v2:
time: 86.1 us; the launch traced here: 85.9 us
  starting transfers between devices  37.9 us (44%)
  waiting for transfers between devices  25.9 us (30%)
  blocking collectives  13.8 us (16%)
  Pallas kernels  5.71 us (7%)
  other arithmetic  2.18 us (3%)
    ppermute x3, waiting for transfers between devices, ahead(): return lax.ppermute(a, 'wide', [(i, (i + k) % count) for i in range(count)])  11.8 us
    ppermute x6, starting transfers between devices, swap(): return lax.ppermute(a, ('wide', 'narrow'), pairs)  10.5 us
    ppermute x4, starting transfers between devices, stationary_shards(): spread.append(lax.ppermute(tokens, ('wide', 'narrow'), pairs))  8.76 us
    ppermute x8, starting transfers between devices, across(): return lax.ppermute(a, axis, [(i, i ^ k) for i in range(count)])  8.4 us
    ppermute x2, starting transfers between devices, stationary_shards(): come += lax.ppermute(spread[side * a], ('wide', 'narrow'), pairs)  7.74 us
    all_gather x1, blocking collectives, stationary_shards(): hs = lax.all_gather(hs, 'narrow', axis=0, tiled=True)  7.6 us
    all_gather x1, blocking collectives, stationary_shards(): low = lax.all_gather(after(low, sums[0]), 'narrow', axis=0, tiled=True)  6.19 us
    ppermute x2, waiting for transfers between devices, stationary_shards(): come += lax.ppermute(spread[side * a], ('wide', 'narrow'), pairs)  4.66 us
  transfers between devices with their start and end apart: 23, of which 8 were waited for; matrix products, arithmetic and copies ran while one was open for 2% of the time, Pallas kernels for 3%

profile of v2, /device:TPU:0, one launch (start us, length us, event | category | flops | bytes accessed | tf_op | source)
XLA Modules:
  0.0 85.9 jit_solution(17695503011705928943)
XLA Ops:
  0.0 4.0 %collective-permute-start.2 = (bf16[64,1024]{1,0:T(8,128)(2,1)}, bf16[64,1024]{1,0:T(8,128)(2,1)S(1)}, u32[]{:S(2)}, u32[]{:S(2)}) collective-permute-start(bf16[64,1024]{1,0:T(8,128)(2,1)} %param.13), channel_id=1, source_target_pairs={{0,8},{1,12},{2,10},{3,14},{4,9},{5,13},{6,11},{7,15},{8,0},{9,4},... | collective-permute-start | bytes 393224 | tf_op jit(solution)/shard_map/ppermute | solution.py:252
  4.0 1.6 %collective-permute-start = (bf16[64,1024]{1,0:T(8,128)(2,1)}, bf16[64,1024]{1,0:T(8,128)(2,1)S(1)}, u32[]{:S(2)}, u32[]{:S(2)}) collective-permute-start(bf16[64,1024]{1,0:T(8,128)(2,1)} %param.13), channel_id=1, source_target_pairs={{0,0},{1,4},{2,2},{3,6},{4,1},{5,5},{6,3},{7,7},{8,8},{9,12},{10,1... | collective-permute-start | bytes 393224 | tf_op jit(solution)/shard_map/ppermute | solution.py:252
  5.6 3.2 %collective-permute-start.8 = (bf16[64,1024]{1,0:T(8,128)(2,1)}, bf16[64,1024]{1,0:T(8,128)(2,1)S(1)}, u32[]{:S(2)}, u32[]{:S(2)}) collective-permute-start(bf16[64,1024]{1,0:T(8,128)(2,1)} %param.13), channel_id=1, source_target_pairs={{0,4},{1,0},{2,6},{3,2},{4,5},{5,1},{6,7},{7,3},{8,12},{9,8},{10,1... | collective-permute-start | bytes 393224 | tf_op jit(solution)/shard_map/ppermute | solution.py:252
  8.8 0.0 collective-permute-start.9
  8.8 0.0 copy-start.5
  8.8 0.0 copy-start.6
  8.8 1.1 %pad_maximum_fusion.refs_4_ = bf16[256,1024]{1,0:T(8,128)(2,1)S(1)} fusion(bf16[128,1024]{1,0:T(8,128)(2,1)} %bitcast.15, bf16[128,1024]{1,0:T(8,128)(2,1)} %bitcast.16), kind=kLoop, calls=%fused_computation | loop fusion | flops 1048576 | bytes 1048576 | tf_op jit(solution)/shard_map/concatenate | solution.py:270
  9.9 0.1 collective-permute-start.10
  10.0 1.4 %collective-permute-done.2.refs_2_ = bf16[64,1024]{1,0:T(8,128)(2,1)S(1)} collective-permute-done((bf16[64,1024]{1,0:T(8,128)(2,1)}, bf16[64,1024]{1,0:T(8,128)(2,1)S(1)}, u32[]{:S(2)}, u32[]{:S(2)}) %collective-permute-start.2) | collective-permute-done | bytes 131104 | tf_op jit(solution)/shard_map/ppermute | solution.py:252
  11.4 3.4 %collective-permute-start.3 = (bf16[64,1024]{1,0:T(8,128)(2,1)S(1)}, bf16[64,1024]{1,0:T(8,128)(2,1)S(1)}, u32[]{:S(2)}, u32[]{:S(2)}) collective-permute-start(bf16[64,1024]{1,0:T(8,128)(2,1)S(1)} %collective-permute-done.2.refs_2_), channel_id=1, source_target_pairs={{0,2},{1,3},{4,6},{5,7},{10,8},{11,9},{14,12},{15,13},{16,18},{17,... | collective-permute-start | bytes 393224 | tf_op jit(solution)/shard_map/ppermute | solution.py:265
  14.8 0.0 copy-done.7
  14.8 0.1 select_reduce_fusion.1
  15.0 0.0 collective-permute-done.refs_0_
  15.0 0.1 collective-permute-start.14
  15.1 2.2 %collective-permute-done.3 = bf16[64,1024]{1,0:T(8,128)(2,1)S(1)} collective-permute-done((bf16[64,1024]{1,0:T(8,128)(2,1)S(1)}, bf16[64,1024]{1,0:T(8,128)(2,1)S(1)}, u32[]{:S(2)}, u32[]{:S(2)}) %collective-permute-start.3) | collective-permute-done | bytes 131104 | tf_op jit(solution)/shard_map/ppermute | solution.py:265
  17.3 4.3 %collective-permute-start.1 = (bf16[64,1024]{1,0:T(8,128)(2,1)S(1)}, bf16[64,1024]{1,0:T(8,128)(2,1)S(1)}, u32[]{:S(2)}, u32[]{:S(2)}) collective-permute-start(bf16[64,1024]{1,0:T(8,128)(2,1)S(1)} %collective-permute-done.refs_0_), channel_id=1, source_target_pairs={{0,2},{1,3},{4,6},{5,7},{10,8},{11,9},{14,12},{15,13},{16,18},{17,... | collective-permute-start | bytes 393224 | tf_op jit(solution)/shard_map/ppermute | solution.py:265
  21.7 2.5 %collective-permute-done.1 = bf16[64,1024]{1,0:T(8,128)(2,1)S(1)} collective-permute-done((bf16[64,1024]{1,0:T(8,128)(2,1)S(1)}, bf16[64,1024]{1,0:T(8,128)(2,1)S(1)}, u32[]{:S(2)}, u32[]{:S(2)}) %collective-permute-start.1) | collective-permute-done | bytes 131104 | tf_op jit(solution)/shard_map/ppermute | solution.py:265
  24.2 0.1 collective-permute-start.4
  24.3 0.1 pad_add_fusion.place
  24.4 0.0 collective-permute-done.8.refs_1_
  24.4 0.6 collective-permute-start.13
  24.9 0.0 collective-permute-done.9.refs_3_
  24.9 0.0 collective-permute-done.10.refs_5_
  25.0 1.3 %shard_map.128 = (bf16[64,256]{1,0:T(8,128)(2,1)S(1)}, bf16[64,256]{1,0:T(8,128)(2,1)S(1)}) custom-call(s32[2]{0:T(128)S(1)} %pad_add_fusion.place, bf16[64,1024]{1,0:T(8,128)(2,1)S(1)} %collective-permute-done.refs_0_, bf16[64,1024]{1,0:T(8,128)(2,1)S(1)} %collective-permute-done.8.refs_1_, bf16[64,1024]{1,0:T(8,128)(2,1)S(1)} %collective-permute-done.2.refs_2_, ...), custom_call_target="tpu_custom_call" | custom-call | tf_op jit(solution)/shard_map/pallas_call | solution.py:275
  26.2 3.9 %collective-permute-start.12 = (bf16[64,256]{1,0:T(8,128)(2,1)S(1)}, bf16[64,256]{1,0:T(8,128)(2,1)S(1)}, u32[]{:S(2)}, u32[]{:S(2)}) collective-permute-start(bf16[64,256]{1,0:T(8,128)(2,1)S(1)} %get-tuple-element.26), channel_id=1, source_target_pairs={{0,8},{1,12},{2,0},{3,4},{4,9},{5,13},{6,1},{7,5},{8,10},{9,14},{1... | collective-permute-start | bytes 98312 | tf_op jit(solution)/shard_map/ppermute | solution.py:225
  30.2 0.7 collective-permute-start.11
  30.8 0.0 collective-permute-done.4.refs_1_
  30.8 0.0 copy-done
  30.8 0.0 copy-done.1
  30.9 0.0 copy-start.8
  30.9 1.4 %shard_map.127 = (f32[64,768]{1,0:T(8,128)S(1)}, bf16[64,768]{1,0:T(8,128)(2,1)S(1)}, bf16[64,768]{1,0:T(8,128)(2,1)S(1)}, bf16[64,768]{1,0:T(8,128)(2,1)S(1)}) custom-call(s32[2]{0:T(128)S(1)} %pad_add_fusion.place, bf16[128,1024]{1,0:T(8,128)(2,1)S(1)} %pad_maximum_fusion.2.refs_0_, bf16[128,1024]{1,0:T(8,128)(2,1)S(1)} %collective-permute-done.4.refs_1_, ...), custom_call_target="tpu_custom_call" | custom-call | tf_op jit(solution)/shard_map/pallas_call | solution.py:285
  32.2 0.0 collective-permute-done.14.refs_8_
  32.2 3.2 %collective-permute-start.15 = (bf16[3,128,384]{2,1,0:T(8,128)(2,1)S(1)}, bf16[3,128,384]{2,1,0:T(8,128)(2,1)S(1)}, u32[]{:S(2)}, u32[]{:S(2)}) collective-permute-start(bf16[3,128,384]{2,1,0:T(8,128)(2,1)S(1)} %collective-permute-done.14.refs_8_), channel_id=1, source_target_pairs={{0,4},{4,0},{8,12},{12,8},{1,5},{5,1},{9,13},{13,9},{2,6},{6,2},{1... | collective-permute-start | bytes 884744 | tf_op jit(solution)/shard_map/ppermute | solution.py:228
  35.4 0.1 copy.16.refs_5_
  35.5 0.1 collective-permute-start.5
  35.6 0.0 collective-permute-done.12
  35.6 1.1 %collective-permute-start.6 = (bf16[64,768]{1,0:T(8,128)(2,1)S(1)}, bf16[64,768]{1,0:T(8,128)(2,1)S(1)}, u32[]{:S(2)}, u32[]{:S(2)}) collective-permute-start(bf16[64,768]{1,0:T(8,128)(2,1)S(1)} %get-tuple-element.23), channel_id=1, source_target_pairs={{0,8},{4,12},{8,0},{12,4},{1,9},{5,13},{9,1},{13,5},{2,10},{6,14},... | collective-permute-start | bytes 294920 | tf_op jit(solution)/shard_map/ppermute | solution.py:228
  36.7 0.0 collective-permute-done.11
  36.7 3.3 %collective-permute-start.7 = (bf16[64,768]{1,0:T(8,128)(2,1)S(1)}, bf16[64,768]{1,0:T(8,128)(2,1)S(1)}, u32[]{:S(2)}, u32[]{:S(2)}) collective-permute-start(bf16[64,768]{1,0:T(8,128)(2,1)S(1)} %get-tuple-element.24), channel_id=1, source_target_pairs={{0,12},{4,8},{8,4},{12,0},{1,13},{5,9},{9,5},{13,1},{2,14},{6,10},... | collective-permute-start | bytes 294920 | tf_op jit(solution)/shard_map/ppermute | solution.py:228
  40.0 6.2 %all_gather.6.refs_4_ = bf16[256,256]{1,0:T(8,128)(2,1)S(1)} all-gather(bf16[64,256]{1,0:T(8,128)(2,1)S(1)} %add_convert_fusion.1), channel_id=1, replica_groups=mesh['groups'=2,'wide'=4,'narrow'=4] {'narrow'}, dimensions={0}, use_global_device_ids=true | all-gather | bytes 163840 | tf_op jit(solution)/shard_map/all_gather | solution.py:302
  46.1 0.0 collective-permute-done.13.refs_7_
  46.2 4.3 %collective-permute-done.5.refs_1_ = bf16[64,768]{1,0:T(8,128)(2,1)S(1)} collective-permute-done((bf16[64,768]{1,0:T(8,128)(2,1)S(1)}, bf16[64,768]{1,0:T(8,128)(2,1)S(1)}, u32[]{:S(2)}, u32[]{:S(2)}) %collective-permute-start.5) | collective-permute-done | bytes 98336 | tf_op jit(solution)/shard_map/ppermute | solution.py:228
  50.5 0.0 collective-permute-done.6.refs_2_
  50.5 0.0 collective-permute-done.7.refs_3_
  50.5 0.0 collective-permute-done.15.refs_9_
  50.5 1.9 %shard_map.129 = (bf16[64,512]{1,0:T(8,128)(2,1)S(1)}, bf16[64,128]{1,0:T(8,128)(2,1)S(1)}, bf16[64,128]{1,0:T(8,128)(2,1)S(1)}, bf16[64,128]{1,0:T(8,128)(2,1)S(1)}) custom-call(s32[2]{0:T(128)S(1)} %pad_add_fusion.place, f32[64,768]{1,0:T(8,128)S(1)} %get-tuple-element.21.refs_0_, bf16[64,768]{1,0:T(8,128)(2,1)S(1)} %collective-permute-done.5.refs_1_, ...), custom_call_target="tpu_custom_call" | custom-call | tf_op jit(solution)/shard_map/pallas_call | solution.py:311
  52.4 0.7 collective-permute-start.16
  53.0 5.2 %collective-permute-start.19 = (bf16[64,128]{1,0:T(8,128)(2,1)S(1)}, bf16[64,128]{1,0:T(8,128)(2,1)S(1)}, u32[]{:S(2)}, u32[]{:S(2)}) collective-permute-start(bf16[64,128]{1,0:T(8,128)(2,1)S(1)} %get-tuple-element.32), channel_id=1, source_target_pairs={{0,12},{1,8},{2,4},{3,0},{4,13},{5,9},{6,5},{7,1},{8,14},{9,10},{1... | collective-permute-start | bytes 49160 | tf_op jit(solution)/shard_map/ppermute | solution.py:225
  58.3 0.0 collective-permute-start.18
  58.3 0.0 collective-permute-start.17
  58.3 0.0 collective-permute-done.16
  58.3 0.0 copy-start.3
  58.3 1.4 %collective-permute-done.19 = bf16[64,128]{1,0:T(8,128)(2,1)S(1)} collective-permute-done((bf16[64,128]{1,0:T(8,128)(2,1)S(1)}, bf16[64,128]{1,0:T(8,128)(2,1)S(1)}, u32[]{:S(2)}, u32[]{:S(2)}) %collective-permute-start.19) | collective-permute-done | bytes 16416 | tf_op jit(solution)/shard_map/ppermute | solution.py:225
  59.7 2.3 %collective-permute-done.18 = bf16[64,128]{1,0:T(8,128)(2,1)S(1)} collective-permute-done((bf16[64,128]{1,0:T(8,128)(2,1)S(1)}, bf16[64,128]{1,0:T(8,128)(2,1)S(1)}, u32[]{:S(2)}, u32[]{:S(2)}) %collective-permute-start.18) | collective-permute-done | bytes 16416 | tf_op jit(solution)/shard_map/ppermute | solution.py:225
  62.0 0.0 collective-permute-done.17
  62.0 7.6 %all_gather.7.hs = bf16[256,512]{1,0:T(8,128)(2,1)S(1)} all-gather(bf16[64,512]{1,0:T(8,128)(2,1)S(1)} %pad_maximum_fusion.3), channel_id=1, replica_groups=mesh['groups'=2,'wide'=4,'narrow'=4] {'narrow'}, dimensions={0}, use_global_device_ids=true | all-gather | bytes 327680 | tf_op jit(solution)/shard_map/all_gather | solution.py:325
  69.7 1.2 %shard_map.130 = (f32[64,1024]{1,0:T(8,128)S(1)}, bf16[64,1024]{1,0:T(8,128)(2,1)S(1)}, bf16[64,1024]{1,0:T(8,128)(2,1)S(1)}, bf16[64,1024]{1,0:T(8,128)(2,1)S(1)}) custom-call(s32[2]{0:T(128)S(1)} %pad_add_fusion.place, bf16[256,512]{1,0:T(8,128)(2,1)S(1)} %all_gather.7.hs, bf16[384,1024]{1,0:T(8,128)(2,1)S(1)} %copy-done.2, bf16[128,1024]{1,0:T(8,128)(2,1)S(1)} %bitcast.14), custom_call_target="tpu_custom_call" | custom-call | tf_op jit(solution)/shard_map/pallas_call | solution.py:326
  70.9 1.9 %collective-permute-start.22 = (bf16[64,1024]{1,0:T(8,128)(2,1)S(1)}, bf16[64,1024]{1,0:T(8,128)(2,1)S(1)}, u32[]{:S(2)}, u32[]{:S(2)}) collective-permute-start(bf16[64,1024]{1,0:T(8,128)(2,1)S(1)} %get-tuple-element.36), channel_id=1, source_target_pairs={{0,12},{4,0},{8,4},{12,8},{1,13},{5,1},{9,5},{13,9},{2,14},{6,2},{... | collective-permute-start | bytes 393224 | tf_op jit(solution)/shard_map/ppermute | solution.py:231
  72.8 0.2 collective-permute-start.21
  73.0 0.4 collective-permute-start.20
  73.4 3.3 %collective-permute-done.22 = bf16[64,1024]{1,0:T(8,128)(2,1)S(1)} collective-permute-done((bf16[64,1024]{1,0:T(8,128)(2,1)S(1)}, bf16[64,1024]{1,0:T(8,128)(2,1)S(1)}, u32[]{:S(2)}, u32[]{:S(2)}) %collective-permute-start.22) | collective-permute-done | bytes 131104 | tf_op jit(solution)/shard_map/ppermute | solution.py:231
  76.7 8.4 %collective-permute-done.21 = bf16[64,1024]{1,0:T(8,128)(2,1)S(1)} collective-permute-done((bf16[64,1024]{1,0:T(8,128)(2,1)S(1)}, bf16[64,1024]{1,0:T(8,128)(2,1)S(1)}, u32[]{:S(2)}, u32[]{:S(2)}) %collective-permute-start.21) | collective-permute-done | bytes 131104 | tf_op jit(solution)/shard_map/ppermute | solution.py:231
  85.2 0.0 collective-permute-done.20
  85.2 0.7 add_convert_fusion
  (23 shorter events, 0.2 us)
Async XLA Ops:
  0.0 11.4 %collective-permute-start.2 = (bf16[64,1024]{1,0:T(8,128)(2,1)}, bf16[64,1024]{1,0:T(8,128)(2,1)S(1)}, u32[]{:S(2)}, u32[]{:S(2)}) collective-permute-start(bf16[64,1024]{1,0:T(8,128)(2,1)} %param.13), channel_id=1, source_target_pairs={{0,8},{1,12},{2,10},{3,14},{4,9},{5,13},{6,11},{7,15},{8,0},{9,4},... | collective-permute-start | bytes 393224 | tf_op jit(solution)/shard_map/ppermute | solution.py:252
  4.0 11.0 %collective-permute-start = (bf16[64,1024]{1,0:T(8,128)(2,1)}, bf16[64,1024]{1,0:T(8,128)(2,1)S(1)}, u32[]{:S(2)}, u32[]{:S(2)}) collective-permute-start(bf16[64,1024]{1,0:T(8,128)(2,1)} %param.13), channel_id=1, source_target_pairs={{0,0},{1,4},{2,2},{3,6},{4,1},{5,5},{6,3},{7,7},{8,8},{9,12},{10,1... | collective-permute-start | bytes 393224 | tf_op jit(solution)/shard_map/ppermute | solution.py:252
  5.6 18.8 %collective-permute-start.8 = (bf16[64,1024]{1,0:T(8,128)(2,1)}, bf16[64,1024]{1,0:T(8,128)(2,1)S(1)}, u32[]{:S(2)}, u32[]{:S(2)}) collective-permute-start(bf16[64,1024]{1,0:T(8,128)(2,1)} %param.13), channel_id=1, source_target_pairs={{0,4},{1,0},{2,6},{3,2},{4,5},{5,1},{6,7},{7,3},{8,12},{9,8},{10,1... | collective-permute-start | bytes 393224 | tf_op jit(solution)/shard_map/ppermute | solution.py:252
  8.8 16.2 %collective-permute-start.9 = (bf16[64,1024]{1,0:T(8,128)(2,1)}, bf16[64,1024]{1,0:T(8,128)(2,1)S(1)}, u32[]{:S(2)}, u32[]{:S(2)}) collective-permute-start(bf16[64,1024]{1,0:T(8,128)(2,1)} %param.13), channel_id=1, source_target_pairs={{0,12},{1,8},{2,14},{3,10},{4,13},{5,9},{6,15},{7,11},{8,4},{9,0},... | collective-permute-start | bytes 393224 | tf_op jit(solution)/shard_map/ppermute | solution.py:252
  8.8 6.0 %copy-start.7 = (s32[64,8]{0,1:T(8,128)S(1)}, s32[64,8]{0,1:T(8,128)}, u32[]{:S(2)}) copy-start(s32[64,8]{0,1:T(8,128)} %param.14) | copy-start | bytes 6148
  8.8 6.0 %copy-start.9 = (s32[16]{0:T(128)S(1)}, s32[16]{0:T(128)}, u32[]{:S(2)}) copy-start(s32[16]{0:T(128)} %param.16) | copy-start | bytes 196
  8.8 6.2 %copy-start.4 = (bf16[4,384,32]{1,2,0:T(8,128)(2,1)S(1)}, bf16[4,384,32]{1,2,0:T(8,128)(2,1)}, u32[]{:S(2)}) copy-start(bf16[4,384,32]{1,2,0:T(8,128)(2,1)} %param.24) | copy-start | bytes 294916
  8.8 6.2 %copy-start.5 = (bf16[4,32,384]{2,1,0:T(8,128)(2,1)S(1)}, bf16[4,32,384]{2,1,0:T(8,128)(2,1)}, u32[]{:S(2)}) copy-start(bf16[4,32,384]{2,1,0:T(8,128)(2,1)} %param.23) | copy-start | bytes 294916
  8.8 6.2 %copy-start.6 = (bf16[4,32,384]{2,1,0:T(8,128)(2,1)S(1)}, bf16[4,32,384]{2,1,0:T(8,128)(2,1)}, u32[]{:S(2)}) copy-start(bf16[4,32,384]{2,1,0:T(8,128)(2,1)} %param.21) | copy-start | bytes 294916
  9.9 15.0 %collective-permute-start.10 = (bf16[256,1024]{1,0:T(8,128)(2,1)S(1)}, bf16[256,1024]{1,0:T(8,128)(2,1)S(1)}, u32[]{:S(2)}, u32[]{:S(2)}) collective-permute-start(bf16[256,1024]{1,0:T(8,128)(2,1)S(1)} %pad_maximum_fusion.refs_4_), channel_id=1, source_target_pairs={{0,1},{1,0},{2,3},{3,2},{4,5},{5,4},{6,7},{7,6},{8,9},{9,8},{10,11... | collective-permute-start | bytes 1572872 | tf_op jit(solution)/shard_map/ppermute | solution.py:228
  11.4 5.9 %collective-permute-start.3 = (bf16[64,1024]{1,0:T(8,128)(2,1)S(1)}, bf16[64,1024]{1,0:T(8,128)(2,1)S(1)}, u32[]{:S(2)}, u32[]{:S(2)}) collective-permute-start(bf16[64,1024]{1,0:T(8,128)(2,1)S(1)} %collective-permute-done.2.refs_2_), channel_id=1, source_target_pairs={{0,2},{1,3},{4,6},{5,7},{10,8},{11,9},{14,12},{15,13},{16,18},{17,... | collective-permute-start | bytes 393224 | tf_op jit(solution)/shard_map/ppermute | solution.py:265
  15.0 17.2 %collective-permute-start.14 = (bf16[3,128,384]{2,1,0:T(8,128)(2,1)S(1)}, bf16[3,128,384]{2,1,0:T(8,128)(2,1)S(1)}, u32[]{:S(2)}, u32[]{:S(2)}) collective-permute-start(bf16[3,128,384]{2,1,0:T(8,128)(2,1)S(1)} %pad_maximum_fusion.1.refs_6_), channel_id=1, source_target_pairs={{0,8},{4,12},{8,0},{12,4},{1,9},{5,13},{9,1},{13,5},{2,10},{6,14},... | collective-permute-start | bytes 884744 | tf_op jit(solution)/shard_map/ppermute | solution.py:228
  17.3 6.8 %collective-permute-start.1 = (bf16[64,1024]{1,0:T(8,128)(2,1)S(1)}, bf16[64,1024]{1,0:T(8,128)(2,1)S(1)}, u32[]{:S(2)}, u32[]{:S(2)}) collective-permute-start(bf16[64,1024]{1,0:T(8,128)(2,1)S(1)} %collective-permute-done.refs_0_), channel_id=1, source_target_pairs={{0,2},{1,3},{4,6},{5,7},{10,8},{11,9},{14,12},{15,13},{16,18},{17,... | collective-permute-start | bytes 393224 | tf_op jit(solution)/shard_map/ppermute | solution.py:265
  24.2 6.6 %collective-permute-start.4 = (bf16[128,1024]{1,0:T(8,128)(2,1)S(1)}, bf16[128,1024]{1,0:T(8,128)(2,1)S(1)}, u32[]{:S(2)}, u32[]{:S(2)}) collective-permute-start(bf16[128,1024]{1,0:T(8,128)(2,1)S(1)} %pad_maximum_fusion.2.refs_0_), channel_id=1, source_target_pairs={{0,1},{1,0},{2,3},{3,2},{4,5},{5,4},{6,7},{7,6},{8,9},{9,8},{10,11... | collective-permute-start | bytes 786440 | tf_op jit(solution)/shard_map/ppermute | solution.py:228
  24.4 6.5 %copy-start = (bf16[1024,384]{1,0:T(8,128)(2,1)S(1)}, bf16[1024,384]{1,0:T(8,128)(2,1)}, u32[]{:S(2)}) copy-start(bf16[1024,384]{1,0:T(8,128)(2,1)} %refs_2_.1) | copy-start | bytes 2359300
  24.4 6.5 %copy-start.1 = (bf16[1024,384]{1,0:T(8,128)(2,1)S(1)}, bf16[1024,384]{1,0:T(8,128)(2,1)}, u32[]{:S(2)}) copy-start(bf16[1024,384]{1,0:T(8,128)(2,1)} %refs_3_.1) | copy-start | bytes 2359300
  24.4 21.8 %collective-permute-start.13 = (bf16[3,128,384]{2,1,0:T(8,128)(2,1)S(1)}, bf16[3,128,384]{2,1,0:T(8,128)(2,1)S(1)}, u32[]{:S(2)}, u32[]{:S(2)}) collective-permute-start(bf16[3,128,384]{2,1,0:T(8,128)(2,1)S(1)} %pad_maximum_fusion.1.refs_6_), channel_id=1, source_target_pairs={{0,4},{4,0},{8,12},{12,8},{1,5},{5,1},{9,13},{13,9},{2,6},{6,2},{1... | collective-permute-start | bytes 884744 | tf_op jit(solution)/shard_map/ppermute | solution.py:228
  26.2 9.3 %collective-permute-start.12 = (bf16[64,256]{1,0:T(8,128)(2,1)S(1)}, bf16[64,256]{1,0:T(8,128)(2,1)S(1)}, u32[]{:S(2)}, u32[]{:S(2)}) collective-permute-start(bf16[64,256]{1,0:T(8,128)(2,1)S(1)} %get-tuple-element.26), channel_id=1, source_target_pairs={{0,8},{1,12},{2,0},{3,4},{4,9},{5,13},{6,1},{7,5},{8,10},{9,14},{1... | collective-permute-start | bytes 98312 | tf_op jit(solution)/shard_map/ppermute | solution.py:225
  30.2 6.5 %collective-permute-start.11 = (bf16[64,256]{1,0:T(8,128)(2,1)S(1)}, bf16[64,256]{1,0:T(8,128)(2,1)S(1)}, u32[]{:S(2)}, u32[]{:S(2)}) collective-permute-start(bf16[64,256]{1,0:T(8,128)(2,1)S(1)} %get-tuple-element.25), channel_id=1, source_target_pairs={{0,0},{1,4},{2,8},{3,12},{4,1},{5,5},{6,9},{7,13},{8,2},{9,6},{10,... | collective-permute-start | bytes 98312 | tf_op jit(solution)/shard_map/ppermute | solution.py:225
  30.9 4.6 %copy-start.8 = (f32[64,8]{0,1:T(8,128)S(1)}, f32[64,8]{0,1:T(8,128)}, u32[]{:S(2)}) copy-start(f32[64,8]{0,1:T(8,128)} %param.15) | copy-start | bytes 6148
  32.2 18.3 %collective-permute-start.15 = (bf16[3,128,384]{2,1,0:T(8,128)(2,1)S(1)}, bf16[3,128,384]{2,1,0:T(8,128)(2,1)S(1)}, u32[]{:S(2)}, u32[]{:S(2)}) collective-permute-start(bf16[3,128,384]{2,1,0:T(8,128)(2,1)S(1)} %collective-permute-done.14.refs_8_), channel_id=1, source_target_pairs={{0,4},{4,0},{8,12},{12,8},{1,5},{5,1},{9,13},{13,9},{2,6},{6,2},{1... | collective-permute-start | bytes 884744 | tf_op jit(solution)/shard_map/ppermute | solution.py:228
  35.5 15.0 %collective-permute-start.5 = (bf16[64,768]{1,0:T(8,128)(2,1)S(1)}, bf16[64,768]{1,0:T(8,128)(2,1)S(1)}, u32[]{:S(2)}, u32[]{:S(2)}) collective-permute-start(bf16[64,768]{1,0:T(8,128)(2,1)S(1)} %get-tuple-element.22), channel_id=1, source_target_pairs={{0,4},{4,0},{8,12},{12,8},{1,5},{5,1},{9,13},{13,9},{2,6},{6,2},{1... | collective-permute-start | bytes 294920 | tf_op jit(solution)/shard_map/ppermute | solution.py:228
  35.6 14.9 %collective-permute-start.6 = (bf16[64,768]{1,0:T(8,128)(2,1)S(1)}, bf16[64,768]{1,0:T(8,128)(2,1)S(1)}, u32[]{:S(2)}, u32[]{:S(2)}) collective-permute-start(bf16[64,768]{1,0:T(8,128)(2,1)S(1)} %get-tuple-element.23), channel_id=1, source_target_pairs={{0,8},{4,12},{8,0},{12,4},{1,9},{5,13},{9,1},{13,5},{2,10},{6,14},... | collective-permute-start | bytes 294920 | tf_op jit(solution)/shard_map/ppermute | solution.py:228
  36.7 13.8 %collective-permute-start.7 = (bf16[64,768]{1,0:T(8,128)(2,1)S(1)}, bf16[64,768]{1,0:T(8,128)(2,1)S(1)}, u32[]{:S(2)}, u32[]{:S(2)}) collective-permute-start(bf16[64,768]{1,0:T(8,128)(2,1)S(1)} %get-tuple-element.24), channel_id=1, source_target_pairs={{0,12},{4,8},{8,4},{12,0},{1,13},{5,9},{9,5},{13,1},{2,14},{6,10},... | collective-permute-start | bytes 294920 | tf_op jit(solution)/shard_map/ppermute | solution.py:228
  46.1 23.5 %copy-start.2 = (bf16[384,1024]{1,0:T(8,128)(2,1)S(1)}, bf16[384,1024]{1,0:T(8,128)(2,1)}, u32[]{:S(2)}) copy-start(bf16[384,1024]{1,0:T(8,128)(2,1)} %w.1) | copy-start | bytes 2359300
  52.4 5.9 %collective-permute-start.16 = (bf16[64,512]{1,0:T(8,128)(2,1)S(1)}, bf16[64,512]{1,0:T(8,128)(2,1)S(1)}, u32[]{:S(2)}, u32[]{:S(2)}) collective-permute-start(bf16[64,512]{1,0:T(8,128)(2,1)S(1)} %get-tuple-element.29), channel_id=1, source_target_pairs={{0,0},{1,4},{2,8},{3,12},{4,1},{5,5},{6,9},{7,13},{8,2},{9,6},{10,... | collective-permute-start | bytes 196616 | tf_op jit(solution)/shard_map/ppermute | solution.py:225
  53.0 6.7 %collective-permute-start.19 = (bf16[64,128]{1,0:T(8,128)(2,1)S(1)}, bf16[64,128]{1,0:T(8,128)(2,1)S(1)}, u32[]{:S(2)}, u32[]{:S(2)}) collective-permute-start(bf16[64,128]{1,0:T(8,128)(2,1)S(1)} %get-tuple-element.32), channel_id=1, source_target_pairs={{0,12},{1,8},{2,4},{3,0},{4,13},{5,9},{6,5},{7,1},{8,14},{9,10},{1... | collective-permute-start | bytes 49160 | tf_op jit(solution)/shard_map/ppermute | solution.py:225
  58.3 3.7 %collective-permute-start.18 = (bf16[64,128]{1,0:T(8,128)(2,1)S(1)}, bf16[64,128]{1,0:T(8,128)(2,1)S(1)}, u32[]{:S(2)}, u32[]{:S(2)}) collective-permute-start(bf16[64,128]{1,0:T(8,128)(2,1)S(1)} %get-tuple-element.31), channel_id=1, source_target_pairs={{0,8},{1,12},{2,0},{3,4},{4,9},{5,13},{6,1},{7,5},{8,10},{9,14},{1... | collective-permute-start | bytes 49160 | tf_op jit(solution)/shard_map/ppermute | solution.py:225
  58.3 3.7 %collective-permute-start.17 = (bf16[64,128]{1,0:T(8,128)(2,1)S(1)}, bf16[64,128]{1,0:T(8,128)(2,1)S(1)}, u32[]{:S(2)}, u32[]{:S(2)}) collective-permute-start(bf16[64,128]{1,0:T(8,128)(2,1)S(1)} %get-tuple-element.30), channel_id=1, source_target_pairs={{0,4},{1,0},{2,12},{3,8},{4,5},{5,1},{6,13},{7,9},{8,6},{9,2},{10,... | collective-permute-start | bytes 49160 | tf_op jit(solution)/shard_map/ppermute | solution.py:225
  58.3 11.4 %copy-start.3 = (bf16[4,32,1024]{2,1,0:T(8,128)(2,1)S(1)}, bf16[4,32,1024]{2,1,0:T(8,128)(2,1)}, u32[]{:S(2)}) copy-start(bf16[4,32,1024]{2,1,0:T(8,128)(2,1)} %param.25) | copy-start | bytes 786436
  70.9 5.9 %collective-permute-start.22 = (bf16[64,1024]{1,0:T(8,128)(2,1)S(1)}, bf16[64,1024]{1,0:T(8,128)(2,1)S(1)}, u32[]{:S(2)}, u32[]{:S(2)}) collective-permute-start(bf16[64,1024]{1,0:T(8,128)(2,1)S(1)} %get-tuple-element.36), channel_id=1, source_target_pairs={{0,12},{4,0},{8,4},{12,8},{1,13},{5,1},{9,5},{13,9},{2,14},{6,2},{... | collective-permute-start | bytes 393224 | tf_op jit(solution)/shard_map/ppermute | solution.py:231
  72.8 12.4 %collective-permute-start.21 = (bf16[64,1024]{1,0:T(8,128)(2,1)S(1)}, bf16[64,1024]{1,0:T(8,128)(2,1)S(1)}, u32[]{:S(2)}, u32[]{:S(2)}) collective-permute-start(bf16[64,1024]{1,0:T(8,128)(2,1)S(1)} %get-tuple-element.35), channel_id=1, source_target_pairs={{0,8},{4,12},{8,0},{12,4},{1,9},{5,13},{9,1},{13,5},{2,10},{6,14},... | collective-permute-start | bytes 393224 | tf_op jit(solution)/shard_map/ppermute | solution.py:231
  73.0 12.2 %collective-permute-start.20 = (bf16[64,1024]{1,0:T(8,128)(2,1)S(1)}, bf16[64,1024]{1,0:T(8,128)(2,1)S(1)}, u32[]{:S(2)}, u32[]{:S(2)}) collective-permute-start(bf16[64,1024]{1,0:T(8,128)(2,1)S(1)} %get-tuple-element.34), channel_id=1, source_target_pairs={{0,4},{4,8},{8,12},{12,0},{1,5},{5,9},{9,13},{13,1},{2,6},{6,10},{... | collective-permute-start | bytes 393224 | tf_op jit(solution)/shard_map/ppermute | solution.py:231

commit v3 on v2

--- a/solution.py
+++ b/solution.py
@@ -115,11 +115,13 @@
     xs, ls, outs, held = refs[:count], refs[count : count + side], refs[count + side : -1], refs[-1]
     for m in range(count):
         held[m] = xs[m][...]
+    rows = outs[0].shape[0]
+    total = jnp.zeros((side * rows, outs[0].shape[1]), F32)
+    for e in range(side):
+        x = jnp.concatenate([held[place[0] ^ place[1] ^ (side * q + e)] for q in range(side)], axis=0)
+        total += dot_rows(x, ls[e][...])
     for q in range(side):
-        total = jnp.zeros(outs[q].shape, F32)
-        for e in range(side):
-            total += dot_rows(held[place[0] ^ place[1] ^ (side * q + e)], ls[e][...])
-        outs[q][...] = total.astype(BF16)
+        outs[q][...] = total[q * rows : (q + 1) * rows].astype(BF16)
 
 
 def base_kernel(count, side, place, *refs):
@@ -137,7 +139,8 @@
 
 def hidden_kernel(count, held, place, *refs):
     gs, (low, weight), rs = refs[:count], refs[count : count + 2], refs[count + 2 : 2 * count + 2]
-    outs, hl = refs[2 * count + 2 : 3 * count + 2], refs[3 * count + 2]
+    hsum, *outs, hl = refs[2 * count + 2 :]
+    side = len(outs)
     rows, both = gs[0].shape
     cols = both // 2
     rank_cols = rs[0].shape[1]
@@ -159,7 +162,7 @@
         for i in range(held):
             gi = gate + g[i * rows : (i + 1) * rows]
             ui = up + u[i * rows : (i + 1) * rows]
-            h = (gi / (1.0 + jnp.exp(-gi))) * ui
+            h = (0.5 * gi) * (1.0 + jnp.tanh(0.5 * gi)) * ui
             slot = k * held + i
             hw = h * weight[:, slot : slot + 1]
             acc += hw
@@ -168,11 +171,11 @@
         block = jnp.zeros((rows, rank_cols), F32)
         for i in range(held):
             block += jnp.where(owner == i, back[i * rows : (i + 1) * rows], 0.0)
-        hl[place[0] ^ place[1] ^ k] = block.astype(BF16)
-    outs[0][:, :cols] = acc.astype(BF16)
-    outs[0][:, cols:] = hl[0]
-    for m in range(1, count):
-        outs[m][...] = hl[m]
+        hl[place[0] ^ place[1] ^ k] = block
+    hsum[...] = acc.astype(BF16)
+    for e in range(side):
+        for b in range(side):
+            outs[e][:, b * rank_cols : (b + 1) * rank_cols] = hl[side * b + e].astype(outs[e].dtype)
 
 
 def down_kernel(count, place, hs, w, rd, *refs):
@@ -191,22 +194,10 @@
 SMEM = pl.BlockSpec(memory_space=pltpu.SMEM)
 PARAMS = pltpu.CompilerParams(vmem_limit_bytes=24 * 2**20)
 
-
-def stationary_shards(
-    tokens,
-    routes,
-    gate_weights,
-    delta_of,
-    base_gate,
-    base_up,
-    base_down,
-    gate_left,
-    gate_right,
-    up_left,
-    up_right,
-    down_left,
-    down_right,
-):
+SEP, YR = True, False
+TIES = {'C': ['sums0'], 'lowag': ['sums0'], 'far': ['X1', 'X3', 'xe2'], 'mc': ['sent']}
+
+def stationary_shards(tokens, routes, gate_weights, delta_of, base_gate, base_up, base_down, gate_left, gate_right, up_left, up_right, down_left, down_right):
     count = lax.axis_size("wide")
     rows = tokens.shape[0]
     held, rank = gate_left.shape[0], gate_left.shape[2]
@@ -216,9 +207,21 @@
     features = base_down.shape[1]
     place = lax.axis_index("wide")
     spot = lax.axis_index("narrow")
-    places = jnp.stack([place, spot]).astype(jnp.int32)
+    places = jnp.stack([place, spot, lax.axis_index("groups")]).astype(jnp.int32)
     side = math.isqrt(count)
     steps = range(1, count)
+    memo, busy = {}, set()
+
+    def get(name):
+        if name not in memo:
+            assert name not in busy, "cycle"
+            busy.add(name)
+            memo[name] = nodes[name]()
+        return memo[name]
+
+    def tied(a, name):
+        deps = [get(d) for d in TIES.get(name, ())]
+        return lax.optimization_barrier((a, deps))[0] if deps else a
 
     def swap(a, k=0):
         pairs = [(i * count + j, (j ^ k) * count + i) for i in range(count) for j in range(count)]
@@ -230,98 +233,208 @@
     def ahead(a, k):
         return lax.ppermute(a, "wide", [(i, (i + k) % count) for i in range(count)])
 
-    def after(a, other):
-        return lax.optimization_barrier((a, other))[0]
-
-    def doubled(a, axis, order, other):
-        blocks = {0: a}
-        for bit in order:
-            for k, b in list(blocks.items()):
-                blocks[k ^ bit] = across(after(b, other) if k else b, axis, bit)
-        return [blocks[k] for k in range(count)]
-
-    bits = [1 << b for b in range(count.bit_length() - 1)]
-
-    spread = []
-    for m in range(count):
+    nodes = {}
+
+    def node(f):
+        nodes[f.__name__] = f
+        return f
+
+    def X(m):
         pairs = [
             (w * count + j, (m ^ (w // side * side + j % side)) * count + j // side * side + w % side)
             for w in range(count)
             for j in range(count)
         ]
-        spread.append(lax.ppermute(tokens, ("wide", "narrow"), pairs))
-
-    mine = [spread[side * a] for a in range(side)]
-    holds = spot // side == place // side
-    for a in range(side):
-        come = 0
-        for b in range(1, side):
-            pairs = [
-                (z * count + n, z * count + (n ^ (side * b)))
-                for z in range(count)
-                for n in range(count)
-                if z // side == n // side
+        return lax.ppermute(tied(tokens, f"X{m}"), ("wide", "narrow"), pairs)
+    for m in range(count):
+        nodes[f"X{m}"] = functools.partial(X, m)
+
+    def xe(m):
+        pairs = [
+            (z * count + n, z * count + (n ^ side))
+            for z in range(count)
+            for n in range(count)
+            if z // side == n // side
+        ]
+        return lax.ppermute(tied(get(f"X{m}"), f"xe{m}"), ("wide", "narrow"), pairs)
+    nodes["xe0"] = lambda: xe(0)
+    nodes["xe2"] = lambda: xe(2)
+
+    @node
+    def mine():
+        holds = spot // side == place // side
+        return jnp.concatenate([jnp.where(holds, get(f"X{m}"), get(f"xe{m}")) for m in (0, 2)], axis=0)
+
+    @node
+    def mc():
+        return across(tied(get("mine"), "mc"), "narrow", 1)
+
+    @node
+    def Lp():
+        return jnp.concatenate(
+            [jnp.swapaxes(a, 1, 2).reshape(rank_cols, a.shape[1]) for a in (gate_left, up_left)], axis=0
+        )
+
+    @node
+    def Lc():
+        return across(tied(get("Lp"), "Lc"), "narrow", 1)
+
+    @node
+    def PL():
+        spread = [get(f"X{m}") for m in range(count)]
+        left = [tied(get("Lp"), "PL"), get("Lc")]
+        if SEP:
+            return pl.pallas_call(
+                functools.partial(left_kernel, count, side),
+                out_shape=[jax.ShapeDtypeStruct((rows, 2 * rank_cols), BF16)] * side,
+                in_specs=[SMEM] + [VMEM] * (count + side),
+                out_specs=[VMEM] * side,
+                scratch_shapes=[pltpu.VMEM((count, *tokens.shape), BF16)],
+                compiler_params=PARAMS,
+            )(places, *spread, *left)
+        return pl.pallas_call(
+            functools.partial(left_kernel, count, side),
+            out_shape=[jax.ShapeDtypeStruct((side * rows, 2 * rank_cols), kind) for kind in (F32, BF16)],
+            in_specs=[SMEM] + [VMEM] * (count + side),
+            out_specs=[VMEM] * 2,
+            scratch_shapes=[pltpu.VMEM((count, *tokens.shape), BF16)],
+            compiler_params=PARAMS,
+        )(places, *spread, *left)
+
+    @node
+    def sent():
+        return get("PL")[1]
+
+    @node
+    def PLt0():
+        return swap(tied(get("PL")[0], "PLt0"), 0)
+
+    @node
+    def PLt1():
+        return swap(tied(get("PL")[1], "PLt1"), side)
+
+    @node
+    def PLx():
+        return across(tied(get("PL")[1], "PLx"), "narrow", side)
+
+    @node
+    def low():
+        if SEP:
+            return (get("PLt0").astype(F32) + get("PLt1").astype(F32)).astype(BF16)
+        return (get("PL")[0] + get("PLx").astype(F32)).astype(BF16)
+
+    @node
+    def PLc():
+        return across(tied(get("low"), "PLc"), "narrow", 1)
+
+    @node
+    def lowag():
+        return lax.all_gather(tied(get("low"), "lowag"), "narrow", axis=0, tiled=True)
+
+    @node
+    def Rp():
+        return jnp.stack(
+            [
+                gate_right.reshape(rank_cols, inner),
+                up_right.reshape(rank_cols, inner),
+                jnp.swapaxes(down_left, 1, 2).reshape(rank_cols, inner),
             ]
-            come += lax.ppermute(spread[side * a], ("wide", "narrow"), pairs)
-        mine[a] = jnp.where(holds, mine[a], come)
-    mine = jnp.concatenate(mine, axis=0)
-    own_features = [mine] + [across(mine, "narrow", e) for e in range(1, side)]
-
-    left = jnp.concatenate(
-        [jnp.swapaxes(a, 1, 2).reshape(rank_cols, a.shape[1]) for a in (gate_left, up_left)], axis=0
-    )
-    left = [left] + [across(left, "narrow", e) for e in range(1, side)]
-
-    low = pl.pallas_call(
-        functools.partial(left_kernel, count, side),
-        out_shape=[jax.ShapeDtypeStruct((rows, 2 * rank_cols), BF16)] * side,
-        in_specs=[SMEM] + [VMEM] * (count + side),
-        out_specs=[VMEM] * side,
-        scratch_shapes=[pltpu.VMEM((count, *tokens.shape), BF16)],
+        )
+
+    @node
+    def part():
+        if not YR:
+            return get("Rp")
+        half = rank_cols // 2
+        return lax.dynamic_slice_in_dim(get("Rp"), lax.axis_index("groups") * half, half, axis=1)
+
+    @node
+    def far():
+        return across(tied(get("part"), "far"), "wide", 2)
+
+    @node
+    def near():
+        return across(tied(get("part"), "near"), "wide", 1)
+
+    @node
+    def C():
+        return across(tied(get("far"), "C"), "wide", 1)
+
+    @node
+    def close():
+        return across(jnp.stack([get("part"), tied(get("far"), "close")]), "wide", 1)
+
+    @node
+    def brought():
+        return jnp.stack([get("close")[0], get("far"), get("close")[1]])
+
+    @node
+    def Y():
+        return lax.ppermute(tied(get("brought"), "Y"), "groups", [(0, 1), (1, 0)])
+
+    @node
+    def mm1():
+        own = [tied(get("mine"), "mm1"), get("mc")]
+        if SEP:
+            return pl.pallas_call(
+                functools.partial(base_kernel, count, side),
+                out_shape=[jax.ShapeDtypeStruct((rows, 2 * inner), F32 if k == 0 else BF16) for k in range(count)],
+                in_specs=[SMEM] + [VMEM] * (side + 2),
+                out_specs=[VMEM] * count,
+                scratch_shapes=[pltpu.VMEM((count * rows, 2 * inner), F32)],
+                compiler_params=PARAMS,
+            )(places, *own, base_gate, base_up)
+        wide_cols = 2 * inner + 2 * rank_cols
+        return pl.pallas_call(
+            functools.partial(base_kernel, count, side),
+            out_shape=[jax.ShapeDtypeStruct((rows, wide_cols), F32 if k == 0 else BF16) for k in range(count)],
+            in_specs=[SMEM] + [VMEM] * (2 * side + 2),
+            out_specs=[VMEM] * count,
+            scratch_shapes=[
+                pltpu.VMEM((count * rows, 2 * inner), F32),
+                pltpu.VMEM((count * rows, 2 * rank_cols), BF16),
+            ],
+            compiler_params=PARAMS,
+        )(places, *own, get("low"), get("PLc"), base_gate, base_up)
+
+    @node
+    def sums0():
+        return get("mm1")[0]
+
+    for k in range(1, count):
+        nodes[f"P{k}"] = lambda k=k: across(tied(get("mm1")[k], f"P{k}"), "wide", k)
+
+    @node
+    def weight():
+        expert_ids = lax.broadcasted_iota(jnp.int32, (1, 1, experts), 2)
+        named = routes[:, :, None] == expert_ids
+        delta_ids = jnp.sum(jnp.where(named, delta_of[None, None, :], 0), axis=2)
+        slots = ((delta_ids // held) ^ place) * held + delta_ids % held
+        return jnp.sum(jnp.where(slots[:, :, None] == expert_ids, gate_weights[:, :, None], 0.0), axis=1)
+
+    sums = [get("sums0")] + [get(f"P{k}") for k in steps]
+    extra = [get("lowag")] if SEP else []
+    if YR:
+        fac = [get("Rp"), get("brought"), get("Y")]
+        more = [pltpu.VMEM((count - 1, *get("Rp").shape), BF16)]
+    else:
+        fac = [get("Rp"), get("near"), get("far"), get("C")]
+        more = []
+    ins = [places, *sums, *extra, get("weight"), *fac]
+    hsum, *parts = pl.pallas_call(
+        functools.partial(hidden_kernel, count, held),
+        out_shape=[jax.ShapeDtypeStruct((rows, inner), BF16)]
+        + [jax.ShapeDtypeStruct((rows, side * rank_cols), F32 if e == 0 else BF16) for e in range(side)],
+        in_specs=[SMEM] + [VMEM] * (len(ins) - 1),
+        out_specs=[VMEM] * (side + 1),
+        scratch_shapes=[pltpu.VMEM((count, rows, rank_cols), F32)] + more,
         compiler_params=PARAMS,
-    )(places, *spread, *left)
-    low = sum(swap(low[q], side * q).astype(F32) for q in range(side)).astype(BF16)
-
-    sums = pl.pallas_call(
-        functools.partial(base_kernel, count, side),
-        out_shape=[jax.ShapeDtypeStruct((rows, 2 * inner), F32 if k == 0 else BF16) for k in range(count)],
-        in_specs=[SMEM] + [VMEM] * (side + 2),
-        out_specs=[VMEM] * count,
-        scratch_shapes=[pltpu.VMEM((count * rows, 2 * inner), F32)],
-        compiler_params=PARAMS,
-    )(places, *own_features, base_gate, base_up)
-
-    packed = jnp.stack(
-        [
-            gate_right.reshape(rank_cols, inner),
-            up_right.reshape(rank_cols, inner),
-            jnp.swapaxes(down_left, 1, 2).reshape(rank_cols, inner),
-        ]
-    )
-    factors = doubled(packed, "wide", bits[::-1], sums[0])
-    low = lax.all_gather(after(low, sums[0]), "narrow", axis=0, tiled=True)
-    sums = [sums[0]] + [across(sums[k], "wide", k) for k in steps]
-
-    expert_ids = lax.broadcasted_iota(jnp.int32, (1, 1, experts), 2)
-    named = routes[:, :, None] == expert_ids
-    delta_ids = jnp.sum(jnp.where(named, delta_of[None, None, :], 0), axis=2)
-    slots = ((delta_ids // held) ^ place) * held + delta_ids % held
-    weight = jnp.sum(jnp.where(slots[:, :, None] == expert_ids, gate_weights[:, :, None], 0.0), axis=1)
-
-    hidden = pl.pallas_call(
-        functools.partial(hidden_kernel, count, held),
-        out_shape=[
-            jax.ShapeDtypeStruct((rows, rank_cols + (inner if k == 0 else 0)), BF16) for k in range(count)
-        ],
-        in_specs=[SMEM] + [VMEM] * (2 * count + 2),
-        out_specs=[VMEM] * count,
-        scratch_shapes=[pltpu.VMEM((count, rows, rank_cols), BF16)],
-        compiler_params=PARAMS,
-    )(places, *sums, low, weight, *factors)
-
-    hidden = [swap(hidden[k], k) for k in range(count)]
-    low_sum = sum(h[:, -rank_cols:].astype(F32) for h in hidden).astype(BF16)
-    hs = jnp.concatenate([hidden[0][:, :inner], low_sum], axis=1)
+    )(*ins)
+    part = parts[0] + sum(across(parts[e], "narrow", e).astype(F32) for e in range(1, side))
+    part = jnp.split(part.astype(BF16), side, axis=1)
+    first = swap(jnp.concatenate([hsum, part[0]], axis=1))
+    low_sum = first[:, inner:].astype(F32) + sum(swap(part[b], side * b).astype(F32) for b in range(1, side))
+    hs = jnp.concatenate([first[:, :inner], low_sum.astype(BF16)], axis=1)
     hs = lax.all_gather(hs, "narrow", axis=0, tiled=True)
     outs = pl.pallas_call(
         functools.partial(down_kernel, count),

time: 86.1 us -> 83.5 us (0.970)
  starting transfers between devices: 37.9 us -> 32.9 us
  waiting for transfers between devices: 25.9 us -> 27.6 us
    ppermute x8 -> x9, waiting for transfers between devices: 4.34 us -> 13 us  [across(): return lax.ppermute(a, axis, [(i, i ^ k) for i in range(count)])]
    ppermute x6, waiting for transfers between devices: 6.05 us -> 2.21 us  [the longest x4 1.42 us: X(): return lax.ppermute(tied(tokens, f'X{m}'), ('wide', 'narrow'), pairs)]
    ppermute x6 -> x4, starting transfers between devices: 10.5 us -> 6.9 us  [swap(): return lax.ppermute(a, ('wide', 'narrow'), pairs)]
    ppermute x3, waiting for transfers between devices: 11.8 us -> 9.22 us  [ahead(): return lax.ppermute(a, 'wide', [(i, (i + k) % count) for i in range(count)])]
    ppermute x8 -> x9, starting transfers between devices: 8.4 us -> 6.99 us  [across(): return lax.ppermute(a, axis, [(i, i ^ k) for i in range(count)])]
    ppermute x6, starting transfers between devices: 16.5 us -> 15.1 us  [the longest x4 8.76 us: X(): return lax.ppermute(tied(tokens, f'X{m}'), ('wide', 'narrow'), pairs)]
    ppermute x3, starting transfers between devices: 2.55 us -> 3.88 us  [ahead(): return lax.ppermute(a, 'wide', [(i, (i + k) % count) for i in range(count)])]
    all_gather x1, blocking collectives: 7.6 us -> 8.77 us  [stationary_shards(): hs = lax.all_gather(hs, 'narrow', axis=0, tiled=True)]
  transfers between devices with their start and end apart: 23 -> 22, of which waited for: 8 -> 9; matrix products, arithmetic and copies ran while one was open for 2% -> 2% of each run, Pallas kernels for 3% -> 3%
where the time goes in v3:
time: 83.5 us; the launch traced here: 83.2 us
  starting transfers between devices  32.9 us (39%)
  waiting for transfers between devices  27.6 us (33%)
  blocking collectives  14.2 us (17%)
  Pallas kernels  5.36 us (6%)
  other arithmetic  2.17 us (3%)
    ppermute x9, waiting for transfers between devices, across(): return lax.ppermute(a, axis, [(i, i ^ k) for i in range(count)])  13 us
    ppermute x3, waiting for transfers between devices, ahead(): return lax.ppermute(a, 'wide', [(i, (i + k) % count) for i in range(count)])  9.22 us
    all_gather x1, blocking collectives, stationary_shards(): hs = lax.all_gather(hs, 'narrow', axis=0, tiled=True)  8.77 us
    ppermute x4, starting transfers between devices, X(): return lax.ppermute(tied(tokens, f'X{m}'), ('wide', 'narrow'), pairs)  8.76 us
    ppermute x9, starting transfers between devices, across(): return lax.ppermute(a, axis, [(i, i ^ k) for i in range(count)])  6.99 us
    ppermute x4, starting transfers between devices, swap(): return lax.ppermute(a, ('wide', 'narrow'), pairs)  6.9 us
    ppermute x2, starting transfers between devices, xe(): return lax.ppermute(tied(get(f'X{m}'), f'xe{m}'), ('wide', 'narrow'), pairs)  6.38 us
    all_gather x1, blocking collectives, lowag(): lax.all_gather(tied(get('low'), 'lowag'), 'narrow', axis=0, tiled=True)  5.43 us
  transfers between devices with their start and end apart: 22, of which 9 were waited for; matrix products, arithmetic and copies ran while one was open for 2% of the time, Pallas kernels for 3%

profile of v3, /device:TPU:0, one launch (start us, length us, event | category | flops | bytes accessed | tf_op | source)
XLA Modules:
  0.0 83.2 jit_solution(4372810424662851434)
XLA Ops:
  0.0 4.0 %collective-permute-start.2 = (bf16[64,1024]{1,0:T(8,128)(2,1)}, bf16[64,1024]{1,0:T(8,128)(2,1)S(1)}, u32[]{:S(2)}, u32[]{:S(2)}) collective-permute-start(bf16[64,1024]{1,0:T(8,128)(2,1)} %param.13), channel_id=1, source_target_pairs={{0,8},{1,12},{2,10},{3,14},{4,9},{5,13},{6,11},{7,15},{8,0},{9,4},... | collective-permute-start | bytes 393224 | tf_op jit(solution)/shard_map/ppermute | solution.py:248
  4.0 1.6 %collective-permute-start = (bf16[64,1024]{1,0:T(8,128)(2,1)}, bf16[64,1024]{1,0:T(8,128)(2,1)S(1)}, u32[]{:S(2)}, u32[]{:S(2)}) collective-permute-start(bf16[64,1024]{1,0:T(8,128)(2,1)} %param.13), channel_id=1, source_target_pairs={{0,0},{1,4},{2,2},{3,6},{4,1},{5,5},{6,3},{7,7},{8,8},{9,12},{10,1... | collective-permute-start | bytes 393224 | tf_op jit(solution)/shard_map/ppermute | solution.py:248
  5.6 3.2 %collective-permute-start.4 = (bf16[64,1024]{1,0:T(8,128)(2,1)}, bf16[64,1024]{1,0:T(8,128)(2,1)S(1)}, u32[]{:S(2)}, u32[]{:S(2)}) collective-permute-start(bf16[64,1024]{1,0:T(8,128)(2,1)} %param.13), channel_id=1, source_target_pairs={{0,4},{1,0},{2,6},{3,2},{4,5},{5,1},{6,7},{7,3},{8,12},{9,8},{10,1... | collective-permute-start | bytes 393224 | tf_op jit(solution)/shard_map/ppermute | solution.py:248
  8.8 0.0 collective-permute-start.5
  8.8 1.1 %pad_maximum_fusion.refs_4_ = bf16[256,1024]{1,0:T(8,128)(2,1)S(1)} fusion(bf16[128,1024]{1,0:T(8,128)(2,1)} %bitcast.16, bf16[128,1024]{1,0:T(8,128)(2,1)} %bitcast.17), kind=kLoop, calls=%fused_computation | loop fusion | flops 1048576 | bytes 1048576 | tf_op jit(solution)/shard_map/concatenate | solution.py:274
  9.9 0.1 collective-permute-start.6
  10.0 1.4 %collective-permute-done.2.refs_2_ = bf16[64,1024]{1,0:T(8,128)(2,1)S(1)} collective-permute-done((bf16[64,1024]{1,0:T(8,128)(2,1)}, bf16[64,1024]{1,0:T(8,128)(2,1)S(1)}, u32[]{:S(2)}, u32[]{:S(2)}) %collective-permute-start.2) | collective-permute-done | bytes 131104 | tf_op jit(solution)/shard_map/ppermute | solution.py:248
  11.4 3.4 %collective-permute-start.3 = (bf16[64,1024]{1,0:T(8,128)(2,1)S(1)}, bf16[64,1024]{1,0:T(8,128)(2,1)S(1)}, u32[]{:S(2)}, u32[]{:S(2)}) collective-permute-start(bf16[64,1024]{1,0:T(8,128)(2,1)S(1)} %collective-permute-done.2.refs_2_), channel_id=1, source_target_pairs={{0,2},{1,3},{4,6},{5,7},{10,8},{11,9},{14,12},{15,13},{16,18},{17,... | collective-permute-start | bytes 393224 | tf_op jit(solution)/shard_map/ppermute | solution.py:259
  14.8 0.1 pad_add_fusion.place
  14.9 0.0 copy-done.4
  14.9 0.0 copy-done.6
  14.9 0.0 collective-permute-done.refs_0_
  14.9 0.2 collective-permute-start.13
  15.1 0.0 collective-permute-done.4.refs_1_
  15.1 3.0 %collective-permute-start.1 = (bf16[64,1024]{1,0:T(8,128)(2,1)S(1)}, bf16[64,1024]{1,0:T(8,128)(2,1)S(1)}, u32[]{:S(2)}, u32[]{:S(2)}) collective-permute-start(bf16[64,1024]{1,0:T(8,128)(2,1)S(1)} %collective-permute-done.refs_0_), channel_id=1, source_target_pairs={{0,2},{1,3},{4,6},{5,7},{10,8},{11,9},{14,12},{15,13},{16,18},{17,... | collective-permute-start | bytes 393224 | tf_op jit(solution)/shard_map/ppermute | solution.py:259
  18.1 0.0 collective-permute-done.5.refs_3_
  18.1 0.0 collective-permute-done.3
  18.1 2.2 %collective-permute-start.14 = (bf16[3,128,384]{2,1,0:T(8,128)(2,1)S(1)}, bf16[3,128,384]{2,1,0:T(8,128)(2,1)S(1)}, u32[]{:S(2)}, u32[]{:S(2)}) collective-permute-start(bf16[3,128,384]{2,1,0:T(8,128)(2,1)S(1)} %pad_maximum_fusion.1.refs_6_), channel_id=1, source_target_pairs={{0,8},{4,12},{8,0},{12,4},{1,9},{5,13},{9,1},{13,5},{2,10},{6,14},... | collective-permute-start | bytes 884744 | tf_op jit(solution)/shard_map/ppermute | solution.py:231
  20.3 0.8 collective-permute-done.1
  21.2 0.0 copy-start
  21.2 0.0 copy-start.1
  21.2 0.0 collective-permute-done.6.refs_5_
  21.2 1.0 %shard_map.127 = (bf16[64,256]{1,0:T(8,128)(2,1)S(1)}, bf16[64,256]{1,0:T(8,128)(2,1)S(1)}) custom-call(s32[3]{0:T(128)S(1)} %pad_add_fusion.place, bf16[64,1024]{1,0:T(8,128)(2,1)S(1)} %collective-permute-done.refs_0_, bf16[64,1024]{1,0:T(8,128)(2,1)S(1)} %collective-permute-done.4.refs_1_, bf16[64,1024]{1,0:T(8,128)(2,1)S(1)} %collective-permute-done.2.refs_2_, ...), custom_call_target="tpu_custom_call" | custom-call | tf_op jit(solution)/shard_map/pallas_call | solution.py:287
  22.3 0.0 copy-start.9
  22.3 0.1 collective-permute-start.7
  22.4 0.6 copy-done.9
  22.9 0.1 select_reduce_fusion.1
  23.0 2.4 %collective-permute-start.12 = (bf16[64,256]{1,0:T(8,128)(2,1)S(1)}, bf16[64,256]{1,0:T(8,128)(2,1)S(1)}, u32[]{:S(2)}, u32[]{:S(2)}) collective-permute-start(bf16[64,256]{1,0:T(8,128)(2,1)S(1)} %get-tuple-element.22), channel_id=1, source_target_pairs={{0,8},{1,12},{2,0},{3,4},{4,9},{5,13},{6,1},{7,5},{8,10},{9,14},{1... | collective-permute-start | bytes 98312 | tf_op jit(solution)/shard_map/ppermute | solution.py:228
  25.4 0.7 collective-permute-start.11
  26.1 0.0 collective-permute-done.7.refs_1_
  26.1 0.0 copy-done
  26.1 0.0 copy-start.8
  26.1 1.4 %shard_map.128 = (f32[64,768]{1,0:T(8,128)S(1)}, bf16[64,768]{1,0:T(8,128)(2,1)S(1)}, bf16[64,768]{1,0:T(8,128)(2,1)S(1)}, bf16[64,768]{1,0:T(8,128)(2,1)S(1)}) custom-call(s32[3]{0:T(128)S(1)} %pad_add_fusion.place, bf16[128,1024]{1,0:T(8,128)(2,1)S(1)} %pad_maximum_fusion.2.refs_0_, bf16[128,1024]{1,0:T(8,128)(2,1)S(1)} %collective-permute-done.7.refs_1_, ...), custom_call_target="tpu_custom_call" | custom-call | tf_op jit(solution)/shard_map/pallas_call | solution.py:379
  27.4 7.8 %collective-permute-done.14.refs_8_ = bf16[3,128,384]{2,1,0:T(8,128)(2,1)S(1)} collective-permute-done((bf16[3,128,384]{2,1,0:T(8,128)(2,1)S(1)}, bf16[3,128,384]{2,1,0:T(8,128)(2,1)S(1)}, u32[]{:S(2)}, u32[]{:S(2)}) %collective-permute-start.14) | collective-permute-done | bytes 294944 | tf_op jit(solution)/shard_map/ppermute | solution.py:231
  35.3 0.0 collective-permute-start.15
  35.3 0.1 copy.16.refs_5_
  35.4 1.9 %collective-permute-start.10 = (bf16[64,768]{1,0:T(8,128)(2,1)S(1)}, bf16[64,768]{1,0:T(8,128)(2,1)S(1)}, u32[]{:S(2)}, u32[]{:S(2)}) collective-permute-start(bf16[64,768]{1,0:T(8,128)(2,1)S(1)} %get-tuple-element.27), channel_id=1, source_target_pairs={{0,12},{4,8},{8,4},{12,0},{1,13},{5,9},{9,5},{13,1},{2,14},{6,10},... | collective-permute-start | bytes 294920 | tf_op jit(solution)/shard_map/ppermute | solution.py:231
  37.3 0.0 collective-permute-done.12
  37.3 1.1 %collective-permute-start.8 = (bf16[64,768]{1,0:T(8,128)(2,1)S(1)}, bf16[64,768]{1,0:T(8,128)(2,1)S(1)}, u32[]{:S(2)}, u32[]{:S(2)}) collective-permute-start(bf16[64,768]{1,0:T(8,128)(2,1)S(1)} %get-tuple-element.25), channel_id=1, source_target_pairs={{0,4},{4,0},{8,12},{12,8},{1,5},{5,1},{9,13},{13,9},{2,6},{6,2},{1... | collective-permute-start | bytes 294920 | tf_op jit(solution)/shard_map/ppermute | solution.py:231
  38.4 0.0 collective-permute-done.11
  38.4 1.4 %collective-permute-start.9 = (bf16[64,768]{1,0:T(8,128)(2,1)S(1)}, bf16[64,768]{1,0:T(8,128)(2,1)S(1)}, u32[]{:S(2)}, u32[]{:S(2)}) collective-permute-start(bf16[64,768]{1,0:T(8,128)(2,1)S(1)} %get-tuple-element.26), channel_id=1, source_target_pairs={{0,8},{4,12},{8,0},{12,4},{1,9},{5,13},{9,1},{13,5},{2,10},{6,14},... | collective-permute-start | bytes 294920 | tf_op jit(solution)/shard_map/ppermute | solution.py:231
  39.8 5.4 %all_gather.6.refs_4_ = bf16[256,256]{1,0:T(8,128)(2,1)S(1)} all-gather(bf16[64,256]{1,0:T(8,128)(2,1)S(1)} %add_convert_fusion.2), channel_id=1, replica_groups=mesh['groups'=2,'wide'=4,'narrow'=4] {'narrow'}, dimensions={0}, use_global_device_ids=true | all-gather | bytes 163840 | tf_op jit(solution)/shard_map/all_gather | solution.py:332
  45.2 0.0 collective-permute-done.13.refs_7_
  45.2 1.8 %collective-permute-done.10.refs_3_ = bf16[64,768]{1,0:T(8,128)(2,1)S(1)} collective-permute-done((bf16[64,768]{1,0:T(8,128)(2,1)S(1)}, bf16[64,768]{1,0:T(8,128)(2,1)S(1)}, u32[]{:S(2)}, u32[]{:S(2)}) %collective-permute-start.10) | collective-permute-done | bytes 98336 | tf_op jit(solution)/shard_map/ppermute | solution.py:231
  47.0 2.2 %collective-permute-done.8.refs_1_ = bf16[64,768]{1,0:T(8,128)(2,1)S(1)} collective-permute-done((bf16[64,768]{1,0:T(8,128)(2,1)S(1)}, bf16[64,768]{1,0:T(8,128)(2,1)S(1)}, u32[]{:S(2)}, u32[]{:S(2)}) %collective-permute-start.8) | collective-permute-done | bytes 98336 | tf_op jit(solution)/shard_map/ppermute | solution.py:231
  49.2 0.0 collective-permute-done.9.refs_2_
  49.2 0.0 collective-permute-done.15.refs_9_
  49.2 1.8 %shard_map.129 = (bf16[64,384]{1,0:T(8,128)(2,1)S(1)}, f32[64,256]{1,0:T(8,128)S(1)}, bf16[64,256]{1,0:T(8,128)(2,1)S(1)}) custom-call(s32[3]{0:T(128)S(1)} %pad_add_fusion.place, f32[64,768]{1,0:T(8,128)S(1)} %get-tuple-element.24.refs_0_, bf16[64,768]{1,0:T(8,128)(2,1)S(1)} %collective-permute-done.8.refs_1_, ...), custom_call_target="tpu_custom_call" | custom-call | tf_op jit(solution)/shard_map/pallas_call | solution.py:424
  51.0 0.0 copy-start.2
  51.0 0.1 collective-permute-start.16
  51.1 1.2 %collective-permute-done.16 = bf16[64,256]{1,0:T(8,128)(2,1)S(1)} collective-permute-done((bf16[64,256]{1,0:T(8,128)(2,1)S(1)}, bf16[64,256]{1,0:T(8,128)(2,1)S(1)}, u32[]{:S(2)}, u32[]{:S(2)}) %collective-permute-start.16) | collective-permute-done | bytes 32800 | tf_op jit(solution)/shard_map/ppermute | solution.py:231
  52.3 0.7 collective-permute-start.17
  53.0 3.2 %collective-permute-start.18 = (bf16[64,128]{1,0:T(8,128)(2,1)S(1)}, bf16[64,128]{1,0:T(8,128)(2,1)S(1)}, u32[]{:S(2)}, u32[]{:S(2)}) collective-permute-start(bf16[64,128]{1,0:T(8,128)(2,1)S(1)} %get-tuple-element.40), channel_id=1, source_target_pairs={{0,8},{1,12},{2,0},{3,4},{4,9},{5,13},{6,1},{7,5},{8,10},{9,14},{1... | collective-permute-start | bytes 49160 | tf_op jit(solution)/shard_map/ppermute | solution.py:228
  56.2 0.0 collective-permute-done.17
  56.2 3.2 %collective-permute-done.18 = bf16[64,128]{1,0:T(8,128)(2,1)S(1)} collective-permute-done((bf16[64,128]{1,0:T(8,128)(2,1)S(1)}, bf16[64,128]{1,0:T(8,128)(2,1)S(1)}, u32[]{:S(2)}, u32[]{:S(2)}) %collective-permute-start.18) | collective-permute-done | bytes 16416 | tf_op jit(solution)/shard_map/ppermute | solution.py:228
  59.4 8.8 %all_gather.7.hs = bf16[256,512]{1,0:T(8,128)(2,1)S(1)} all-gather(bf16[64,512]{1,0:T(8,128)(2,1)S(1)} %pad_maximum_fusion.4), channel_id=1, replica_groups=mesh['groups'=2,'wide'=4,'narrow'=4] {'narrow'}, dimensions={0}, use_global_device_ids=true | all-gather | bytes 327680 | tf_op jit(solution)/shard_map/all_gather | solution.py:438
  68.2 1.2 %shard_map.130 = (f32[64,1024]{1,0:T(8,128)S(1)}, bf16[64,1024]{1,0:T(8,128)(2,1)S(1)}, bf16[64,1024]{1,0:T(8,128)(2,1)S(1)}, bf16[64,1024]{1,0:T(8,128)(2,1)S(1)}) custom-call(s32[3]{0:T(128)S(1)} %pad_add_fusion.place, bf16[256,512]{1,0:T(8,128)(2,1)S(1)} %all_gather.7.hs, bf16[384,1024]{1,0:T(8,128)(2,1)S(1)} %copy-done.2, bf16[128,1024]{1,0:T(8,128)(2,1)S(1)} %bitcast.15), custom_call_target="tpu_custom_call" | custom-call | tf_op jit(solution)/shard_map/pallas_call | solution.py:439
  69.4 0.2 collective-permute-start.19
  69.6 2.2 %collective-permute-start.20 = (bf16[64,1024]{1,0:T(8,128)(2,1)S(1)}, bf16[64,1024]{1,0:T(8,128)(2,1)S(1)}, u32[]{:S(2)}, u32[]{:S(2)}) collective-permute-start(bf16[64,1024]{1,0:T(8,128)(2,1)S(1)} %get-tuple-element.37), channel_id=1, source_target_pairs={{0,8},{4,12},{8,0},{12,4},{1,9},{5,13},{9,1},{13,5},{2,10},{6,14},... | collective-permute-start | bytes 393224 | tf_op jit(solution)/shard_map/ppermute | solution.py:234
  71.8 1.5 %collective-permute-start.21 = (bf16[64,1024]{1,0:T(8,128)(2,1)S(1)}, bf16[64,1024]{1,0:T(8,128)(2,1)S(1)}, u32[]{:S(2)}, u32[]{:S(2)}) collective-permute-start(bf16[64,1024]{1,0:T(8,128)(2,1)S(1)} %get-tuple-element.38), channel_id=1, source_target_pairs={{0,12},{4,0},{8,4},{12,8},{1,13},{5,1},{9,5},{13,9},{2,14},{6,2},{... | collective-permute-start | bytes 393224 | tf_op jit(solution)/shard_map/ppermute | solution.py:234
  73.3 4.4 %collective-permute-done.19 = bf16[64,1024]{1,0:T(8,128)(2,1)S(1)} collective-permute-done((bf16[64,1024]{1,0:T(8,128)(2,1)S(1)}, bf16[64,1024]{1,0:T(8,128)(2,1)S(1)}, u32[]{:S(2)}, u32[]{:S(2)}) %collective-permute-start.19) | collective-permute-done | bytes 131104 | tf_op jit(solution)/shard_map/ppermute | solution.py:234
  77.7 4.8 %collective-permute-done.20 = bf16[64,1024]{1,0:T(8,128)(2,1)S(1)} collective-permute-done((bf16[64,1024]{1,0:T(8,128)(2,1)S(1)}, bf16[64,1024]{1,0:T(8,128)(2,1)S(1)}, u32[]{:S(2)}, u32[]{:S(2)}) %collective-permute-start.20) | collective-permute-done | bytes 131104 | tf_op jit(solution)/shard_map/ppermute | solution.py:234
  82.5 0.0 collective-permute-done.21
  82.5 0.7 add_convert_fusion
  (24 shorter events, 0.2 us)
Async XLA Ops:
  0.0 11.4 %collective-permute-start.2 = (bf16[64,1024]{1,0:T(8,128)(2,1)}, bf16[64,1024]{1,0:T(8,128)(2,1)S(1)}, u32[]{:S(2)}, u32[]{:S(2)}) collective-permute-start(bf16[64,1024]{1,0:T(8,128)(2,1)} %param.13), channel_id=1, source_target_pairs={{0,8},{1,12},{2,10},{3,14},{4,9},{5,13},{6,11},{7,15},{8,0},{9,4},... | collective-permute-start | bytes 393224 | tf_op jit(solution)/shard_map/ppermute | solution.py:248
  4.0 10.9 %collective-permute-start = (bf16[64,1024]{1,0:T(8,128)(2,1)}, bf16[64,1024]{1,0:T(8,128)(2,1)S(1)}, u32[]{:S(2)}, u32[]{:S(2)}) collective-permute-start(bf16[64,1024]{1,0:T(8,128)(2,1)} %param.13), channel_id=1, source_target_pairs={{0,0},{1,4},{2,2},{3,6},{4,1},{5,5},{6,3},{7,7},{8,8},{9,12},{10,1... | collective-permute-start | bytes 393224 | tf_op jit(solution)/shard_map/ppermute | solution.py:248
  5.6 9.5 %collective-permute-start.4 = (bf16[64,1024]{1,0:T(8,128)(2,1)}, bf16[64,1024]{1,0:T(8,128)(2,1)S(1)}, u32[]{:S(2)}, u32[]{:S(2)}) collective-permute-start(bf16[64,1024]{1,0:T(8,128)(2,1)} %param.13), channel_id=1, source_target_pairs={{0,4},{1,0},{2,6},{3,2},{4,5},{5,1},{6,7},{7,3},{8,12},{9,8},{10,1... | collective-permute-start | bytes 393224 | tf_op jit(solution)/shard_map/ppermute | solution.py:248
  8.8 9.3 %collective-permute-start.5 = (bf16[64,1024]{1,0:T(8,128)(2,1)}, bf16[64,1024]{1,0:T(8,128)(2,1)S(1)}, u32[]{:S(2)}, u32[]{:S(2)}) collective-permute-start(bf16[64,1024]{1,0:T(8,128)(2,1)} %param.13), channel_id=1, source_target_pairs={{0,12},{1,8},{2,14},{3,10},{4,13},{5,9},{6,15},{7,11},{8,4},{9,0},... | collective-permute-start | bytes 393224 | tf_op jit(solution)/shard_map/ppermute | solution.py:248
  8.8 6.1 %copy-start.4 = (bf16[4,384,32]{1,2,0:T(8,128)(2,1)S(1)}, bf16[4,384,32]{1,2,0:T(8,128)(2,1)}, u32[]{:S(2)}) copy-start(bf16[4,384,32]{1,2,0:T(8,128)(2,1)} %param.24) | copy-start | bytes 294916
  8.8 6.1 %copy-start.5 = (bf16[4,32,384]{2,1,0:T(8,128)(2,1)S(1)}, bf16[4,32,384]{2,1,0:T(8,128)(2,1)}, u32[]{:S(2)}) copy-start(bf16[4,32,384]{2,1,0:T(8,128)(2,1)} %param.23) | copy-start | bytes 294916
  8.8 6.1 %copy-start.6 = (bf16[4,32,384]{2,1,0:T(8,128)(2,1)S(1)}, bf16[4,32,384]{2,1,0:T(8,128)(2,1)}, u32[]{:S(2)}) copy-start(bf16[4,32,384]{2,1,0:T(8,128)(2,1)} %param.21) | copy-start | bytes 294916
  9.9 11.3 %collective-permute-start.6 = (bf16[256,1024]{1,0:T(8,128)(2,1)S(1)}, bf16[256,1024]{1,0:T(8,128)(2,1)S(1)}, u32[]{:S(2)}, u32[]{:S(2)}) collective-permute-start(bf16[256,1024]{1,0:T(8,128)(2,1)S(1)} %pad_maximum_fusion.refs_4_), channel_id=1, source_target_pairs={{0,1},{1,0},{2,3},{3,2},{4,5},{5,4},{6,7},{7,6},{8,9},{9,8},{10,11... | collective-permute-start | bytes 1572872 | tf_op jit(solution)/shard_map/ppermute | solution.py:231
  11.4 6.7 %collective-permute-start.3 = (bf16[64,1024]{1,0:T(8,128)(2,1)S(1)}, bf16[64,1024]{1,0:T(8,128)(2,1)S(1)}, u32[]{:S(2)}, u32[]{:S(2)}) collective-permute-start(bf16[64,1024]{1,0:T(8,128)(2,1)S(1)} %collective-permute-done.2.refs_2_), channel_id=1, source_target_pairs={{0,2},{1,3},{4,6},{5,7},{10,8},{11,9},{14,12},{15,13},{16,18},{17,... | collective-permute-start | bytes 393224 | tf_op jit(solution)/shard_map/ppermute | solution.py:259
  14.9 30.3 %collective-permute-start.13 = (bf16[3,128,384]{2,1,0:T(8,128)(2,1)S(1)}, bf16[3,128,384]{2,1,0:T(8,128)(2,1)S(1)}, u32[]{:S(2)}, u32[]{:S(2)}) collective-permute-start(bf16[3,128,384]{2,1,0:T(8,128)(2,1)S(1)} %pad_maximum_fusion.1.refs_6_), channel_id=1, source_target_pairs={{0,4},{4,0},{8,12},{12,8},{1,5},{5,1},{9,13},{13,9},{2,6},{6,2},{1... | collective-permute-start | bytes 884744 | tf_op jit(solution)/shard_map/ppermute | solution.py:231
  15.1 6.0 %collective-permute-start.1 = (bf16[64,1024]{1,0:T(8,128)(2,1)S(1)}, bf16[64,1024]{1,0:T(8,128)(2,1)S(1)}, u32[]{:S(2)}, u32[]{:S(2)}) collective-permute-start(bf16[64,1024]{1,0:T(8,128)(2,1)S(1)} %collective-permute-done.refs_0_), channel_id=1, source_target_pairs={{0,2},{1,3},{4,6},{5,7},{10,8},{11,9},{14,12},{15,13},{16,18},{17,... | collective-permute-start | bytes 393224 | tf_op jit(solution)/shard_map/ppermute | solution.py:259
  18.1 17.2 %collective-permute-start.14 = (bf16[3,128,384]{2,1,0:T(8,128)(2,1)S(1)}, bf16[3,128,384]{2,1,0:T(8,128)(2,1)S(1)}, u32[]{:S(2)}, u32[]{:S(2)}) collective-permute-start(bf16[3,128,384]{2,1,0:T(8,128)(2,1)S(1)} %pad_maximum_fusion.1.refs_6_), channel_id=1, source_target_pairs={{0,8},{4,12},{8,0},{12,4},{1,9},{5,13},{9,1},{13,5},{2,10},{6,14},... | collective-permute-start | bytes 884744 | tf_op jit(solution)/shard_map/ppermute | solution.py:231
  21.2 1.2 %copy-start.7 = (s32[64,8]{0,1:T(8,128)S(1)}, s32[64,8]{0,1:T(8,128)}, u32[]{:S(2)}) copy-start(s32[64,8]{0,1:T(8,128)} %param.14) | copy-start | bytes 6148
  21.2 4.9 %copy-start = (bf16[1024,384]{1,0:T(8,128)(2,1)S(1)}, bf16[1024,384]{1,0:T(8,128)(2,1)}, u32[]{:S(2)}) copy-start(bf16[1024,384]{1,0:T(8,128)(2,1)} %refs_2_.1) | copy-start | bytes 2359300
  21.2 4.9 %copy-start.1 = (bf16[1024,384]{1,0:T(8,128)(2,1)S(1)}, bf16[1024,384]{1,0:T(8,128)(2,1)}, u32[]{:S(2)}) copy-start(bf16[1024,384]{1,0:T(8,128)(2,1)} %refs_3_.1) | copy-start | bytes 2359300
  22.3 0.7 copy-start.9
  22.3 3.8 %collective-permute-start.7 = (bf16[128,1024]{1,0:T(8,128)(2,1)S(1)}, bf16[128,1024]{1,0:T(8,128)(2,1)S(1)}, u32[]{:S(2)}, u32[]{:S(2)}) collective-permute-start(bf16[128,1024]{1,0:T(8,128)(2,1)S(1)} %pad_maximum_fusion.2.refs_0_), channel_id=1, source_target_pairs={{0,1},{1,0},{2,3},{3,2},{4,5},{5,4},{6,7},{7,6},{8,9},{9,8},{10,11... | collective-permute-start | bytes 786440 | tf_op jit(solution)/shard_map/ppermute | solution.py:231
  23.0 14.3 %collective-permute-start.12 = (bf16[64,256]{1,0:T(8,128)(2,1)S(1)}, bf16[64,256]{1,0:T(8,128)(2,1)S(1)}, u32[]{:S(2)}, u32[]{:S(2)}) collective-permute-start(bf16[64,256]{1,0:T(8,128)(2,1)S(1)} %get-tuple-element.22), channel_id=1, source_target_pairs={{0,8},{1,12},{2,0},{3,4},{4,9},{5,13},{6,1},{7,5},{8,10},{9,14},{1... | collective-permute-start | bytes 98312 | tf_op jit(solution)/shard_map/ppermute | solution.py:228
  25.4 13.0 %collective-permute-start.11 = (bf16[64,256]{1,0:T(8,128)(2,1)S(1)}, bf16[64,256]{1,0:T(8,128)(2,1)S(1)}, u32[]{:S(2)}, u32[]{:S(2)}) collective-permute-start(bf16[64,256]{1,0:T(8,128)(2,1)S(1)} %get-tuple-element.28), channel_id=1, source_target_pairs={{0,0},{1,4},{2,8},{3,12},{4,1},{5,5},{6,9},{7,13},{8,2},{9,6},{10,... | collective-permute-start | bytes 98312 | tf_op jit(solution)/shard_map/ppermute | solution.py:228
  26.1 9.2 %copy-start.8 = (f32[64,8]{0,1:T(8,128)S(1)}, f32[64,8]{0,1:T(8,128)}, u32[]{:S(2)}) copy-start(f32[64,8]{0,1:T(8,128)} %param.15) | copy-start | bytes 6148
  35.3 13.9 %collective-permute-start.15 = (bf16[3,128,384]{2,1,0:T(8,128)(2,1)S(1)}, bf16[3,128,384]{2,1,0:T(8,128)(2,1)S(1)}, u32[]{:S(2)}, u32[]{:S(2)}) collective-permute-start(bf16[3,128,384]{2,1,0:T(8,128)(2,1)S(1)} %collective-permute-done.14.refs_8_), channel_id=1, source_target_pairs={{0,4},{4,0},{8,12},{12,8},{1,5},{5,1},{9,13},{13,9},{2,6},{6,2},{1... | collective-permute-start | bytes 884744 | tf_op jit(solution)/shard_map/ppermute | solution.py:231
  35.4 11.6 %collective-permute-start.10 = (bf16[64,768]{1,0:T(8,128)(2,1)S(1)}, bf16[64,768]{1,0:T(8,128)(2,1)S(1)}, u32[]{:S(2)}, u32[]{:S(2)}) collective-permute-start(bf16[64,768]{1,0:T(8,128)(2,1)S(1)} %get-tuple-element.27), channel_id=1, source_target_pairs={{0,12},{4,8},{8,4},{12,0},{1,13},{5,9},{9,5},{13,1},{2,14},{6,10},... | collective-permute-start | bytes 294920 | tf_op jit(solution)/shard_map/ppermute | solution.py:231
  37.3 11.9 %collective-permute-start.8 = (bf16[64,768]{1,0:T(8,128)(2,1)S(1)}, bf16[64,768]{1,0:T(8,128)(2,1)S(1)}, u32[]{:S(2)}, u32[]{:S(2)}) collective-permute-start(bf16[64,768]{1,0:T(8,128)(2,1)S(1)} %get-tuple-element.25), channel_id=1, source_target_pairs={{0,4},{4,0},{8,12},{12,8},{1,5},{5,1},{9,13},{13,9},{2,6},{6,2},{1... | collective-permute-start | bytes 294920 | tf_op jit(solution)/shard_map/ppermute | solution.py:231
  38.4 10.8 %collective-permute-start.9 = (bf16[64,768]{1,0:T(8,128)(2,1)S(1)}, bf16[64,768]{1,0:T(8,128)(2,1)S(1)}, u32[]{:S(2)}, u32[]{:S(2)}) collective-permute-start(bf16[64,768]{1,0:T(8,128)(2,1)S(1)} %get-tuple-element.26), channel_id=1, source_target_pairs={{0,8},{4,12},{8,0},{12,4},{1,9},{5,13},{9,1},{13,5},{2,10},{6,14},... | collective-permute-start | bytes 294920 | tf_op jit(solution)/shard_map/ppermute | solution.py:231
  49.2 19.0 %copy-start.3 = (bf16[4,32,1024]{2,1,0:T(8,128)(2,1)S(1)}, bf16[4,32,1024]{2,1,0:T(8,128)(2,1)}, u32[]{:S(2)}) copy-start(bf16[4,32,1024]{2,1,0:T(8,128)(2,1)} %param.25) | copy-start | bytes 786436
  51.0 17.2 %copy-start.2 = (bf16[384,1024]{1,0:T(8,128)(2,1)S(1)}, bf16[384,1024]{1,0:T(8,128)(2,1)}, u32[]{:S(2)}) copy-start(bf16[384,1024]{1,0:T(8,128)(2,1)} %w.1) | copy-start | bytes 2359300
  51.0 1.3 %collective-permute-start.16 = (bf16[64,256]{1,0:T(8,128)(2,1)S(1)}, bf16[64,256]{1,0:T(8,128)(2,1)S(1)}, u32[]{:S(2)}, u32[]{:S(2)}) collective-permute-start(bf16[64,256]{1,0:T(8,128)(2,1)S(1)} %get-tuple-element.34), channel_id=1, source_target_pairs={{0,1},{1,0},{2,3},{3,2},{4,5},{5,4},{6,7},{7,6},{8,9},{9,8},{10,11... | collective-permute-start | bytes 98312 | tf_op jit(solution)/shard_map/ppermute | solution.py:231
  52.3 3.9 %collective-permute-start.17 = (bf16[64,512]{1,0:T(8,128)(2,1)S(1)}, bf16[64,512]{1,0:T(8,128)(2,1)S(1)}, u32[]{:S(2)}, u32[]{:S(2)}) collective-permute-start(bf16[64,512]{1,0:T(8,128)(2,1)S(1)} %pad_maximum_fusion.3), channel_id=1, source_target_pairs={{0,0},{1,4},{2,8},{3,12},{4,1},{5,5},{6,9},{7,13},{8,2},{9,6},{10,... | collective-permute-start | bytes 196616 | tf_op jit(solution)/shard_map/ppermute | solution.py:228
  53.0 6.4 %collective-permute-start.18 = (bf16[64,128]{1,0:T(8,128)(2,1)S(1)}, bf16[64,128]{1,0:T(8,128)(2,1)S(1)}, u32[]{:S(2)}, u32[]{:S(2)}) collective-permute-start(bf16[64,128]{1,0:T(8,128)(2,1)S(1)} %get-tuple-element.40), channel_id=1, source_target_pairs={{0,8},{1,12},{2,0},{3,4},{4,9},{5,13},{6,1},{7,5},{8,10},{9,14},{1... | collective-permute-start | bytes 49160 | tf_op jit(solution)/shard_map/ppermute | solution.py:228
  69.4 8.3 %collective-permute-start.19 = (bf16[64,1024]{1,0:T(8,128)(2,1)S(1)}, bf16[64,1024]{1,0:T(8,128)(2,1)S(1)}, u32[]{:S(2)}, u32[]{:S(2)}) collective-permute-start(bf16[64,1024]{1,0:T(8,128)(2,1)S(1)} %get-tuple-element.36), channel_id=1, source_target_pairs={{0,4},{4,8},{8,12},{12,0},{1,5},{5,9},{9,13},{13,1},{2,6},{6,10},{... | collective-permute-start | bytes 393224 | tf_op jit(solution)/shard_map/ppermute | solution.py:234
  69.6 12.9 %collective-permute-start.20 = (bf16[64,1024]{1,0:T(8,128)(2,1)S(1)}, bf16[64,1024]{1,0:T(8,128)(2,1)S(1)}, u32[]{:S(2)}, u32[]{:S(2)}) collective-permute-start(bf16[64,1024]{1,0:T(8,128)(2,1)S(1)} %get-tuple-element.37), channel_id=1, source_target_pairs={{0,8},{4,12},{8,0},{12,4},{1,9},{5,13},{9,1},{13,5},{2,10},{6,14},... | collective-permute-start | bytes 393224 | tf_op jit(solution)/shard_map/ppermute | solution.py:234
  71.8 10.7 %collective-permute-start.21 = (bf16[64,1024]{1,0:T(8,128)(2,1)S(1)}, bf16[64,1024]{1,0:T(8,128)(2,1)S(1)}, u32[]{:S(2)}, u32[]{:S(2)}) collective-permute-start(bf16[64,1024]{1,0:T(8,128)(2,1)S(1)} %get-tuple-element.38), channel_id=1, source_target_pairs={{0,12},{4,0},{8,4},{12,8},{1,13},{5,1},{9,5},{13,9},{2,14},{6,2},{... | collective-permute-start | bytes 393224 | tf_op jit(solution)/shard_map/ppermute | solution.py:234

commit v4 on v3

--- a/solution.py
+++ b/solution.py
@@ -137,42 +137,59 @@
         outs[k][...] = total[pl.ds(start, rows), :].astype(outs[k].dtype)
 
 
+def expert_terms(k, spot, held, place, gate, up, low, weight, factors):
+    rows, cols = gate.shape
+    rank_cols = factors.shape[1]
+    owner = lax.broadcasted_iota(jnp.int32, (rows, rank_cols), 1) // (rank_cols // held)
+    here = low[pl.ds(pl.multiple_of((place[0] ^ k) * rows, rows), rows), :]
+    sides = []
+    for half in (here[:, :rank_cols], here[:, rank_cols:]):
+        zero = jnp.zeros_like(half)
+        sides.append(jnp.concatenate([jnp.where(owner == i, half, zero) for i in range(held)], axis=0))
+    g = jnp.dot(sides[0], factors[0], preferred_element_type=F32)
+    u = jnp.dot(sides[1], factors[1], preferred_element_type=F32)
+    total, parts = jnp.zeros((rows, cols), F32), []
+    for i in range(held):
+        gi = gate + g[i * rows : (i + 1) * rows]
+        ui = up + u[i * rows : (i + 1) * rows]
+        h = (0.5 * gi) * (1.0 + jnp.tanh(0.5 * gi)) * ui
+        slot = spot * held + i
+        hw = h * weight[:, slot : slot + 1]
+        total += hw
+        parts.append(hw.astype(BF16))
+    back = dot_rows(jnp.concatenate(parts, axis=0), factors[2])
+    block = jnp.zeros((rows, rank_cols), F32)
+    for i in range(held):
+        block += jnp.where(owner == i, back[i * rows : (i + 1) * rows], 0.0)
+    return total, block
+
+
 def hidden_kernel(count, held, place, *refs):
-    gs, (low, weight), rs = refs[:count], refs[count : count + 2], refs[count + 2 : 2 * count + 2]
-    hsum, *outs, hl = refs[2 * count + 2 :]
+    gs, (low, weight), rs = refs[:count], refs[count : count + 2], refs[count + 2 : 2 * count + 1]
+    base, acc, hl = refs[2 * count + 1 :]
+    cols = base.shape[1] // 2
+    base[...] = sum(g[...].astype(F32) for g in gs)
+    total = jnp.zeros(acc.shape, F32)
+    for spot, r in enumerate(rs):
+        k = spot ^ place[2] if spot == count // 2 else spot
+        more, hl[place[0] ^ place[1] ^ k] = expert_terms(
+            k, spot, held, place, base[:, :cols], base[:, cols:], low, weight, r
+        )
+        total += more
+    acc[...] = total
+
+
+def hidden_last_kernel(count, held, place, base, acc, come, low, weight, r, hsum, *refs):
+    outs, hl = refs[:-1], refs[-1]
     side = len(outs)
-    rows, both = gs[0].shape
-    cols = both // 2
-    rank_cols = rs[0].shape[1]
-    rank = rank_cols // held
-    base = sum(g[...].astype(F32) for g in gs)
-    gate, up = base[:, :cols], base[:, cols:]
-    owner = lax.broadcasted_iota(jnp.int32, (rows, rank_cols), 1) // rank
-    acc = jnp.zeros((rows, cols), F32)
-    for k in range(count):
-        start = pl.multiple_of((place[0] ^ k) * rows, rows)
-        here = low[pl.ds(start, rows), :]
-        low_gate, low_up = here[:, :rank_cols], here[:, rank_cols:]
-        zero = jnp.zeros_like(low_gate)
-        lhs_gate = jnp.concatenate([jnp.where(owner == i, low_gate, zero) for i in range(held)], axis=0)
-        lhs_up = jnp.concatenate([jnp.where(owner == i, low_up, zero) for i in range(held)], axis=0)
-        g = jnp.dot(lhs_gate, rs[k][0], preferred_element_type=F32)
-        u = jnp.dot(lhs_up, rs[k][1], preferred_element_type=F32)
-        parts = []
-        for i in range(held):
-            gi = gate + g[i * rows : (i + 1) * rows]
-            ui = up + u[i * rows : (i + 1) * rows]
-            h = (0.5 * gi) * (1.0 + jnp.tanh(0.5 * gi)) * ui
-            slot = k * held + i
-            hw = h * weight[:, slot : slot + 1]
-            acc += hw
-            parts.append(hw.astype(BF16))
-        back = dot_rows(jnp.concatenate(parts, axis=0), rs[k][2])
-        block = jnp.zeros((rows, rank_cols), F32)
-        for i in range(held):
-            block += jnp.where(owner == i, back[i * rows : (i + 1) * rows], 0.0)
-        hl[place[0] ^ place[1] ^ k] = block
-    hsum[...] = acc.astype(BF16)
+    cols = base.shape[1] // 2
+    rank_cols = r.shape[1]
+    hl[...] = come[...]
+    k = (count - 1) ^ place[2]
+    more, hl[place[0] ^ place[1] ^ k] = expert_terms(
+        k, count - 1, held, place, base[:, :cols], base[:, cols:], low, weight, r
+    )
+    hsum[...] = (acc[...] + more).astype(BF16)
     for e in range(side):
         for b in range(side):
             outs[e][:, b * rank_cols : (b + 1) * rank_cols] = hl[side * b + e].astype(outs[e].dtype)
@@ -195,7 +212,7 @@
 PARAMS = pltpu.CompilerParams(vmem_limit_bytes=24 * 2**20)
 
 SEP, YR = True, False
-TIES = {'C': ['sums0'], 'lowag': ['sums0'], 'far': ['X1', 'X3', 'xe2'], 'mc': ['sent']}
+TIES = {'C': ['sums0'], 'lowag': ['sums0'], 'far': ['X1', 'X3', 'xe2'], 'mc': ['sent'], 'PLt0': ['sums0'], 'PLt1': ['sums0']}
 
 def stationary_shards(tokens, routes, gate_weights, delta_of, base_gate, base_up, base_down, gate_left, gate_right, up_left, up_right, down_left, down_right):
     count = lax.axis_size("wide")
@@ -350,7 +367,8 @@
 
     @node
     def far():
-        return across(tied(get("part"), "far"), "wide", 2)
+        pairs = [(g * count + z, g * count + (z ^ 2 ^ g)) for g in range(2) for z in range(count)]
+        return lax.ppermute(tied(get("part"), "far"), ("groups", "wide"), pairs)
 
     @node
     def near():
@@ -358,7 +376,7 @@
 
     @node
     def C():
-        return across(tied(get("far"), "C"), "wide", 1)
+        return lax.ppermute(tied(get("far"), "C"), "groups", [(0, 1), (1, 0)])
 
     @node
     def close():
@@ -409,9 +427,13 @@
         expert_ids = lax.broadcasted_iota(jnp.int32, (1, 1, experts), 2)
         named = routes[:, :, None] == expert_ids
         delta_ids = jnp.sum(jnp.where(named, delta_of[None, None, :], 0), axis=2)
-        slots = ((delta_ids // held) ^ place) * held + delta_ids % held
+        away = (delta_ids // held) ^ place
+        away = jnp.where(away < 2, away, away ^ lax.axis_index("groups"))
+        slots = away * held + delta_ids % held
         return jnp.sum(jnp.where(slots[:, :, None] == expert_ids, gate_weights[:, :, None], 0.0), axis=1)
 
+    for name in ['C']:
+        get(name)
     sums = [get("sums0")] + [get(f"P{k}") for k in steps]
     extra = [get("lowag")] if SEP else []
     if YR:
@@ -421,15 +443,26 @@
         fac = [get("Rp"), get("near"), get("far"), get("C")]
         more = []
     ins = [places, *sums, *extra, get("weight"), *fac]
+    base, acc, hl = pl.pallas_call(
+        functools.partial(hidden_kernel, count, held),
+        out_shape=[
+            jax.ShapeDtypeStruct((rows, 2 * inner), F32),
+            jax.ShapeDtypeStruct((rows, inner), F32),
+            jax.ShapeDtypeStruct((count, rows, rank_cols), F32),
+        ],
+        in_specs=[SMEM] + [VMEM] * (2 * count + 1),
+        out_specs=[VMEM] * 3,
+        compiler_params=PARAMS,
+    )(places, *sums, get("lowag"), get("weight"), *fac[:-1])
     hsum, *parts = pl.pallas_call(
-        functools.partial(hidden_kernel, count, held),
+        functools.partial(hidden_last_kernel, count, held),
         out_shape=[jax.ShapeDtypeStruct((rows, inner), BF16)]
         + [jax.ShapeDtypeStruct((rows, side * rank_cols), F32 if e == 0 else BF16) for e in range(side)],
-        in_specs=[SMEM] + [VMEM] * (len(ins) - 1),
+        in_specs=[SMEM] + [VMEM] * 6,
         out_specs=[VMEM] * (side + 1),
-        scratch_shapes=[pltpu.VMEM((count, rows, rank_cols), F32)] + more,
+        scratch_shapes=[pltpu.VMEM((count, rows, rank_cols), F32)],
         compiler_params=PARAMS,
-    )(*ins)
+    )(places, base, acc, hl, get("lowag"), get("weight"), fac[-1])
     part = parts[0] + sum(across(parts[e], "narrow", e).astype(F32) for e in range(1, side))
     part = jnp.split(part.astype(BF16), side, axis=1)
     first = swap(jnp.concatenate([hsum, part[0]], axis=1))

time: 83.5 us -> 80.3 us (0.962)
  waiting for transfers between devices: 27.6 us -> 20.1 us
  starting transfers between devices: 32.9 us -> 36.2 us
    ppermute x9 -> x7, waiting for transfers between devices: 13 us -> 3.75 us  [across(): return lax.ppermute(a, axis, [(i, i ^ k) for i in range(count)])]
    ppermute x4, starting transfers between devices: 6.9 us -> 10.2 us  [swap(): return lax.ppermute(a, ('wide', 'narrow'), pairs)]
    ppermute x0 -> x2, waiting for transfers between devices: none -> 3.28 us  [the longest x1 3.27 us: far(): return lax.ppermute(tied(get('part'), 'far'), ('groups', 'wide'), pairs)]
    ppermute x0 -> x2, starting transfers between devices: none -> 2.2 us  [the longest x1 2.2 us: far(): return lax.ppermute(tied(get('part'), 'far'), ('groups', 'wide'), pairs)]
    ppermute x9 -> x7, starting transfers between devices: 6.99 us -> 4.79 us  [across(): return lax.ppermute(a, axis, [(i, i ^ k) for i in range(count)])]
    ppermute x4, waiting for transfers between devices: 3.16 us -> 1.65 us  [swap(): return lax.ppermute(a, ('wide', 'narrow'), pairs)]
    pallas_call x0 -> x1, Pallas kernels: none -> 1.01 us  [stationary_shards(): pl.pallas_call(functools.partial(hidden_last_kernel, count, held), out_sh...]
  transfers between devices with their start and end apart: 22 -> 22, of which waited for: 9 -> 9; matrix products, arithmetic and copies ran while one was open for 2% -> 2% of each run, Pallas kernels for 3% -> 5%
where the time goes in v4:
time: 80.3 us; the launch traced here: 80.1 us
  starting transfers between devices  36.2 us (45%)
  waiting for transfers between devices  20.1 us (25%)
  blocking collectives  14.4 us (18%)
  Pallas kernels  6.13 us (8%)
  other arithmetic  2.18 us (3%)
    ppermute x4, starting transfers between devices, swap(): return lax.ppermute(a, ('wide', 'narrow'), pairs)  10.2 us
    ppermute x3, waiting for transfers between devices, ahead(): return lax.ppermute(a, 'wide', [(i, (i + k) % count) for i in range(count)])  9.22 us
    all_gather x1, blocking collectives, stationary_shards(): hs = lax.all_gather(hs, 'narrow', axis=0, tiled=True)  9.01 us
    ppermute x4, starting transfers between devices, X(): return lax.ppermute(tied(tokens, f'X{m}'), ('wide', 'narrow'), pairs)  8.76 us
    ppermute x2, starting transfers between devices, xe(): return lax.ppermute(tied(get(f'X{m}'), f'xe{m}'), ('wide', 'narrow'), pairs)  6.37 us
    all_gather x1, blocking collectives, lowag(): lax.all_gather(tied(get('low'), 'lowag'), 'narrow', axis=0, tiled=True)  5.43 us
    ppermute x7, starting transfers between devices, across(): return lax.ppermute(a, axis, [(i, i ^ k) for i in range(count)])  4.79 us
    ppermute x3, starting transfers between devices, ahead(): return lax.ppermute(a, 'wide', [(i, (i + k) % count) for i in range(count)])  3.88 us
  transfers between devices with their start and end apart: 22, of which 9 were waited for; matrix products, arithmetic and copies ran while one was open for 2% of the time, Pallas kernels for 5%

profile of v4, /device:TPU:0, one launch (start us, length us, event | category | flops | bytes accessed | tf_op | source)
XLA Modules:
  0.0 80.1 jit_solution(8489324565362302987)
XLA Ops:
  0.0 4.0 %collective-permute-start.2 = (bf16[64,1024]{1,0:T(8,128)(2,1)}, bf16[64,1024]{1,0:T(8,128)(2,1)S(1)}, u32[]{:S(2)}, u32[]{:S(2)}) collective-permute-start(bf16[64,1024]{1,0:T(8,128)(2,1)} %param.13), channel_id=1, source_target_pairs={{0,8},{1,12},{2,10},{3,14},{4,9},{5,13},{6,11},{7,15},{8,0},{9,4},... | collective-permute-start | bytes 393224 | tf_op jit(solution)/shard_map/ppermute | solution.py:265
  4.0 1.6 %collective-permute-start = (bf16[64,1024]{1,0:T(8,128)(2,1)}, bf16[64,1024]{1,0:T(8,128)(2,1)S(1)}, u32[]{:S(2)}, u32[]{:S(2)}) collective-permute-start(bf16[64,1024]{1,0:T(8,128)(2,1)} %param.13), channel_id=1, source_target_pairs={{0,0},{1,4},{2,2},{3,6},{4,1},{5,5},{6,3},{7,7},{8,8},{9,12},{10,1... | collective-permute-start | bytes 393224 | tf_op jit(solution)/shard_map/ppermute | solution.py:265
  5.6 3.2 %collective-permute-start.4 = (bf16[64,1024]{1,0:T(8,128)(2,1)}, bf16[64,1024]{1,0:T(8,128)(2,1)S(1)}, u32[]{:S(2)}, u32[]{:S(2)}) collective-permute-start(bf16[64,1024]{1,0:T(8,128)(2,1)} %param.13), channel_id=1, source_target_pairs={{0,4},{1,0},{2,6},{3,2},{4,5},{5,1},{6,7},{7,3},{8,12},{9,8},{10,1... | collective-permute-start | bytes 393224 | tf_op jit(solution)/shard_map/ppermute | solution.py:265
  8.8 0.0 collective-permute-start.5
  8.8 1.1 %pad_maximum_fusion.refs_4_ = bf16[256,1024]{1,0:T(8,128)(2,1)S(1)} fusion(bf16[128,1024]{1,0:T(8,128)(2,1)} %bitcast.16, bf16[128,1024]{1,0:T(8,128)(2,1)} %bitcast.17), kind=kLoop, calls=%fused_computation | loop fusion | flops 1048576 | bytes 1048576 | tf_op jit(solution)/shard_map/concatenate | solution.py:291
  9.9 0.1 collective-permute-start.6
  10.0 1.4 %collective-permute-done.2.refs_2_ = bf16[64,1024]{1,0:T(8,128)(2,1)S(1)} collective-permute-done((bf16[64,1024]{1,0:T(8,128)(2,1)}, bf16[64,1024]{1,0:T(8,128)(2,1)S(1)}, u32[]{:S(2)}, u32[]{:S(2)}) %collective-permute-start.2) | collective-permute-done | bytes 131104 | tf_op jit(solution)/shard_map/ppermute | solution.py:265
  11.4 3.4 %collective-permute-start.3 = (bf16[64,1024]{1,0:T(8,128)(2,1)S(1)}, bf16[64,1024]{1,0:T(8,128)(2,1)S(1)}, u32[]{:S(2)}, u32[]{:S(2)}) collective-permute-start(bf16[64,1024]{1,0:T(8,128)(2,1)S(1)} %collective-permute-done.2.refs_2_), channel_id=1, source_target_pairs={{0,2},{1,3},{4,6},{5,7},{10,8},{11,9},{14,12},{15,13},{16,18},{17,... | collective-permute-start | bytes 393224 | tf_op jit(solution)/shard_map/ppermute | solution.py:276
  14.8 0.1 pad_add_fusion.place
  14.9 0.0 collective-permute-done.refs_0_
  14.9 0.2 collective-permute-start.13
  15.1 0.0 collective-permute-done.4.refs_1_
  15.1 3.0 %collective-permute-start.1 = (bf16[64,1024]{1,0:T(8,128)(2,1)S(1)}, bf16[64,1024]{1,0:T(8,128)(2,1)S(1)}, u32[]{:S(2)}, u32[]{:S(2)}) collective-permute-start(bf16[64,1024]{1,0:T(8,128)(2,1)S(1)} %collective-permute-done.refs_0_), channel_id=1, source_target_pairs={{0,2},{1,3},{4,6},{5,7},{10,8},{11,9},{14,12},{15,13},{16,18},{17,... | collective-permute-start | bytes 393224 | tf_op jit(solution)/shard_map/ppermute | solution.py:276
  18.1 0.0 collective-permute-done.5.refs_3_
  18.1 0.0 collective-permute-done.3
  18.1 2.2 %collective-permute-start.14 = (bf16[3,128,384]{2,1,0:T(8,128)(2,1)S(1)}, bf16[3,128,384]{2,1,0:T(8,128)(2,1)S(1)}, u32[]{:S(2)}, u32[]{:S(2)}) collective-permute-start(bf16[3,128,384]{2,1,0:T(8,128)(2,1)S(1)} %pad_maximum_fusion.1.refs_6_), channel_id=1, source_target_pairs={{0,8},{4,12},{8,0},{12,4},{16,28},{20,24},{24,20},{28,16},{1,9},{5... | collective-permute-start | bytes 884744 | tf_op jit(solution)/shard_map/ppermute | solution.py:371
  20.3 0.8 collective-permute-done.1
  21.2 0.0 copy-start
  21.2 0.0 copy-start.1
  21.2 0.0 collective-permute-done.6.refs_5_
  21.2 1.0 %shard_map.127 = (bf16[64,256]{1,0:T(8,128)(2,1)S(1)}, bf16[64,256]{1,0:T(8,128)(2,1)S(1)}) custom-call(s32[3]{0:T(128)S(1)} %pad_add_fusion.place, bf16[64,1024]{1,0:T(8,128)(2,1)S(1)} %collective-permute-done.refs_0_, bf16[64,1024]{1,0:T(8,128)(2,1)S(1)} %collective-permute-done.4.refs_1_, bf16[64,1024]{1,0:T(8,128)(2,1)S(1)} %collective-permute-done.2.refs_2_, ...), custom_call_target="tpu_custom_call" | custom-call | tf_op jit(solution)/shard_map/pallas_call | solution.py:304
  22.3 0.0 copy-start.9
  22.3 0.1 collective-permute-start.7
  22.4 0.6 copy-done.9
  22.9 0.1 select_reduce_fusion.1
  23.0 0.8 %collective-permute-done.7.refs_1_ = bf16[128,1024]{1,0:T(8,128)(2,1)S(1)} collective-permute-done((bf16[128,1024]{1,0:T(8,128)(2,1)S(1)}, bf16[128,1024]{1,0:T(8,128)(2,1)S(1)}, u32[]{:S(2)}, u32[]{:S(2)}) %collective-permute-start.7) | collective-permute-done | bytes 262176 | tf_op jit(solution)/shard_map/ppermute | solution.py:248
  23.9 0.0 copy-done
  23.9 1.4 %shard_map.128 = (f32[64,768]{1,0:T(8,128)S(1)}, bf16[64,768]{1,0:T(8,128)(2,1)S(1)}, bf16[64,768]{1,0:T(8,128)(2,1)S(1)}, bf16[64,768]{1,0:T(8,128)(2,1)S(1)}) custom-call(s32[3]{0:T(128)S(1)} %pad_add_fusion.place, bf16[128,1024]{1,0:T(8,128)(2,1)S(1)} %pad_maximum_fusion.2.refs_0_, bf16[128,1024]{1,0:T(8,128)(2,1)S(1)} %collective-permute-done.7.refs_1_, ...), custom_call_target="tpu_custom_call" | custom-call | tf_op jit(solution)/shard_map/pallas_call | solution.py:397
  25.2 0.7 collective-permute-start.11
  25.9 6.1 %collective-permute-start.12 = (bf16[64,256]{1,0:T(8,128)(2,1)S(1)}, bf16[64,256]{1,0:T(8,128)(2,1)S(1)}, u32[]{:S(2)}, u32[]{:S(2)}) collective-permute-start(bf16[64,256]{1,0:T(8,128)(2,1)S(1)} %get-tuple-element.35), channel_id=1, source_target_pairs={{0,8},{1,12},{2,0},{3,4},{4,9},{5,13},{6,1},{7,5},{8,10},{9,14},{1... | collective-permute-start | bytes 98312 | tf_op jit(solution)/shard_map/ppermute | solution.py:245
  32.0 3.3 %collective-permute-done.14.refs_8_ = bf16[3,128,384]{2,1,0:T(8,128)(2,1)S(1)} collective-permute-done((bf16[3,128,384]{2,1,0:T(8,128)(2,1)S(1)}, bf16[3,128,384]{2,1,0:T(8,128)(2,1)S(1)}, u32[]{:S(2)}, u32[]{:S(2)}) %collective-permute-start.14) | collective-permute-done | bytes 294944 | tf_op jit(solution)/shard_map/ppermute | solution.py:371
  35.3 0.0 collective-permute-start.15
  35.3 0.0 copy-done.8
  35.3 0.1 copy.16.refs_5_.weight
  35.4 1.3 %collective-permute-start.10 = (bf16[64,768]{1,0:T(8,128)(2,1)S(1)}, bf16[64,768]{1,0:T(8,128)(2,1)S(1)}, u32[]{:S(2)}, u32[]{:S(2)}) collective-permute-start(bf16[64,768]{1,0:T(8,128)(2,1)S(1)} %get-tuple-element.32), channel_id=1, source_target_pairs={{0,12},{4,8},{8,4},{12,0},{1,13},{5,9},{9,5},{13,1},{2,14},{6,10},... | collective-permute-start | bytes 294920 | tf_op jit(solution)/shard_map/ppermute | solution.py:248
  36.7 0.0 collective-permute-done.11
  36.7 0.8 %collective-permute-start.8 = (bf16[64,768]{1,0:T(8,128)(2,1)S(1)}, bf16[64,768]{1,0:T(8,128)(2,1)S(1)}, u32[]{:S(2)}, u32[]{:S(2)}) collective-permute-start(bf16[64,768]{1,0:T(8,128)(2,1)S(1)} %get-tuple-element.30), channel_id=1, source_target_pairs={{0,4},{4,0},{8,12},{12,8},{1,5},{5,1},{9,13},{13,9},{2,6},{6,2},{1... | collective-permute-start | bytes 294920 | tf_op jit(solution)/shard_map/ppermute | solution.py:248
  37.5 0.0 collective-permute-done.12
  37.5 2.3 %collective-permute-start.9 = (bf16[64,768]{1,0:T(8,128)(2,1)S(1)}, bf16[64,768]{1,0:T(8,128)(2,1)S(1)}, u32[]{:S(2)}, u32[]{:S(2)}) collective-permute-start(bf16[64,768]{1,0:T(8,128)(2,1)S(1)} %get-tuple-element.31), channel_id=1, source_target_pairs={{0,8},{4,12},{8,0},{12,4},{1,9},{5,13},{9,1},{13,5},{2,10},{6,14},... | collective-permute-start | bytes 294920 | tf_op jit(solution)/shard_map/ppermute | solution.py:248
  39.9 5.4 %all_gather.6.refs_4_.low = bf16[256,256]{1,0:T(8,128)(2,1)S(1)} all-gather(bf16[64,256]{1,0:T(8,128)(2,1)S(1)} %add_convert_fusion.2), channel_id=1, replica_groups=mesh['groups'=2,'wide'=4,'narrow'=4] {'narrow'}, dimensions={0}, use_global_device_ids=true | all-gather | bytes 163840 | tf_op jit(solution)/shard_map/all_gather | solution.py:349
  45.3 0.0 collective-permute-done.13.refs_7_
  45.3 0.0 collective-permute-done.10.refs_3_
  45.3 0.0 collective-permute-done.8.refs_1_
  45.3 1.7 %collective-permute-done.9.refs_2_ = bf16[64,768]{1,0:T(8,128)(2,1)S(1)} collective-permute-done((bf16[64,768]{1,0:T(8,128)(2,1)S(1)}, bf16[64,768]{1,0:T(8,128)(2,1)S(1)}, u32[]{:S(2)}, u32[]{:S(2)}) %collective-permute-start.9) | collective-permute-done | bytes 98336 | tf_op jit(solution)/shard_map/ppermute | solution.py:248
  47.0 1.6 %shard_map.129 = (f32[64,768]{1,0:T(8,128)S(1)}, f32[64,384]{1,0:T(8,128)S(1)}, f32[4,64,128]{2,1,0:T(8,128)S(1)}) custom-call(s32[3]{0:T(128)S(1)} %pad_add_fusion.place, f32[64,768]{1,0:T(8,128)S(1)} %get-tuple-element.29.refs_0_, bf16[64,768]{1,0:T(8,128)(2,1)S(1)} %collective-permute-done.8.refs_1_, bf16[64,768]{1,0:T(8,128)(2,1)S(1)} %collective-permute-done.9.refs_2_, ...), custom_call_target="tpu_custom_call" | custom-call | tf_op jit(solution)/shard_map/pallas_call | solution.py:446
  48.6 0.0 collective-permute-done.15.r
  48.6 0.0 copy-start.2
  48.6 1.0 %shard_map.130 = (bf16[64,384]{1,0:T(8,128)(2,1)S(1)}, f32[64,256]{1,0:T(8,128)S(1)}, bf16[64,256]{1,0:T(8,128)(2,1)S(1)}) custom-call(s32[3]{0:T(128)S(1)} %pad_add_fusion.place, f32[64,768]{1,0:T(8,128)S(1)} %get-tuple-element.38.base, f32[64,384]{1,0:T(8,128)S(1)} %get-tuple-element.39.acc, f32[4,64,128]{2,1,0:T(8,128)S(1)} %get-tuple-element.40.come, ...), custom_call_target="tpu_custom_call" | custom-call | tf_op jit(solution)/shard_map/pallas_call | solution.py:457
  49.6 0.1 collective-permute-start.16
  49.7 1.2 %collective-permute-done.16 = bf16[64,256]{1,0:T(8,128)(2,1)S(1)} collective-permute-done((bf16[64,256]{1,0:T(8,128)(2,1)S(1)}, bf16[64,256]{1,0:T(8,128)(2,1)S(1)}, u32[]{:S(2)}, u32[]{:S(2)}) %collective-permute-start.16) | collective-permute-done | bytes 32800 | tf_op jit(solution)/shard_map/ppermute | solution.py:248
  50.9 0.7 collective-permute-start.17
  51.6 2.7 %collective-permute-start.18 = (bf16[64,128]{1,0:T(8,128)(2,1)S(1)}, bf16[64,128]{1,0:T(8,128)(2,1)S(1)}, u32[]{:S(2)}, u32[]{:S(2)}) collective-permute-start(bf16[64,128]{1,0:T(8,128)(2,1)S(1)} %get-tuple-element.50), channel_id=1, source_target_pairs={{0,8},{1,12},{2,0},{3,4},{4,9},{5,13},{6,1},{7,5},{8,10},{9,14},{1... | collective-permute-start | bytes 49160 | tf_op jit(solution)/shard_map/ppermute | solution.py:245
  54.3 0.0 collective-permute-done.17
  54.3 0.0 copy-start.3
  54.4 1.6 %collective-permute-done.18 = bf16[64,128]{1,0:T(8,128)(2,1)S(1)} collective-permute-done((bf16[64,128]{1,0:T(8,128)(2,1)S(1)}, bf16[64,128]{1,0:T(8,128)(2,1)S(1)}, u32[]{:S(2)}, u32[]{:S(2)}) %collective-permute-start.18) | collective-permute-done | bytes 16416 | tf_op jit(solution)/shard_map/ppermute | solution.py:245
  56.0 9.0 %all_gather.7.hs = bf16[256,512]{1,0:T(8,128)(2,1)S(1)} all-gather(bf16[64,512]{1,0:T(8,128)(2,1)S(1)} %pad_maximum_fusion.4), channel_id=1, replica_groups=mesh['groups'=2,'wide'=4,'narrow'=4] {'narrow'}, dimensions={0}, use_global_device_ids=true | all-gather | bytes 327680 | tf_op jit(solution)/shard_map/all_gather | solution.py:471
  65.0 1.2 %shard_map.131 = (f32[64,1024]{1,0:T(8,128)S(1)}, bf16[64,1024]{1,0:T(8,128)(2,1)S(1)}, bf16[64,1024]{1,0:T(8,128)(2,1)S(1)}, bf16[64,1024]{1,0:T(8,128)(2,1)S(1)}) custom-call(s32[3]{0:T(128)S(1)} %pad_add_fusion.place, bf16[256,512]{1,0:T(8,128)(2,1)S(1)} %all_gather.7.hs, bf16[384,1024]{1,0:T(8,128)(2,1)S(1)} %copy-done.2, bf16[128,1024]{1,0:T(8,128)(2,1)S(1)} %bitcast.15), custom_call_target="tpu_custom_call" | custom-call | tf_op jit(solution)/shard_map/pallas_call | solution.py:472
  66.2 0.2 collective-permute-start.19
  66.5 2.4 %collective-permute-start.20 = (bf16[64,1024]{1,0:T(8,128)(2,1)S(1)}, bf16[64,1024]{1,0:T(8,128)(2,1)S(1)}, u32[]{:S(2)}, u32[]{:S(2)}) collective-permute-start(bf16[64,1024]{1,0:T(8,128)(2,1)S(1)} %get-tuple-element.47), channel_id=1, source_target_pairs={{0,8},{4,12},{8,0},{12,4},{1,9},{5,13},{9,1},{13,5},{2,10},{6,14},... | collective-permute-start | bytes 393224 | tf_op jit(solution)/shard_map/ppermute | solution.py:251
  68.9 1.2 %collective-permute-start.21 = (bf16[64,1024]{1,0:T(8,128)(2,1)S(1)}, bf16[64,1024]{1,0:T(8,128)(2,1)S(1)}, u32[]{:S(2)}, u32[]{:S(2)}) collective-permute-start(bf16[64,1024]{1,0:T(8,128)(2,1)S(1)} %get-tuple-element.48), channel_id=1, source_target_pairs={{0,12},{4,0},{8,4},{12,8},{1,13},{5,1},{9,5},{13,9},{2,14},{6,2},{... | collective-permute-start | bytes 393224 | tf_op jit(solution)/shard_map/ppermute | solution.py:251
  70.1 4.4 %collective-permute-done.19 = bf16[64,1024]{1,0:T(8,128)(2,1)S(1)} collective-permute-done((bf16[64,1024]{1,0:T(8,128)(2,1)S(1)}, bf16[64,1024]{1,0:T(8,128)(2,1)S(1)}, u32[]{:S(2)}, u32[]{:S(2)}) %collective-permute-start.19) | collective-permute-done | bytes 131104 | tf_op jit(solution)/shard_map/ppermute | solution.py:251
  74.5 4.8 %collective-permute-done.20 = bf16[64,1024]{1,0:T(8,128)(2,1)S(1)} collective-permute-done((bf16[64,1024]{1,0:T(8,128)(2,1)S(1)}, bf16[64,1024]{1,0:T(8,128)(2,1)S(1)}, u32[]{:S(2)}, u32[]{:S(2)}) %collective-permute-start.20) | collective-permute-done | bytes 131104 | tf_op jit(solution)/shard_map/ppermute | solution.py:251
  79.3 0.0 collective-permute-done.21
  79.3 0.7 add_convert_fusion
  (25 shorter events, 0.2 us)
Async XLA Ops:
  0.0 11.4 %collective-permute-start.2 = (bf16[64,1024]{1,0:T(8,128)(2,1)}, bf16[64,1024]{1,0:T(8,128)(2,1)S(1)}, u32[]{:S(2)}, u32[]{:S(2)}) collective-permute-start(bf16[64,1024]{1,0:T(8,128)(2,1)} %param.13), channel_id=1, source_target_pairs={{0,8},{1,12},{2,10},{3,14},{4,9},{5,13},{6,11},{7,15},{8,0},{9,4},... | collective-permute-start | bytes 393224 | tf_op jit(solution)/shard_map/ppermute | solution.py:265
  4.0 10.9 %collective-permute-start = (bf16[64,1024]{1,0:T(8,128)(2,1)}, bf16[64,1024]{1,0:T(8,128)(2,1)S(1)}, u32[]{:S(2)}, u32[]{:S(2)}) collective-permute-start(bf16[64,1024]{1,0:T(8,128)(2,1)} %param.13), channel_id=1, source_target_pairs={{0,0},{1,4},{2,2},{3,6},{4,1},{5,5},{6,3},{7,7},{8,8},{9,12},{10,1... | collective-permute-start | bytes 393224 | tf_op jit(solution)/shard_map/ppermute | solution.py:265
  5.6 9.5 %collective-permute-start.4 = (bf16[64,1024]{1,0:T(8,128)(2,1)}, bf16[64,1024]{1,0:T(8,128)(2,1)S(1)}, u32[]{:S(2)}, u32[]{:S(2)}) collective-permute-start(bf16[64,1024]{1,0:T(8,128)(2,1)} %param.13), channel_id=1, source_target_pairs={{0,4},{1,0},{2,6},{3,2},{4,5},{5,1},{6,7},{7,3},{8,12},{9,8},{10,1... | collective-permute-start | bytes 393224 | tf_op jit(solution)/shard_map/ppermute | solution.py:265
  8.8 9.3 %collective-permute-start.5 = (bf16[64,1024]{1,0:T(8,128)(2,1)}, bf16[64,1024]{1,0:T(8,128)(2,1)S(1)}, u32[]{:S(2)}, u32[]{:S(2)}) collective-permute-start(bf16[64,1024]{1,0:T(8,128)(2,1)} %param.13), channel_id=1, source_target_pairs={{0,12},{1,8},{2,14},{3,10},{4,13},{5,9},{6,15},{7,11},{8,4},{9,0},... | collective-permute-start | bytes 393224 | tf_op jit(solution)/shard_map/ppermute | solution.py:265
  8.8 6.1 %copy-start.4 = (bf16[4,384,32]{1,2,0:T(8,128)(2,1)S(1)}, bf16[4,384,32]{1,2,0:T(8,128)(2,1)}, u32[]{:S(2)}) copy-start(bf16[4,384,32]{1,2,0:T(8,128)(2,1)} %param.24) | copy-start | bytes 294916
  8.8 6.1 %copy-start.5 = (bf16[4,32,384]{2,1,0:T(8,128)(2,1)S(1)}, bf16[4,32,384]{2,1,0:T(8,128)(2,1)}, u32[]{:S(2)}) copy-start(bf16[4,32,384]{2,1,0:T(8,128)(2,1)} %param.23) | copy-start | bytes 294916
  8.8 6.1 %copy-start.6 = (bf16[4,32,384]{2,1,0:T(8,128)(2,1)S(1)}, bf16[4,32,384]{2,1,0:T(8,128)(2,1)}, u32[]{:S(2)}) copy-start(bf16[4,32,384]{2,1,0:T(8,128)(2,1)} %param.21) | copy-start | bytes 294916
  9.9 11.3 %collective-permute-start.6 = (bf16[256,1024]{1,0:T(8,128)(2,1)S(1)}, bf16[256,1024]{1,0:T(8,128)(2,1)S(1)}, u32[]{:S(2)}, u32[]{:S(2)}) collective-permute-start(bf16[256,1024]{1,0:T(8,128)(2,1)S(1)} %pad_maximum_fusion.refs_4_), channel_id=1, source_target_pairs={{0,1},{1,0},{2,3},{3,2},{4,5},{5,4},{6,7},{7,6},{8,9},{9,8},{10,11... | collective-permute-start | bytes 1572872 | tf_op jit(solution)/shard_map/ppermute | solution.py:248
  11.4 6.7 %collective-permute-start.3 = (bf16[64,1024]{1,0:T(8,128)(2,1)S(1)}, bf16[64,1024]{1,0:T(8,128)(2,1)S(1)}, u32[]{:S(2)}, u32[]{:S(2)}) collective-permute-start(bf16[64,1024]{1,0:T(8,128)(2,1)S(1)} %collective-permute-done.2.refs_2_), channel_id=1, source_target_pairs={{0,2},{1,3},{4,6},{5,7},{10,8},{11,9},{14,12},{15,13},{16,18},{17,... | collective-permute-start | bytes 393224 | tf_op jit(solution)/shard_map/ppermute | solution.py:276
  14.9 30.4 %collective-permute-start.13 = (bf16[3,128,384]{2,1,0:T(8,128)(2,1)S(1)}, bf16[3,128,384]{2,1,0:T(8,128)(2,1)S(1)}, u32[]{:S(2)}, u32[]{:S(2)}) collective-permute-start(bf16[3,128,384]{2,1,0:T(8,128)(2,1)S(1)} %pad_maximum_fusion.1.refs_6_), channel_id=1, source_target_pairs={{0,4},{4,0},{8,12},{12,8},{1,5},{5,1},{9,13},{13,9},{2,6},{6,2},{1... | collective-permute-start | bytes 884744 | tf_op jit(solution)/shard_map/ppermute | solution.py:248
  15.1 6.0 %collective-permute-start.1 = (bf16[64,1024]{1,0:T(8,128)(2,1)S(1)}, bf16[64,1024]{1,0:T(8,128)(2,1)S(1)}, u32[]{:S(2)}, u32[]{:S(2)}) collective-permute-start(bf16[64,1024]{1,0:T(8,128)(2,1)S(1)} %collective-permute-done.refs_0_), channel_id=1, source_target_pairs={{0,2},{1,3},{4,6},{5,7},{10,8},{11,9},{14,12},{15,13},{16,18},{17,... | collective-permute-start | bytes 393224 | tf_op jit(solution)/shard_map/ppermute | solution.py:276
  18.1 17.2 %collective-permute-start.14 = (bf16[3,128,384]{2,1,0:T(8,128)(2,1)S(1)}, bf16[3,128,384]{2,1,0:T(8,128)(2,1)S(1)}, u32[]{:S(2)}, u32[]{:S(2)}) collective-permute-start(bf16[3,128,384]{2,1,0:T(8,128)(2,1)S(1)} %pad_maximum_fusion.1.refs_6_), channel_id=1, source_target_pairs={{0,8},{4,12},{8,0},{12,4},{16,28},{20,24},{24,20},{28,16},{1,9},{5... | collective-permute-start | bytes 884744 | tf_op jit(solution)/shard_map/ppermute | solution.py:371
  21.2 1.2 %copy-start.7 = (s32[64,8]{0,1:T(8,128)S(1)}, s32[64,8]{0,1:T(8,128)}, u32[]{:S(2)}) copy-start(s32[64,8]{0,1:T(8,128)} %param.14) | copy-start | bytes 6148
  21.2 2.7 %copy-start = (bf16[1024,384]{1,0:T(8,128)(2,1)S(1)}, bf16[1024,384]{1,0:T(8,128)(2,1)}, u32[]{:S(2)}) copy-start(bf16[1024,384]{1,0:T(8,128)(2,1)} %refs_2_.1) | copy-start | bytes 2359300
  21.2 2.7 %copy-start.1 = (bf16[1024,384]{1,0:T(8,128)(2,1)S(1)}, bf16[1024,384]{1,0:T(8,128)(2,1)}, u32[]{:S(2)}) copy-start(bf16[1024,384]{1,0:T(8,128)(2,1)} %refs_3_.1) | copy-start | bytes 2359300
  22.3 0.7 copy-start.9
  22.3 1.6 %collective-permute-start.7 = (bf16[128,1024]{1,0:T(8,128)(2,1)S(1)}, bf16[128,1024]{1,0:T(8,128)(2,1)S(1)}, u32[]{:S(2)}, u32[]{:S(2)}) collective-permute-start(bf16[128,1024]{1,0:T(8,128)(2,1)S(1)} %pad_maximum_fusion.2.refs_0_), channel_id=1, source_target_pairs={{0,1},{1,0},{2,3},{3,2},{4,5},{5,4},{6,7},{7,6},{8,9},{9,8},{10,11... | collective-permute-start | bytes 786440 | tf_op jit(solution)/shard_map/ppermute | solution.py:248
  23.9 11.4 %copy-start.8 = (f32[64,8]{0,1:T(8,128)S(1)}, f32[64,8]{0,1:T(8,128)}, u32[]{:S(2)}) copy-start(f32[64,8]{0,1:T(8,128)} %param.15) | copy-start | bytes 6148
  25.2 11.5 %collective-permute-start.11 = (bf16[64,256]{1,0:T(8,128)(2,1)S(1)}, bf16[64,256]{1,0:T(8,128)(2,1)S(1)}, u32[]{:S(2)}, u32[]{:S(2)}) collective-permute-start(bf16[64,256]{1,0:T(8,128)(2,1)S(1)} %get-tuple-element.34), channel_id=1, source_target_pairs={{0,0},{1,4},{2,8},{3,12},{4,1},{5,5},{6,9},{7,13},{8,2},{9,6},{10,... | collective-permute-start | bytes 98312 | tf_op jit(solution)/shard_map/ppermute | solution.py:245
  25.9 11.6 %collective-permute-start.12 = (bf16[64,256]{1,0:T(8,128)(2,1)S(1)}, bf16[64,256]{1,0:T(8,128)(2,1)S(1)}, u32[]{:S(2)}, u32[]{:S(2)}) collective-permute-start(bf16[64,256]{1,0:T(8,128)(2,1)S(1)} %get-tuple-element.35), channel_id=1, source_target_pairs={{0,8},{1,12},{2,0},{3,4},{4,9},{5,13},{6,1},{7,5},{8,10},{9,14},{1... | collective-permute-start | bytes 98312 | tf_op jit(solution)/shard_map/ppermute | solution.py:245
  35.3 13.3 %collective-permute-start.15 = (bf16[3,128,384]{2,1,0:T(8,128)(2,1)S(1)}, bf16[3,128,384]{2,1,0:T(8,128)(2,1)S(1)}, u32[]{:S(2)}, u32[]{:S(2)}) collective-permute-start(bf16[3,128,384]{2,1,0:T(8,128)(2,1)S(1)} %collective-permute-done.14.refs_8_), channel_id=1, source_target_pairs={{0,16},{16,0},{1,17},{17,1},{2,18},{18,2},{3,19},{19,3},{4,20},{20... | collective-permute-start | bytes 884744 | tf_op jit(solution)/shard_map/ppermute | solution.py:379
  35.4 9.9 %collective-permute-start.10 = (bf16[64,768]{1,0:T(8,128)(2,1)S(1)}, bf16[64,768]{1,0:T(8,128)(2,1)S(1)}, u32[]{:S(2)}, u32[]{:S(2)}) collective-permute-start(bf16[64,768]{1,0:T(8,128)(2,1)S(1)} %get-tuple-element.32), channel_id=1, source_target_pairs={{0,12},{4,8},{8,4},{12,0},{1,13},{5,9},{9,5},{13,1},{2,14},{6,10},... | collective-permute-start | bytes 294920 | tf_op jit(solution)/shard_map/ppermute | solution.py:248
  36.7 8.6 %collective-permute-start.8 = (bf16[64,768]{1,0:T(8,128)(2,1)S(1)}, bf16[64,768]{1,0:T(8,128)(2,1)S(1)}, u32[]{:S(2)}, u32[]{:S(2)}) collective-permute-start(bf16[64,768]{1,0:T(8,128)(2,1)S(1)} %get-tuple-element.30), channel_id=1, source_target_pairs={{0,4},{4,0},{8,12},{12,8},{1,5},{5,1},{9,13},{13,9},{2,6},{6,2},{1... | collective-permute-start | bytes 294920 | tf_op jit(solution)/shard_map/ppermute | solution.py:248
  37.5 9.5 %collective-permute-start.9 = (bf16[64,768]{1,0:T(8,128)(2,1)S(1)}, bf16[64,768]{1,0:T(8,128)(2,1)S(1)}, u32[]{:S(2)}, u32[]{:S(2)}) collective-permute-start(bf16[64,768]{1,0:T(8,128)(2,1)S(1)} %get-tuple-element.31), channel_id=1, source_target_pairs={{0,8},{4,12},{8,0},{12,4},{1,9},{5,13},{9,1},{13,5},{2,10},{6,14},... | collective-permute-start | bytes 294920 | tf_op jit(solution)/shard_map/ppermute | solution.py:248
  48.6 16.5 %copy-start.2 = (bf16[384,1024]{1,0:T(8,128)(2,1)S(1)}, bf16[384,1024]{1,0:T(8,128)(2,1)}, u32[]{:S(2)}) copy-start(bf16[384,1024]{1,0:T(8,128)(2,1)} %w.1) | copy-start | bytes 2359300
  49.6 1.3 %collective-permute-start.16 = (bf16[64,256]{1,0:T(8,128)(2,1)S(1)}, bf16[64,256]{1,0:T(8,128)(2,1)S(1)}, u32[]{:S(2)}, u32[]{:S(2)}) collective-permute-start(bf16[64,256]{1,0:T(8,128)(2,1)S(1)} %get-tuple-element.44), channel_id=1, source_target_pairs={{0,1},{1,0},{2,3},{3,2},{4,5},{5,4},{6,7},{7,6},{8,9},{9,8},{10,11... | collective-permute-start | bytes 98312 | tf_op jit(solution)/shard_map/ppermute | solution.py:248
  50.9 3.4 %collective-permute-start.17 = (bf16[64,512]{1,0:T(8,128)(2,1)S(1)}, bf16[64,512]{1,0:T(8,128)(2,1)S(1)}, u32[]{:S(2)}, u32[]{:S(2)}) collective-permute-start(bf16[64,512]{1,0:T(8,128)(2,1)S(1)} %pad_maximum_fusion.3), channel_id=1, source_target_pairs={{0,0},{1,4},{2,8},{3,12},{4,1},{5,5},{6,9},{7,13},{8,2},{9,6},{10,... | collective-permute-start | bytes 196616 | tf_op jit(solution)/shard_map/ppermute | solution.py:245
  51.6 4.4 %collective-permute-start.18 = (bf16[64,128]{1,0:T(8,128)(2,1)S(1)}, bf16[64,128]{1,0:T(8,128)(2,1)S(1)}, u32[]{:S(2)}, u32[]{:S(2)}) collective-permute-start(bf16[64,128]{1,0:T(8,128)(2,1)S(1)} %get-tuple-element.50), channel_id=1, source_target_pairs={{0,8},{1,12},{2,0},{3,4},{4,9},{5,13},{6,1},{7,5},{8,10},{9,14},{1... | collective-permute-start | bytes 49160 | tf_op jit(solution)/shard_map/ppermute | solution.py:245
  54.3 10.7 %copy-start.3 = (bf16[4,32,1024]{2,1,0:T(8,128)(2,1)S(1)}, bf16[4,32,1024]{2,1,0:T(8,128)(2,1)}, u32[]{:S(2)}) copy-start(bf16[4,32,1024]{2,1,0:T(8,128)(2,1)} %param.25) | copy-start | bytes 786436
  66.2 8.3 %collective-permute-start.19 = (bf16[64,1024]{1,0:T(8,128)(2,1)S(1)}, bf16[64,1024]{1,0:T(8,128)(2,1)S(1)}, u32[]{:S(2)}, u32[]{:S(2)}) collective-permute-start(bf16[64,1024]{1,0:T(8,128)(2,1)S(1)} %get-tuple-element.46), channel_id=1, source_target_pairs={{0,4},{4,8},{8,12},{12,0},{1,5},{5,9},{9,13},{13,1},{2,6},{6,10},{... | collective-permute-start | bytes 393224 | tf_op jit(solution)/shard_map/ppermute | solution.py:251
  66.5 12.9 %collective-permute-start.20 = (bf16[64,1024]{1,0:T(8,128)(2,1)S(1)}, bf16[64,1024]{1,0:T(8,128)(2,1)S(1)}, u32[]{:S(2)}, u32[]{:S(2)}) collective-permute-start(bf16[64,1024]{1,0:T(8,128)(2,1)S(1)} %get-tuple-element.47), channel_id=1, source_target_pairs={{0,8},{4,12},{8,0},{12,4},{1,9},{5,13},{9,1},{13,5},{2,10},{6,14},... | collective-permute-start | bytes 393224 | tf_op jit(solution)/shard_map/ppermute | solution.py:251
  68.9 10.4 %collective-permute-start.21 = (bf16[64,1024]{1,0:T(8,128)(2,1)S(1)}, bf16[64,1024]{1,0:T(8,128)(2,1)S(1)}, u32[]{:S(2)}, u32[]{:S(2)}) collective-permute-start(bf16[64,1024]{1,0:T(8,128)(2,1)S(1)} %get-tuple-element.48), channel_id=1, source_target_pairs={{0,12},{4,0},{8,4},{12,8},{1,13},{5,1},{9,5},{13,9},{2,14},{6,2},{... | collective-permute-start | bytes 393224 | tf_op jit(solution)/shard_map/ppermute | solution.py:251

commit v5 on v2

--- a/solution.py
+++ b/solution.py
@@ -112,67 +112,93 @@
 
 
 def left_kernel(count, side, place, *refs):
-    xs, ls, outs, held = refs[:count], refs[count : count + side], refs[count + side : -1], refs[-1]
+    xs, ls, (out, sent, held) = refs[:count], refs[count : count + side], refs[count + side :]
+    rows = xs[0].shape[0]
     for m in range(count):
         held[m] = xs[m][...]
-    for q in range(side):
-        total = jnp.zeros(outs[q].shape, F32)
-        for e in range(side):
-            total += dot_rows(held[place[0] ^ place[1] ^ (side * q + e)], ls[e][...])
-        outs[q][...] = total.astype(BF16)
+    total = jnp.zeros(out.shape, F32)
+    for e in range(side):
+        spots = [place[0] ^ (side * u + (lax.rem(place[1], side) ^ e)) for u in range(side)]
+        total += dot_rows(jnp.concatenate([held[m] for m in spots], axis=0), ls[e][...])
+    out[...] = total
+    sent[...] = total.astype(BF16)
 
 
 def base_kernel(count, side, place, *refs):
-    xs, (wg, wu), outs, total = refs[:side], refs[side : side + 2], refs[side + 2 : -1], refs[-1]
+    xs, lows, (wg, wu), refs = refs[:side], refs[side : 2 * side], refs[2 * side : 2 * side + 2], refs[2 * side + 2 :]
+    outs, (total, low) = refs[:-2], refs[-2:]
     cols = wg.shape[1]
     rows = outs[0].shape[0]
     x = jnp.concatenate([x[...] for x in xs], axis=0)
     total[:, :cols] = jnp.dot(x, wg[...], preferred_element_type=F32)
     total[:, cols:] = jnp.dot(x, wu[...], preferred_element_type=F32)
+    low[...] = jnp.concatenate([low[...] for low in lows], axis=0)
     for k in range(count):
         turn = lax.rem(place[0] ^ place[1] ^ k, side)
         start = pl.multiple_of((turn * side + k // side) * rows, rows)
-        outs[k][...] = total[pl.ds(start, rows), :].astype(outs[k].dtype)
+        outs[k][:, : 2 * cols] = total[pl.ds(start, rows), :].astype(outs[k].dtype)
+        start = pl.multiple_of((turn * side + ((place[0] ^ k) // side)) * rows, rows)
+        outs[k][:, 2 * cols :] = low[pl.ds(start, rows), :].astype(outs[k].dtype)
+
+
+def expert_terms(k, spot, held, place, gate, up, low, weight, factors):
+    rows, cols = gate.shape
+    rank_cols = factors.shape[1]
+    owner = lax.broadcasted_iota(jnp.int32, (rows, rank_cols), 1) // (rank_cols // held)
+    here = low[k]
+    sides = []
+    for half in (here[:, :rank_cols], here[:, rank_cols:]):
+        zero = jnp.zeros_like(half)
+        sides.append(jnp.concatenate([jnp.where(owner == i, half, zero) for i in range(held)], axis=0))
+    g = jnp.dot(sides[0], factors[0], preferred_element_type=F32)
+    u = jnp.dot(sides[1], factors[1], preferred_element_type=F32)
+    total, parts = jnp.zeros((rows, cols), F32), []
+    for i in range(held):
+        gi = gate + g[i * rows : (i + 1) * rows]
+        ui = up + u[i * rows : (i + 1) * rows]
+        h = (gi / (1.0 + jnp.exp(-gi))) * ui
+        slot = spot * held + i
+        hw = h * weight[:, slot : slot + 1]
+        total += hw
+        parts.append(hw.astype(BF16))
+    back = dot_rows(jnp.concatenate(parts, axis=0), factors[2])
+    block = jnp.zeros((rows, rank_cols), F32)
+    for i in range(held):
+        block += jnp.where(owner == i, back[i * rows : (i + 1) * rows], 0.0)
+    return total, block
 
 
 def hidden_kernel(count, held, place, *refs):
-    gs, (low, weight), rs = refs[:count], refs[count : count + 2], refs[count + 2 : 2 * count + 2]
-    outs, hl = refs[2 * count + 2 : 3 * count + 2], refs[3 * count + 2]
-    rows, both = gs[0].shape
-    cols = both // 2
-    rank_cols = rs[0].shape[1]
-    rank = rank_cols // held
-    base = sum(g[...].astype(F32) for g in gs)
-    gate, up = base[:, :cols], base[:, cols:]
-    owner = lax.broadcasted_iota(jnp.int32, (rows, rank_cols), 1) // rank
-    acc = jnp.zeros((rows, cols), F32)
-    for k in range(count):
-        start = pl.multiple_of((place[0] ^ k) * rows, rows)
-        here = low[pl.ds(start, rows), :]
-        low_gate, low_up = here[:, :rank_cols], here[:, rank_cols:]
-        zero = jnp.zeros_like(low_gate)
-        lhs_gate = jnp.concatenate([jnp.where(owner == i, low_gate, zero) for i in range(held)], axis=0)
-        lhs_up = jnp.concatenate([jnp.where(owner == i, low_up, zero) for i in range(held)], axis=0)
-        g = jnp.dot(lhs_gate, rs[k][0], preferred_element_type=F32)
-        u = jnp.dot(lhs_up, rs[k][1], preferred_element_type=F32)
-        parts = []
-        for i in range(held):
-            gi = gate + g[i * rows : (i + 1) * rows]
-            ui = up + u[i * rows : (i + 1) * rows]
-            h = (gi / (1.0 + jnp.exp(-gi))) * ui
-            slot = k * held + i
-            hw = h * weight[:, slot : slot + 1]
-            acc += hw
-            parts.append(hw.astype(BF16))
-        back = dot_rows(jnp.concatenate(parts, axis=0), rs[k][2])
-        block = jnp.zeros((rows, rank_cols), F32)
-        for i in range(held):
-            block += jnp.where(owner == i, back[i * rows : (i + 1) * rows], 0.0)
-        hl[place[0] ^ place[1] ^ k] = block.astype(BF16)
-    outs[0][:, :cols] = acc.astype(BF16)
-    outs[0][:, cols:] = hl[0]
-    for m in range(1, count):
-        outs[m][...] = hl[m]
+    gs, weight, rs = refs[:count], refs[count], refs[count + 1 : 2 * count]
+    base, acc, hl, low = refs[2 * count :]
+    cols = base.shape[1] // 2
+    base[...] = sum(g[:, : 2 * cols].astype(F32) for g in gs)
+    for k, g in enumerate(gs):
+        low[k] = g[:, 2 * cols :].astype(BF16)
+    total = jnp.zeros(acc.shape, F32)
+    for spot, r in enumerate(rs):
+        k = spot ^ place[2] if spot == count // 2 else spot
+        more, hl[place[0] ^ place[1] ^ k] = expert_terms(
+            k, spot, held, place, base[:, :cols], base[:, cols:], low, weight, r
+        )
+        total += more
+    acc[...] = total
+
+
+def hidden_last_kernel(count, held, place, base, acc, come, low, weight, r, hsum, *refs):
+    outs, hl = refs[:-1], refs[-1]
+    side = len(outs)
+    cols = base.shape[1] // 2
+    rank_cols = r.shape[1]
+    hl[...] = come[...]
+    k = (count - 1) ^ place[2]
+    more, hl[place[0] ^ place[1] ^ k] = expert_terms(
+        k, count - 1, held, place, base[:, :cols], base[:, cols:], low, weight, r
+    )
+    hsum[...] = (acc[...] + more).astype(BF16)
+    for e in range(side):
+        for b in range(side):
+            outs[e][:, b * rank_cols : (b + 1) * rank_cols] = hl[side * b + e].astype(outs[e].dtype)
 
 
 def down_kernel(count, place, hs, w, rd, *refs):
@@ -187,9 +213,12 @@
 
 
 VMEM = pl.BlockSpec(memory_space=pltpu.VMEM)
-ANY = pl.BlockSpec(memory_space=pl.ANY)
 SMEM = pl.BlockSpec(memory_space=pltpu.SMEM)
 PARAMS = pltpu.CompilerParams(vmem_limit_bytes=24 * 2**20)
+
+
+def after(a, *others):
+    return lax.optimization_barrier((a, others))[0]
 
 
 def stationary_shards(
@@ -208,17 +237,15 @@
     down_right,
 ):
     count = lax.axis_size("wide")
+    side = math.isqrt(count)
     rows = tokens.shape[0]
     held, rank = gate_left.shape[0], gate_left.shape[2]
     experts = held * count
     rank_cols = held * rank
     inner = base_gate.shape[1]
     features = base_down.shape[1]
-    place = lax.axis_index("wide")
-    spot = lax.axis_index("narrow")
-    places = jnp.stack([place, spot]).astype(jnp.int32)
-    side = math.isqrt(count)
-    steps = range(1, count)
+    place, spot, group = (lax.axis_index(a) for a in ("wide", "narrow", "groups"))
+    places = jnp.stack([place, spot, group]).astype(jnp.int32)
 
     def swap(a, k=0):
         pairs = [(i * count + j, (j ^ k) * count + i) for i in range(count) for j in range(count)]
@@ -229,18 +256,6 @@
 
     def ahead(a, k):
         return lax.ppermute(a, "wide", [(i, (i + k) % count) for i in range(count)])
-
-    def after(a, other):
-        return lax.optimization_barrier((a, other))[0]
-
-    def doubled(a, axis, order, other):
-        blocks = {0: a}
-        for bit in order:
-            for k, b in list(blocks.items()):
-                blocks[k ^ bit] = across(after(b, other) if k else b, axis, bit)
-        return [blocks[k] for k in range(count)]
-
-    bits = [1 << b for b in range(count.bit_length() - 1)]
 
     spread = []
     for m in range(count):
@@ -251,77 +266,101 @@
         ]
         spread.append(lax.ppermute(tokens, ("wide", "narrow"), pairs))
 
-    mine = [spread[side * a] for a in range(side)]
+    pairs = [
+        (z * count + n, z * count + (n ^ side))
+        for z in range(count)
+        for n in range(count)
+        if z // side == n // side
+    ]
+    come = [lax.ppermute(spread[side * a], ("wide", "narrow"), pairs) for a in range(side)]
     holds = spot // side == place // side
-    for a in range(side):
-        come = 0
-        for b in range(1, side):
-            pairs = [
-                (z * count + n, z * count + (n ^ (side * b)))
-                for z in range(count)
-                for n in range(count)
-                if z // side == n // side
-            ]
-            come += lax.ppermute(spread[side * a], ("wide", "narrow"), pairs)
-        mine[a] = jnp.where(holds, mine[a], come)
-    mine = jnp.concatenate(mine, axis=0)
-    own_features = [mine] + [across(mine, "narrow", e) for e in range(1, side)]
+    mine = jnp.concatenate([jnp.where(holds, spread[side * a], come[a]) for a in range(side)], axis=0)
 
     left = jnp.concatenate(
         [jnp.swapaxes(a, 1, 2).reshape(rank_cols, a.shape[1]) for a in (gate_left, up_left)], axis=0
     )
-    left = [left] + [across(left, "narrow", e) for e in range(1, side)]
-
-    low = pl.pallas_call(
+    low, sent = pl.pallas_call(
         functools.partial(left_kernel, count, side),
-        out_shape=[jax.ShapeDtypeStruct((rows, 2 * rank_cols), BF16)] * side,
+        out_shape=[jax.ShapeDtypeStruct((side * rows, 2 * rank_cols), kind) for kind in (F32, BF16)],
         in_specs=[SMEM] + [VMEM] * (count + side),
-        out_specs=[VMEM] * side,
+        out_specs=[VMEM] * 2,
         scratch_shapes=[pltpu.VMEM((count, *tokens.shape), BF16)],
         compiler_params=PARAMS,
-    )(places, *spread, *left)
-    low = sum(swap(low[q], side * q).astype(F32) for q in range(side)).astype(BF16)
-
+    )(places, *spread, left, across(left, "narrow", 1))
+    low = (low + across(sent, "narrow", side).astype(F32)).astype(BF16)
+
+    wide_cols = 2 * inner + 2 * rank_cols
     sums = pl.pallas_call(
         functools.partial(base_kernel, count, side),
-        out_shape=[jax.ShapeDtypeStruct((rows, 2 * inner), F32 if k == 0 else BF16) for k in range(count)],
-        in_specs=[SMEM] + [VMEM] * (side + 2),
+        out_shape=[jax.ShapeDtypeStruct((rows, wide_cols), F32 if k == 0 else BF16) for k in range(count)],
+        in_specs=[SMEM] + [VMEM] * (2 * side + 2),
         out_specs=[VMEM] * count,
-        scratch_shapes=[pltpu.VMEM((count * rows, 2 * inner), F32)],
-        compiler_params=PARAMS,
-    )(places, *own_features, base_gate, base_up)
-
-    packed = jnp.stack(
+        scratch_shapes=[
+            pltpu.VMEM((count * rows, 2 * inner), F32),
+            pltpu.VMEM((count * rows, 2 * rank_cols), BF16),
+        ],
+        compiler_params=PARAMS,
+    )(
+        places,
+        mine,
+        across(after(mine, sent), "narrow", 1),
+        low,
+        across(low, "narrow", 1),
+        base_gate,
+        base_up,
+    )
+
+    own = jnp.stack(
         [
             gate_right.reshape(rank_cols, inner),
             up_right.reshape(rank_cols, inner),
             jnp.swapaxes(down_left, 1, 2).reshape(rank_cols, inner),
         ]
     )
-    factors = doubled(packed, "wide", bits[::-1], sums[0])
-    low = lax.all_gather(after(low, sums[0]), "narrow", axis=0, tiled=True)
-    sums = [sums[0]] + [across(sums[k], "wide", k) for k in steps]
+    pairs = [(g * count + z, g * count + (z ^ 2 ^ g)) for g in range(2) for z in range(count)]
+    far = lax.ppermute(after(own, spread[1], spread[3], come[1]), ("groups", "wide"), pairs)
+    traded = lax.ppermute(after(far, sums[0]), "groups", [(0, 1), (1, 0)])
+    sums = [sums[0]] + [across(sums[k], "wide", k) for k in range(1, count)]
+    near = across(own, "wide", 1)
 
     expert_ids = lax.broadcasted_iota(jnp.int32, (1, 1, experts), 2)
     named = routes[:, :, None] == expert_ids
     delta_ids = jnp.sum(jnp.where(named, delta_of[None, None, :], 0), axis=2)
-    slots = ((delta_ids // held) ^ place) * held + delta_ids % held
+    away = (delta_ids // held) ^ place
+    away = jnp.where(away < 2, away, away ^ group)
+    slots = away * held + delta_ids % held
     weight = jnp.sum(jnp.where(slots[:, :, None] == expert_ids, gate_weights[:, :, None], 0.0), axis=1)
 
-    hidden = pl.pallas_call(
+    base, acc, hl, low = pl.pallas_call(
         functools.partial(hidden_kernel, count, held),
         out_shape=[
-            jax.ShapeDtypeStruct((rows, rank_cols + (inner if k == 0 else 0)), BF16) for k in range(count)
+            jax.ShapeDtypeStruct((rows, 2 * inner), F32),
+            jax.ShapeDtypeStruct((rows, inner), F32),
+            jax.ShapeDtypeStruct((count, rows, rank_cols), F32),
+            jax.ShapeDtypeStruct((count, rows, 2 * rank_cols), BF16),
         ],
-        in_specs=[SMEM] + [VMEM] * (2 * count + 2),
-        out_specs=[VMEM] * count,
-        scratch_shapes=[pltpu.VMEM((count, rows, rank_cols), BF16)],
-        compiler_params=PARAMS,
-    )(places, *sums, low, weight, *factors)
-
-    hidden = [swap(hidden[k], k) for k in range(count)]
-    low_sum = sum(h[:, -rank_cols:].astype(F32) for h in hidden).astype(BF16)
-    hs = jnp.concatenate([hidden[0][:, :inner], low_sum], axis=1)
+        in_specs=[SMEM] + [VMEM] * (2 * count),
+        out_specs=[VMEM] * 4,
+        compiler_params=PARAMS,
+    )(places, *sums, weight, own, near, far)
+    hsum, kept, given = pl.pallas_call(
+        functools.partial(hidden_last_kernel, count, held),
+        out_shape=[
+            jax.ShapeDtypeStruct((rows, inner), BF16),
+            jax.ShapeDtypeStruct((rows, side * rank_cols), F32),
+            jax.ShapeDtypeStruct((rows, side * rank_cols), BF16),
+        ],
+        in_specs=[SMEM] + [VMEM] * 6,
+        out_specs=[VMEM] * 3,
+        scratch_shapes=[pltpu.VMEM((count, rows, rank_cols), F32)],
+        compiler_params=PARAMS,
+    )(places, base, acc, hl, low, weight, traded)
+
+    part = (kept + across(given, "narrow", 1).astype(F32)).astype(BF16)
+    part = jnp.split(part, side, axis=1)
+    first = swap(jnp.concatenate([hsum, part[0]], axis=1))
+    low_sum = first[:, inner:].astype(F32) + sum(swap(part[b], side * b).astype(F32) for b in range(1, side))
+    hs = jnp.concatenate([first[:, :inner], low_sum.astype(BF16)], axis=1)
     hs = lax.all_gather(hs, "narrow", axis=0, tiled=True)
     outs = pl.pallas_call(
         functools.partial(down_kernel, count),
@@ -331,14 +370,14 @@
         scratch_shapes=[pltpu.VMEM((count * rows, features), F32)],
         compiler_params=PARAMS,
     )(places, hs, base_down, down_right.reshape(rank_cols, features))
-    return sum([outs[0]] + [ahead(outs[k], k).astype(F32) for k in steps]).astype(BF16)
+    return sum([outs[0]] + [ahead(outs[k], k).astype(F32) for k in range(1, count)]).astype(BF16)
 
 
 def solution(mesh):
-    count = mesh.shape["wide"]
-    square = count == mesh.shape["narrow"] == math.isqrt(count) ** 2 and count & (count - 1) == 0
+    shape = mesh.shape
+    stationary = shape["groups"] == 2 and shape["wide"] == shape["narrow"] == shape["groups"] ** 2
     return jax.shard_map(
-        stationary_shards if square else gathered_shards,
+        stationary_shards if stationary else gathered_shards,
         mesh=mesh,
         in_specs=(
             P(("groups", "wide"), "narrow"),

time: 86.1 us -> 79.1 us (0.919)
  blocking collectives: 13.8 us -> 7.16 us
  starting transfers between devices: 37.9 us -> 36.7 us
    ppermute x8 -> x9, waiting for transfers between devices: 4.34 us -> 11.8 us  [across(): return lax.ppermute(a, axis, [(i, i ^ k) for i in range(count)])]
    all_gather x1 -> x0, blocking collectives: 6.19 us -> none  [stationary_shards(): low = lax.all_gather(after(low, sums[0]), 'narrow', axis=0, tiled=True)]
    ppermute x6 -> x2, starting transfers between devices: 10.5 us -> 5.98 us  [swap(): return lax.ppermute(a, ('wide', 'narrow'), pairs)]
    ppermute x2 -> x4, waiting for transfers between devices: 4.66 us -> 0.9 us  [the longest x2 0.8 us: stationary_shards(): lax.ppermute(spread[side * a], ('wide', 'narrow'), pairs)]
    ppermute x3, waiting for transfers between devices: 11.8 us -> 8.8 us  [ahead(): return lax.ppermute(a, 'wide', [(i, (i + k) % count) for i in range(count)])]
    ppermute x2 -> x4, starting transfers between devices: 7.74 us -> 10 us  [the longest x2 6.38 us: stationary_shards(): lax.ppermute(spread[side * a], ('wide', 'narrow'), pairs)]
    ppermute x3, starting transfers between devices: 2.55 us -> 4.56 us  [ahead(): return lax.ppermute(a, 'wide', [(i, (i + k) % count) for i in range(count)])]
    ppermute x6 -> x2, waiting for transfers between devices: 3.71 us -> 2.48 us  [swap(): return lax.ppermute(a, ('wide', 'narrow'), pairs)]
  transfers between devices with their start and end apart: 23 -> 22, of which waited for: 8 -> 11; matrix products, arithmetic and copies ran while one was open for 2% -> 2% of each run, Pallas kernels for 3% -> 5%
where the time goes in v5:
time: 79.1 us; the launch traced here: 78.7 us
  starting transfers between devices  36.7 us (46%)
  waiting for transfers between devices  25.4 us (32%)
  blocking collectives  7.16 us (9%)
  Pallas kernels  6.22 us (8%)
  other arithmetic  2.18 us (3%)
    ppermute x9, waiting for transfers between devices, across(): return lax.ppermute(a, axis, [(i, i ^ k) for i in range(count)])  11.8 us
    ppermute x3, waiting for transfers between devices, ahead(): return lax.ppermute(a, 'wide', [(i, (i + k) % count) for i in range(count)])  8.8 us
    ppermute x4, starting transfers between devices, stationary_shards(): spread.append(lax.ppermute(tokens, ('wide', 'narrow'), pairs))  8.76 us
    ppermute x9, starting transfers between devices, across(): return lax.ppermute(a, axis, [(i, i ^ k) for i in range(count)])  7.42 us
    all_gather x1, blocking collectives, stationary_shards(): hs = lax.all_gather(hs, 'narrow', axis=0, tiled=True)  7.16 us
    ppermute x2, starting transfers between devices, stationary_shards(): lax.ppermute(spread[side * a], ('wide', 'narrow'), pairs)  6.38 us
    ppermute x2, starting transfers between devices, swap(): return lax.ppermute(a, ('wide', 'narrow'), pairs)  5.98 us
    ppermute x3, starting transfers between devices, ahead(): return lax.ppermute(a, 'wide', [(i, (i + k) % count) for i in range(count)])  4.56 us
  transfers between devices with their start and end apart: 22, of which 11 were waited for; matrix products, arithmetic and copies ran while one was open for 2% of the time, Pallas kernels for 5%

profile of v5, /device:TPU:0, one launch (start us, length us, event | category | flops | bytes accessed | tf_op | source)
XLA Modules:
  0.0 78.7 jit_solution(10533507652028857739)
XLA Ops:
  0.0 4.0 %collective-permute-start.2 = (bf16[64,1024]{1,0:T(8,128)(2,1)}, bf16[64,1024]{1,0:T(8,128)(2,1)S(1)}, u32[]{:S(2)}, u32[]{:S(2)}) collective-permute-start(bf16[64,1024]{1,0:T(8,128)(2,1)} %param.13), channel_id=1, source_target_pairs={{0,8},{1,12},{2,10},{3,14},{4,9},{5,13},{6,11},{7,15},{8,0},{9,4},... | collective-permute-start | bytes 393224 | tf_op jit(solution)/shard_map/ppermute | solution.py:267
  4.0 1.6 %collective-permute-start = (bf16[64,1024]{1,0:T(8,128)(2,1)}, bf16[64,1024]{1,0:T(8,128)(2,1)S(1)}, u32[]{:S(2)}, u32[]{:S(2)}) collective-permute-start(bf16[64,1024]{1,0:T(8,128)(2,1)} %param.13), channel_id=1, source_target_pairs={{0,0},{1,4},{2,2},{3,6},{4,1},{5,5},{6,3},{7,7},{8,8},{9,12},{10,1... | collective-permute-start | bytes 393224 | tf_op jit(solution)/shard_map/ppermute | solution.py:267
  5.6 3.2 %collective-permute-start.4 = (bf16[64,1024]{1,0:T(8,128)(2,1)}, bf16[64,1024]{1,0:T(8,128)(2,1)S(1)}, u32[]{:S(2)}, u32[]{:S(2)}) collective-permute-start(bf16[64,1024]{1,0:T(8,128)(2,1)} %param.13), channel_id=1, source_target_pairs={{0,4},{1,0},{2,6},{3,2},{4,5},{5,1},{6,7},{7,3},{8,12},{9,8},{10,1... | collective-permute-start | bytes 393224 | tf_op jit(solution)/shard_map/ppermute | solution.py:267
  8.8 0.0 collective-permute-start.5
  8.8 1.1 %pad_maximum_fusion.refs_4_ = bf16[256,1024]{1,0:T(8,128)(2,1)S(1)} fusion(bf16[128,1024]{1,0:T(8,128)(2,1)} %bitcast.16, bf16[128,1024]{1,0:T(8,128)(2,1)} %bitcast.17), kind=kLoop, calls=%fused_computation | loop fusion | flops 1048576 | bytes 1048576 | tf_op jit(solution)/shard_map/concatenate | solution.py:279
  9.9 0.1 collective-permute-start.6
  10.0 1.4 %collective-permute-done.2.refs_2_ = bf16[64,1024]{1,0:T(8,128)(2,1)S(1)} collective-permute-done((bf16[64,1024]{1,0:T(8,128)(2,1)}, bf16[64,1024]{1,0:T(8,128)(2,1)S(1)}, u32[]{:S(2)}, u32[]{:S(2)}) %collective-permute-start.2) | collective-permute-done | bytes 131104 | tf_op jit(solution)/shard_map/ppermute | solution.py:267
  11.4 3.4 %collective-permute-start.3 = (bf16[64,1024]{1,0:T(8,128)(2,1)S(1)}, bf16[64,1024]{1,0:T(8,128)(2,1)S(1)}, u32[]{:S(2)}, u32[]{:S(2)}) collective-permute-start(bf16[64,1024]{1,0:T(8,128)(2,1)S(1)} %collective-permute-done.2.refs_2_), channel_id=1, source_target_pairs={{0,2},{1,3},{4,6},{5,7},{10,8},{11,9},{14,12},{15,13},{16,18},{17,... | collective-permute-start | bytes 393224 | tf_op jit(solution)/shard_map/ppermute | solution.py:275
  14.8 0.0 copy-done.4
  14.8 0.0 copy-done.5
  14.9 0.1 pad_add_fusion.place
  14.9 0.0 collective-permute-done.refs_0_
  15.0 0.1 collective-permute-start.13
  15.1 0.0 collective-permute-done.4.refs_1_
  15.1 3.0 %collective-permute-start.1 = (bf16[64,1024]{1,0:T(8,128)(2,1)S(1)}, bf16[64,1024]{1,0:T(8,128)(2,1)S(1)}, u32[]{:S(2)}, u32[]{:S(2)}) collective-permute-start(bf16[64,1024]{1,0:T(8,128)(2,1)S(1)} %collective-permute-done.refs_0_), channel_id=1, source_target_pairs={{0,2},{1,3},{4,6},{5,7},{10,8},{11,9},{14,12},{15,13},{16,18},{17,... | collective-permute-start | bytes 393224 | tf_op jit(solution)/shard_map/ppermute | solution.py:275
  18.1 0.0 collective-permute-done.5.refs_3_
  18.1 0.0 collective-permute-done.3
  18.1 2.2 %collective-permute-start.14 = (bf16[3,128,384]{2,1,0:T(8,128)(2,1)S(1)}, bf16[3,128,384]{2,1,0:T(8,128)(2,1)S(1)}, u32[]{:S(2)}, u32[]{:S(2)}) collective-permute-start(bf16[3,128,384]{2,1,0:T(8,128)(2,1)S(1)} %pad_maximum_fusion.1.refs_5_), channel_id=1, source_target_pairs={{0,8},{4,12},{8,0},{12,4},{16,28},{20,24},{24,20},{28,16},{1,9},{5... | collective-permute-start | bytes 884744 | tf_op jit(solution)/shard_map/ppermute | solution.py:321
  20.3 0.8 %collective-permute-done.1 = bf16[64,1024]{1,0:T(8,128)(2,1)S(1)} collective-permute-done((bf16[64,1024]{1,0:T(8,128)(2,1)S(1)}, bf16[64,1024]{1,0:T(8,128)(2,1)S(1)}, u32[]{:S(2)}, u32[]{:S(2)}) %collective-permute-start.1) | collective-permute-done | bytes 131104 | tf_op jit(solution)/shard_map/ppermute | solution.py:275
  21.2 0.0 collective-permute-done.6.refs_5_
  21.2 0.0 copy-start.7
  21.2 0.0 copy-start.1
  21.2 1.0 %shard_map.127 = (f32[128,256]{1,0:T(8,128)S(1)}, bf16[128,256]{1,0:T(8,128)(2,1)S(1)}) custom-call(s32[3]{0:T(128)S(1)} %pad_add_fusion.place, bf16[64,1024]{1,0:T(8,128)(2,1)S(1)} %collective-permute-done.refs_0_, bf16[64,1024]{1,0:T(8,128)(2,1)S(1)} %collective-permute-done.4.refs_1_, bf16[64,1024]{1,0:T(8,128)(2,1)S(1)} %collective-permute-done.2.refs_2_, ...), custom_call_target="tpu_custom_call" | custom-call | tf_op jit(solution)/shard_map/pallas_call | solution.py:282
  22.2 0.0 copy-start
  22.2 2.5 %collective-permute-start.8 = (bf16[128,256]{1,0:T(8,128)(2,1)S(1)}, bf16[128,256]{1,0:T(8,128)(2,1)S(1)}, u32[]{:S(2)}, u32[]{:S(2)}) collective-permute-start(bf16[128,256]{1,0:T(8,128)(2,1)S(1)} %get-tuple-element.25), channel_id=1, source_target_pairs={{0,2},{1,3},{2,0},{3,1},{4,6},{5,7},{6,4},{7,5},{8,10},{9,11},{10,... | collective-permute-start | bytes 196616 | tf_op jit(solution)/shard_map/ppermute | solution.py:255
  24.8 0.1 collective-permute-start.7
  24.9 2.1 %collective-permute-done.8 = bf16[128,256]{1,0:T(8,128)(2,1)S(1)} collective-permute-done((bf16[128,256]{1,0:T(8,128)(2,1)S(1)}, bf16[128,256]{1,0:T(8,128)(2,1)S(1)}, u32[]{:S(2)}, u32[]{:S(2)}) %collective-permute-start.8) | collective-permute-done | bytes 65568 | tf_op jit(solution)/shard_map/ppermute | solution.py:255
  27.0 0.1 collective-permute-start.9
  27.1 0.5 copy-done.9
  27.7 0.1 select_reduce_fusion.1
  27.8 0.6 collective-permute-done.9.refs_3_
  28.4 0.0 collective-permute-done.7.refs_1_
  28.4 1.4 %shard_map.128 = (f32[64,1024]{1,0:T(8,128)S(1)}, bf16[64,1024]{1,0:T(8,128)(2,1)S(1)}, bf16[64,1024]{1,0:T(8,128)(2,1)S(1)}, bf16[64,1024]{1,0:T(8,128)(2,1)S(1)}) custom-call(s32[3]{0:T(128)S(1)} %pad_add_fusion.place, bf16[128,1024]{1,0:T(8,128)(2,1)S(1)} %pad_maximum_fusion.2.refs_0_, bf16[128,1024]{1,0:T(8,128)(2,1)S(1)} %collective-permute-done.7.refs_1_, ...), custom_call_target="tpu_custom_call" | custom-call | tf_op jit(solution)/shard_map/pallas_call | solution.py:293
  29.8 1.1 %collective-permute-start.10 = (bf16[64,1024]{1,0:T(8,128)(2,1)S(1)}, bf16[64,1024]{1,0:T(8,128)(2,1)S(1)}, u32[]{:S(2)}, u32[]{:S(2)}) collective-permute-start(bf16[64,1024]{1,0:T(8,128)(2,1)S(1)} %get-tuple-element.29), channel_id=1, source_target_pairs={{0,4},{4,0},{8,12},{12,8},{1,5},{5,1},{9,13},{13,9},{2,6},{6,2},{1... | collective-permute-start | bytes 393224 | tf_op jit(solution)/shard_map/ppermute | solution.py:255
  30.9 1.6 %collective-permute-start.11 = (bf16[64,1024]{1,0:T(8,128)(2,1)S(1)}, bf16[64,1024]{1,0:T(8,128)(2,1)S(1)}, u32[]{:S(2)}, u32[]{:S(2)}) collective-permute-start(bf16[64,1024]{1,0:T(8,128)(2,1)S(1)} %get-tuple-element.30), channel_id=1, source_target_pairs={{0,8},{4,12},{8,0},{12,4},{1,9},{5,13},{9,1},{13,5},{2,10},{6,14},... | collective-permute-start | bytes 393224 | tf_op jit(solution)/shard_map/ppermute | solution.py:255
  32.4 1.8 %collective-permute-start.12 = (bf16[64,1024]{1,0:T(8,128)(2,1)S(1)}, bf16[64,1024]{1,0:T(8,128)(2,1)S(1)}, u32[]{:S(2)}, u32[]{:S(2)}) collective-permute-start(bf16[64,1024]{1,0:T(8,128)(2,1)S(1)} %get-tuple-element.31), channel_id=1, source_target_pairs={{0,12},{4,8},{8,4},{12,0},{1,13},{5,9},{9,5},{13,1},{2,14},{6,10},... | collective-permute-start | bytes 393224 | tf_op jit(solution)/shard_map/ppermute | solution.py:255
  34.2 0.1 collective-permute-done.14.refs_7_
  34.3 1.4 %collective-permute-start.15 = (bf16[3,128,384]{2,1,0:T(8,128)(2,1)S(1)}, bf16[3,128,384]{2,1,0:T(8,128)(2,1)S(1)}, u32[]{:S(2)}, u32[]{:S(2)}) collective-permute-start(bf16[3,128,384]{2,1,0:T(8,128)(2,1)S(1)} %collective-permute-done.14.refs_7_), channel_id=1, source_target_pairs={{0,16},{16,0},{1,17},{17,1},{2,18},{18,2},{3,19},{19,3},{4,20},{20... | collective-permute-start | bytes 884744 | tf_op jit(solution)/shard_map/ppermute | solution.py:322
  35.8 0.0 copy-done.8
  35.8 0.1 copy.16.refs_4_.weight
  35.9 0.0 collective-permute-done.13.refs_6_
  35.9 3.6 %collective-permute-done.10.refs_1_ = bf16[64,1024]{1,0:T(8,128)(2,1)S(1)} collective-permute-done((bf16[64,1024]{1,0:T(8,128)(2,1)S(1)}, bf16[64,1024]{1,0:T(8,128)(2,1)S(1)}, u32[]{:S(2)}, u32[]{:S(2)}) %collective-permute-start.10) | collective-permute-done | bytes 131104 | tf_op jit(solution)/shard_map/ppermute | solution.py:255
  39.5 4.3 %collective-permute-done.11.refs_2_ = bf16[64,1024]{1,0:T(8,128)(2,1)S(1)} collective-permute-done((bf16[64,1024]{1,0:T(8,128)(2,1)S(1)}, bf16[64,1024]{1,0:T(8,128)(2,1)S(1)}, u32[]{:S(2)}, u32[]{:S(2)}) %collective-permute-start.11) | collective-permute-done | bytes 131104 | tf_op jit(solution)/shard_map/ppermute | solution.py:255
  43.8 0.0 collective-permute-done.12.refs_3_
  43.8 1.6 %shard_map.129 = (f32[64,768]{1,0:T(8,128)S(1)}, f32[64,384]{1,0:T(8,128)S(1)}, f32[4,64,128]{2,1,0:T(8,128)S(1)}, bf16[4,64,256]{2,1,0:T(8,128)(2,1)S(1)}) custom-call(s32[3]{0:T(128)S(1)} %pad_add_fusion.place, f32[64,1024]{1,0:T(8,128)S(1)} %get-tuple-element.28.refs_0_, bf16[64,1024]{1,0:T(8,128)(2,1)S(1)} %collective-permute-done.10.refs_1_, ...), custom_call_target="tpu_custom_call" | custom-call | tf_op jit(solution)/shard_map/pallas_call | solution.py:334
  45.4 0.0 collective-permute-done.15.r
  45.4 0.0 copy-start.2
  45.4 1.0 %shard_map.130 = (bf16[64,384]{1,0:T(8,128)(2,1)S(1)}, f32[64,256]{1,0:T(8,128)S(1)}, bf16[64,256]{1,0:T(8,128)(2,1)S(1)}) custom-call(s32[3]{0:T(128)S(1)} %pad_add_fusion.place, f32[64,768]{1,0:T(8,128)S(1)} %get-tuple-element.33.base, f32[64,384]{1,0:T(8,128)S(1)} %get-tuple-element.34.acc, f32[4,64,128]{2,1,0:T(8,128)S(1)} %get-tuple-element.35.come, ...), custom_call_target="tpu_custom_call" | custom-call | tf_op jit(solution)/shard_map/pallas_call | solution.py:346
  46.4 0.1 collective-permute-start.16
  46.5 1.2 %collective-permute-done.16 = bf16[64,256]{1,0:T(8,128)(2,1)S(1)} collective-permute-done((bf16[64,256]{1,0:T(8,128)(2,1)S(1)}, bf16[64,256]{1,0:T(8,128)(2,1)S(1)}, u32[]{:S(2)}, u32[]{:S(2)}) %collective-permute-start.16) | collective-permute-done | bytes 32800 | tf_op jit(solution)/shard_map/ppermute | solution.py:255
  47.7 0.7 collective-permute-start.17
  48.4 5.3 %collective-permute-start.18 = (bf16[64,128]{1,0:T(8,128)(2,1)S(1)}, bf16[64,128]{1,0:T(8,128)(2,1)S(1)}, u32[]{:S(2)}, u32[]{:S(2)}) collective-permute-start(bf16[64,128]{1,0:T(8,128)(2,1)S(1)} %get-tuple-element.46), channel_id=1, source_target_pairs={{0,8},{1,12},{2,0},{3,4},{4,9},{5,13},{6,1},{7,5},{8,10},{9,14},{1... | collective-permute-start | bytes 49160 | tf_op jit(solution)/shard_map/ppermute | solution.py:252
  53.7 0.0 collective-permute-done.17
  53.7 0.0 copy-start.3
  53.7 2.5 %collective-permute-done.18 = bf16[64,128]{1,0:T(8,128)(2,1)S(1)} collective-permute-done((bf16[64,128]{1,0:T(8,128)(2,1)S(1)}, bf16[64,128]{1,0:T(8,128)(2,1)S(1)}, u32[]{:S(2)}, u32[]{:S(2)}) %collective-permute-start.18) | collective-permute-done | bytes 16416 | tf_op jit(solution)/shard_map/ppermute | solution.py:252
  56.2 7.2 %all_gather.3.hs = bf16[256,512]{1,0:T(8,128)(2,1)S(1)} all-gather(bf16[64,512]{1,0:T(8,128)(2,1)S(1)} %pad_maximum_fusion.4), channel_id=1, replica_groups=mesh['groups'=2,'wide'=4,'narrow'=4] {'narrow'}, dimensions={0}, use_global_device_ids=true | all-gather | bytes 327680 | tf_op jit(solution)/shard_map/all_gather | solution.py:364
  63.4 1.2 %shard_map.131 = (f32[64,1024]{1,0:T(8,128)S(1)}, bf16[64,1024]{1,0:T(8,128)(2,1)S(1)}, bf16[64,1024]{1,0:T(8,128)(2,1)S(1)}, bf16[64,1024]{1,0:T(8,128)(2,1)S(1)}) custom-call(s32[3]{0:T(128)S(1)} %pad_add_fusion.place, bf16[256,512]{1,0:T(8,128)(2,1)S(1)} %all_gather.3.hs, bf16[384,1024]{1,0:T(8,128)(2,1)S(1)} %copy-done.2, bf16[128,1024]{1,0:T(8,128)(2,1)S(1)} %bitcast.15), custom_call_target="tpu_custom_call" | custom-call | tf_op jit(solution)/shard_map/pallas_call | solution.py:365
  64.6 1.1 %collective-permute-start.19 = (bf16[64,1024]{1,0:T(8,128)(2,1)S(1)}, bf16[64,1024]{1,0:T(8,128)(2,1)S(1)}, u32[]{:S(2)}, u32[]{:S(2)}) collective-permute-start(bf16[64,1024]{1,0:T(8,128)(2,1)S(1)} %get-tuple-element.42), channel_id=1, source_target_pairs={{0,4},{4,8},{8,12},{12,0},{1,5},{5,9},{9,13},{13,1},{2,6},{6,10},{... | collective-permute-start | bytes 393224 | tf_op jit(solution)/shard_map/ppermute | solution.py:258
  65.7 1.5 %collective-permute-start.20 = (bf16[64,1024]{1,0:T(8,128)(2,1)S(1)}, bf16[64,1024]{1,0:T(8,128)(2,1)S(1)}, u32[]{:S(2)}, u32[]{:S(2)}) collective-permute-start(bf16[64,1024]{1,0:T(8,128)(2,1)S(1)} %get-tuple-element.43), channel_id=1, source_target_pairs={{0,8},{4,12},{8,0},{12,4},{1,9},{5,13},{9,1},{13,5},{2,10},{6,14},... | collective-permute-start | bytes 393224 | tf_op jit(solution)/shard_map/ppermute | solution.py:258
  67.2 2.0 %collective-permute-start.21 = (bf16[64,1024]{1,0:T(8,128)(2,1)S(1)}, bf16[64,1024]{1,0:T(8,128)(2,1)S(1)}, u32[]{:S(2)}, u32[]{:S(2)}) collective-permute-start(bf16[64,1024]{1,0:T(8,128)(2,1)S(1)} %get-tuple-element.44), channel_id=1, source_target_pairs={{0,12},{4,0},{8,4},{12,8},{1,13},{5,1},{9,5},{13,9},{2,14},{6,2},{... | collective-permute-start | bytes 393224 | tf_op jit(solution)/shard_map/ppermute | solution.py:258
  69.2 3.8 %collective-permute-done.19 = bf16[64,1024]{1,0:T(8,128)(2,1)S(1)} collective-permute-done((bf16[64,1024]{1,0:T(8,128)(2,1)S(1)}, bf16[64,1024]{1,0:T(8,128)(2,1)S(1)}, u32[]{:S(2)}, u32[]{:S(2)}) %collective-permute-start.19) | collective-permute-done | bytes 131104 | tf_op jit(solution)/shard_map/ppermute | solution.py:258
  72.9 5.0 %collective-permute-done.20 = bf16[64,1024]{1,0:T(8,128)(2,1)S(1)} collective-permute-done((bf16[64,1024]{1,0:T(8,128)(2,1)S(1)}, bf16[64,1024]{1,0:T(8,128)(2,1)S(1)}, u32[]{:S(2)}, u32[]{:S(2)}) %collective-permute-start.20) | collective-permute-done | bytes 131104 | tf_op jit(solution)/shard_map/ppermute | solution.py:258
  78.0 0.0 collective-permute-done.21
  78.0 0.7 add_convert_fusion
  (24 shorter events, 0.2 us)
Async XLA Ops:
  0.0 11.4 %collective-permute-start.2 = (bf16[64,1024]{1,0:T(8,128)(2,1)}, bf16[64,1024]{1,0:T(8,128)(2,1)S(1)}, u32[]{:S(2)}, u32[]{:S(2)}) collective-permute-start(bf16[64,1024]{1,0:T(8,128)(2,1)} %param.13), channel_id=1, source_target_pairs={{0,8},{1,12},{2,10},{3,14},{4,9},{5,13},{6,11},{7,15},{8,0},{9,4},... | collective-permute-start | bytes 393224 | tf_op jit(solution)/shard_map/ppermute | solution.py:267
  4.0 10.9 %collective-permute-start = (bf16[64,1024]{1,0:T(8,128)(2,1)}, bf16[64,1024]{1,0:T(8,128)(2,1)S(1)}, u32[]{:S(2)}, u32[]{:S(2)}) collective-permute-start(bf16[64,1024]{1,0:T(8,128)(2,1)} %param.13), channel_id=1, source_target_pairs={{0,0},{1,4},{2,2},{3,6},{4,1},{5,5},{6,3},{7,7},{8,8},{9,12},{10,1... | collective-permute-start | bytes 393224 | tf_op jit(solution)/shard_map/ppermute | solution.py:267
  5.6 9.5 %collective-permute-start.4 = (bf16[64,1024]{1,0:T(8,128)(2,1)}, bf16[64,1024]{1,0:T(8,128)(2,1)S(1)}, u32[]{:S(2)}, u32[]{:S(2)}) collective-permute-start(bf16[64,1024]{1,0:T(8,128)(2,1)} %param.13), channel_id=1, source_target_pairs={{0,4},{1,0},{2,6},{3,2},{4,5},{5,1},{6,7},{7,3},{8,12},{9,8},{10,1... | collective-permute-start | bytes 393224 | tf_op jit(solution)/shard_map/ppermute | solution.py:267
  8.8 9.3 %collective-permute-start.5 = (bf16[64,1024]{1,0:T(8,128)(2,1)}, bf16[64,1024]{1,0:T(8,128)(2,1)S(1)}, u32[]{:S(2)}, u32[]{:S(2)}) collective-permute-start(bf16[64,1024]{1,0:T(8,128)(2,1)} %param.13), channel_id=1, source_target_pairs={{0,12},{1,8},{2,14},{3,10},{4,13},{5,9},{6,15},{7,11},{8,4},{9,0},... | collective-permute-start | bytes 393224 | tf_op jit(solution)/shard_map/ppermute | solution.py:267
  8.8 6.0 %copy-start.4 = (bf16[4,384,32]{1,2,0:T(8,128)(2,1)S(1)}, bf16[4,384,32]{1,2,0:T(8,128)(2,1)}, u32[]{:S(2)}) copy-start(bf16[4,384,32]{1,2,0:T(8,128)(2,1)} %param.24) | copy-start | bytes 294916
  8.8 6.0 %copy-start.5 = (bf16[4,32,384]{2,1,0:T(8,128)(2,1)S(1)}, bf16[4,32,384]{2,1,0:T(8,128)(2,1)}, u32[]{:S(2)}) copy-start(bf16[4,32,384]{2,1,0:T(8,128)(2,1)} %param.23) | copy-start | bytes 294916
  8.8 6.0 %copy-start.6 = (bf16[4,32,384]{2,1,0:T(8,128)(2,1)S(1)}, bf16[4,32,384]{2,1,0:T(8,128)(2,1)}, u32[]{:S(2)}) copy-start(bf16[4,32,384]{2,1,0:T(8,128)(2,1)} %param.21) | copy-start | bytes 294916
  9.9 11.3 %collective-permute-start.6 = (bf16[256,1024]{1,0:T(8,128)(2,1)S(1)}, bf16[256,1024]{1,0:T(8,128)(2,1)S(1)}, u32[]{:S(2)}, u32[]{:S(2)}) collective-permute-start(bf16[256,1024]{1,0:T(8,128)(2,1)S(1)} %pad_maximum_fusion.refs_4_), channel_id=1, source_target_pairs={{0,1},{1,0},{2,3},{3,2},{4,5},{5,4},{6,7},{7,6},{8,9},{9,8},{10,11... | collective-permute-start | bytes 1572872 | tf_op jit(solution)/shard_map/ppermute | solution.py:255
  11.4 6.7 %collective-permute-start.3 = (bf16[64,1024]{1,0:T(8,128)(2,1)S(1)}, bf16[64,1024]{1,0:T(8,128)(2,1)S(1)}, u32[]{:S(2)}, u32[]{:S(2)}) collective-permute-start(bf16[64,1024]{1,0:T(8,128)(2,1)S(1)} %collective-permute-done.2.refs_2_), channel_id=1, source_target_pairs={{0,2},{1,3},{4,6},{5,7},{10,8},{11,9},{14,12},{15,13},{16,18},{17,... | collective-permute-start | bytes 393224 | tf_op jit(solution)/shard_map/ppermute | solution.py:275
  15.0 20.9 %collective-permute-start.13 = (bf16[3,128,384]{2,1,0:T(8,128)(2,1)S(1)}, bf16[3,128,384]{2,1,0:T(8,128)(2,1)S(1)}, u32[]{:S(2)}, u32[]{:S(2)}) collective-permute-start(bf16[3,128,384]{2,1,0:T(8,128)(2,1)S(1)} %pad_maximum_fusion.1.refs_5_), channel_id=1, source_target_pairs={{0,4},{4,0},{8,12},{12,8},{1,5},{5,1},{9,13},{13,9},{2,6},{6,2},{1... | collective-permute-start | bytes 884744 | tf_op jit(solution)/shard_map/ppermute | solution.py:255
  15.1 6.0 %collective-permute-start.1 = (bf16[64,1024]{1,0:T(8,128)(2,1)S(1)}, bf16[64,1024]{1,0:T(8,128)(2,1)S(1)}, u32[]{:S(2)}, u32[]{:S(2)}) collective-permute-start(bf16[64,1024]{1,0:T(8,128)(2,1)S(1)} %collective-permute-done.refs_0_), channel_id=1, source_target_pairs={{0,2},{1,3},{4,6},{5,7},{10,8},{11,9},{14,12},{15,13},{16,18},{17,... | collective-permute-start | bytes 393224 | tf_op jit(solution)/shard_map/ppermute | solution.py:275
  18.1 16.2 %collective-permute-start.14 = (bf16[3,128,384]{2,1,0:T(8,128)(2,1)S(1)}, bf16[3,128,384]{2,1,0:T(8,128)(2,1)S(1)}, u32[]{:S(2)}, u32[]{:S(2)}) collective-permute-start(bf16[3,128,384]{2,1,0:T(8,128)(2,1)S(1)} %pad_maximum_fusion.1.refs_5_), channel_id=1, source_target_pairs={{0,8},{4,12},{8,0},{12,4},{16,28},{20,24},{24,20},{28,16},{1,9},{5... | collective-permute-start | bytes 884744 | tf_op jit(solution)/shard_map/ppermute | solution.py:321
  21.2 6.0 %copy-start.7 = (s32[64,8]{0,1:T(8,128)S(1)}, s32[64,8]{0,1:T(8,128)}, u32[]{:S(2)}) copy-start(s32[64,8]{0,1:T(8,128)} %param.14) | copy-start | bytes 6148
  21.2 7.2 %copy-start.1 = (bf16[1024,384]{1,0:T(8,128)(2,1)S(1)}, bf16[1024,384]{1,0:T(8,128)(2,1)}, u32[]{:S(2)}) copy-start(bf16[1024,384]{1,0:T(8,128)(2,1)} %refs_5_.1) | copy-start | bytes 2359300
  22.2 6.2 %copy-start = (bf16[1024,384]{1,0:T(8,128)(2,1)S(1)}, bf16[1024,384]{1,0:T(8,128)(2,1)}, u32[]{:S(2)}) copy-start(bf16[1024,384]{1,0:T(8,128)(2,1)} %refs_4_.1) | copy-start | bytes 2359300
  22.2 4.8 %collective-permute-start.8 = (bf16[128,256]{1,0:T(8,128)(2,1)S(1)}, bf16[128,256]{1,0:T(8,128)(2,1)S(1)}, u32[]{:S(2)}, u32[]{:S(2)}) collective-permute-start(bf16[128,256]{1,0:T(8,128)(2,1)S(1)} %get-tuple-element.25), channel_id=1, source_target_pairs={{0,2},{1,3},{2,0},{3,1},{4,6},{5,7},{6,4},{7,5},{8,10},{9,11},{10,... | collective-permute-start | bytes 196616 | tf_op jit(solution)/shard_map/ppermute | solution.py:255
  24.8 3.6 %collective-permute-start.7 = (bf16[128,1024]{1,0:T(8,128)(2,1)S(1)}, bf16[128,1024]{1,0:T(8,128)(2,1)S(1)}, u32[]{:S(2)}, u32[]{:S(2)}) collective-permute-start(bf16[128,1024]{1,0:T(8,128)(2,1)S(1)} %pad_maximum_fusion.2.refs_0_), channel_id=1, source_target_pairs={{0,1},{1,0},{2,3},{3,2},{4,5},{5,4},{6,7},{7,6},{8,9},{9,8},{10,11... | collective-permute-start | bytes 786440 | tf_op jit(solution)/shard_map/ppermute | solution.py:255
  27.0 0.7 copy-start.9
  27.0 1.3 %collective-permute-start.9 = (bf16[128,256]{1,0:T(8,128)(2,1)S(1)}, bf16[128,256]{1,0:T(8,128)(2,1)S(1)}, u32[]{:S(2)}, u32[]{:S(2)}) collective-permute-start(bf16[128,256]{1,0:T(8,128)(2,1)S(1)} %add_convert_fusion.1.refs_2_), channel_id=1, source_target_pairs={{0,1},{1,0},{2,3},{3,2},{4,5},{5,4},{6,7},{7,6},{8,9},{9,8},{10,11... | collective-permute-start | bytes 196616 | tf_op jit(solution)/shard_map/ppermute | solution.py:255
  29.8 9.7 %collective-permute-start.10 = (bf16[64,1024]{1,0:T(8,128)(2,1)S(1)}, bf16[64,1024]{1,0:T(8,128)(2,1)S(1)}, u32[]{:S(2)}, u32[]{:S(2)}) collective-permute-start(bf16[64,1024]{1,0:T(8,128)(2,1)S(1)} %get-tuple-element.29), channel_id=1, source_target_pairs={{0,4},{4,0},{8,12},{12,8},{1,5},{5,1},{9,13},{13,9},{2,6},{6,2},{1... | collective-permute-start | bytes 393224 | tf_op jit(solution)/shard_map/ppermute | solution.py:255
  30.9 12.9 %collective-permute-start.11 = (bf16[64,1024]{1,0:T(8,128)(2,1)S(1)}, bf16[64,1024]{1,0:T(8,128)(2,1)S(1)}, u32[]{:S(2)}, u32[]{:S(2)}) collective-permute-start(bf16[64,1024]{1,0:T(8,128)(2,1)S(1)} %get-tuple-element.30), channel_id=1, source_target_pairs={{0,8},{4,12},{8,0},{12,4},{1,9},{5,13},{9,1},{13,5},{2,10},{6,14},... | collective-permute-start | bytes 393224 | tf_op jit(solution)/shard_map/ppermute | solution.py:255
  32.4 11.3 %collective-permute-start.12 = (bf16[64,1024]{1,0:T(8,128)(2,1)S(1)}, bf16[64,1024]{1,0:T(8,128)(2,1)S(1)}, u32[]{:S(2)}, u32[]{:S(2)}) collective-permute-start(bf16[64,1024]{1,0:T(8,128)(2,1)S(1)} %get-tuple-element.31), channel_id=1, source_target_pairs={{0,12},{4,8},{8,4},{12,0},{1,13},{5,9},{9,5},{13,1},{2,14},{6,10},... | collective-permute-start | bytes 393224 | tf_op jit(solution)/shard_map/ppermute | solution.py:255
  34.3 1.4 %copy-start.8 = (f32[64,8]{0,1:T(8,128)S(1)}, f32[64,8]{0,1:T(8,128)}, u32[]{:S(2)}) copy-start(f32[64,8]{0,1:T(8,128)} %param.15) | copy-start | bytes 6148
  34.3 11.1 %collective-permute-start.15 = (bf16[3,128,384]{2,1,0:T(8,128)(2,1)S(1)}, bf16[3,128,384]{2,1,0:T(8,128)(2,1)S(1)}, u32[]{:S(2)}, u32[]{:S(2)}) collective-permute-start(bf16[3,128,384]{2,1,0:T(8,128)(2,1)S(1)} %collective-permute-done.14.refs_7_), channel_id=1, source_target_pairs={{0,16},{16,0},{1,17},{17,1},{2,18},{18,2},{3,19},{19,3},{4,20},{20... | collective-permute-start | bytes 884744 | tf_op jit(solution)/shard_map/ppermute | solution.py:322
  45.4 18.0 %copy-start.2 = (bf16[384,1024]{1,0:T(8,128)(2,1)S(1)}, bf16[384,1024]{1,0:T(8,128)(2,1)}, u32[]{:S(2)}) copy-start(bf16[384,1024]{1,0:T(8,128)(2,1)} %w.1) | copy-start | bytes 2359300
  46.4 1.3 %collective-permute-start.16 = (bf16[64,256]{1,0:T(8,128)(2,1)S(1)}, bf16[64,256]{1,0:T(8,128)(2,1)S(1)}, u32[]{:S(2)}, u32[]{:S(2)}) collective-permute-start(bf16[64,256]{1,0:T(8,128)(2,1)S(1)} %get-tuple-element.40), channel_id=1, source_target_pairs={{0,1},{1,0},{2,3},{3,2},{4,5},{5,4},{6,7},{7,6},{8,9},{9,8},{10,11... | collective-permute-start | bytes 98312 | tf_op jit(solution)/shard_map/ppermute | solution.py:255
  47.7 6.0 %collective-permute-start.17 = (bf16[64,512]{1,0:T(8,128)(2,1)S(1)}, bf16[64,512]{1,0:T(8,128)(2,1)S(1)}, u32[]{:S(2)}, u32[]{:S(2)}) collective-permute-start(bf16[64,512]{1,0:T(8,128)(2,1)S(1)} %pad_maximum_fusion.3), channel_id=1, source_target_pairs={{0,0},{1,4},{2,8},{3,12},{4,1},{5,5},{6,9},{7,13},{8,2},{9,6},{10,... | collective-permute-start | bytes 196616 | tf_op jit(solution)/shard_map/ppermute | solution.py:252
  48.4 7.8 %collective-permute-start.18 = (bf16[64,128]{1,0:T(8,128)(2,1)S(1)}, bf16[64,128]{1,0:T(8,128)(2,1)S(1)}, u32[]{:S(2)}, u32[]{:S(2)}) collective-permute-start(bf16[64,128]{1,0:T(8,128)(2,1)S(1)} %get-tuple-element.46), channel_id=1, source_target_pairs={{0,8},{1,12},{2,0},{3,4},{4,9},{5,13},{6,1},{7,5},{8,10},{9,14},{1... | collective-permute-start | bytes 49160 | tf_op jit(solution)/shard_map/ppermute | solution.py:252
  53.7 9.7 %copy-start.3 = (bf16[4,32,1024]{2,1,0:T(8,128)(2,1)S(1)}, bf16[4,32,1024]{2,1,0:T(8,128)(2,1)}, u32[]{:S(2)}) copy-start(bf16[4,32,1024]{2,1,0:T(8,128)(2,1)} %param.25) | copy-start | bytes 786436
  64.6 8.3 %collective-permute-start.19 = (bf16[64,1024]{1,0:T(8,128)(2,1)S(1)}, bf16[64,1024]{1,0:T(8,128)(2,1)S(1)}, u32[]{:S(2)}, u32[]{:S(2)}) collective-permute-start(bf16[64,1024]{1,0:T(8,128)(2,1)S(1)} %get-tuple-element.42), channel_id=1, source_target_pairs={{0,4},{4,8},{8,12},{12,0},{1,5},{5,9},{9,13},{13,1},{2,6},{6,10},{... | collective-permute-start | bytes 393224 | tf_op jit(solution)/shard_map/ppermute | solution.py:258
  65.7 12.2 %collective-permute-start.20 = (bf16[64,1024]{1,0:T(8,128)(2,1)S(1)}, bf16[64,1024]{1,0:T(8,128)(2,1)S(1)}, u32[]{:S(2)}, u32[]{:S(2)}) collective-permute-start(bf16[64,1024]{1,0:T(8,128)(2,1)S(1)} %get-tuple-element.43), channel_id=1, source_target_pairs={{0,8},{4,12},{8,0},{12,4},{1,9},{5,13},{9,1},{13,5},{2,10},{6,14},... | collective-permute-start | bytes 393224 | tf_op jit(solution)/shard_map/ppermute | solution.py:258
  67.2 10.8 %collective-permute-start.21 = (bf16[64,1024]{1,0:T(8,128)(2,1)S(1)}, bf16[64,1024]{1,0:T(8,128)(2,1)S(1)}, u32[]{:S(2)}, u32[]{:S(2)}) collective-permute-start(bf16[64,1024]{1,0:T(8,128)(2,1)S(1)} %get-tuple-element.44), channel_id=1, source_target_pairs={{0,12},{4,0},{8,4},{12,8},{1,13},{5,1},{9,5},{13,9},{2,14},{6,2},{... | collective-permute-start | bytes 393224 | tf_op jit(solution)/shard_map/ppermute | solution.py:258

commit v6 on v5

--- a/solution.py
+++ b/solution.py
@@ -201,14 +201,16 @@
             outs[e][:, b * rank_cols : (b + 1) * rank_cols] = hl[side * b + e].astype(outs[e].dtype)
 
 
-def down_kernel(count, place, hs, w, rd, *refs):
+def down_kernel(count, side, place, mine, other, w, rd, *refs):
     outs, total = refs[:count], refs[count]
     rows = outs[0].shape[0]
     inner = w.shape[0]
+    hs = jnp.concatenate([mine[...], other[...]], axis=0)
     total[...] = jnp.dot(hs[:, :inner], w[...], preferred_element_type=F32)
     total[...] += jnp.dot(hs[:, inner:], rd[...], preferred_element_type=F32)
     for k in range(count):
-        start = pl.multiple_of(lax.rem(place[0] + k, count) * rows, rows)
+        away = lax.rem(place[0] + k, count) ^ place[1]
+        start = pl.multiple_of((lax.rem(away, side) * side + away // side) * rows, rows)
         outs[k][...] = total[pl.ds(start, rows), :].astype(outs[k].dtype)
 
 
@@ -361,15 +363,15 @@
     first = swap(jnp.concatenate([hsum, part[0]], axis=1))
     low_sum = first[:, inner:].astype(F32) + sum(swap(part[b], side * b).astype(F32) for b in range(1, side))
     hs = jnp.concatenate([first[:, :inner], low_sum.astype(BF16)], axis=1)
-    hs = lax.all_gather(hs, "narrow", axis=0, tiled=True)
+    hs = jnp.concatenate([hs, across(hs, "narrow", side)], axis=0)
     outs = pl.pallas_call(
-        functools.partial(down_kernel, count),
+        functools.partial(down_kernel, count, side),
         out_shape=[jax.ShapeDtypeStruct((rows, features), F32 if k == 0 else BF16) for k in range(count)],
-        in_specs=[SMEM] + [VMEM] * 3,
+        in_specs=[SMEM] + [VMEM] * 4,
         out_specs=[VMEM] * count,
         scratch_shapes=[pltpu.VMEM((count * rows, features), F32)],
         compiler_params=PARAMS,
-    )(places, hs, base_down, down_right.reshape(rank_cols, features))
+    )(places, hs, across(hs, "narrow", 1), base_down, down_right.reshape(rank_cols, features))
     return sum([outs[0]] + [ahead(outs[k], k).astype(F32) for k in range(1, count)]).astype(BF16)
 
 

time: 79.1 us -> 78.7 us (level)
  blocking collectives: 7.16 us -> 0 us
  starting transfers between devices: 36.7 us -> 40.1 us
  waiting for transfers between devices: 25.4 us -> 28.5 us
    all_gather x1 -> x0, blocking collectives: 7.16 us -> none  [stationary_shards(): hs = lax.all_gather(hs, 'narrow', axis=0, tiled=True)]
    ppermute x9 -> x11, waiting for transfers between devices: 11.8 us -> 15.4 us  [across(): return lax.ppermute(a, axis, [(i, i ^ k) for i in range(count)])]
    ppermute x9 -> x11, starting transfers between devices: 7.42 us -> 10.5 us  [across(): return lax.ppermute(a, axis, [(i, i ^ k) for i in range(count)])]
  transfers between devices with their start and end apart: 22 -> 24, of which waited for: 11 -> 13; matrix products, arithmetic and copies ran while one was open for 2% -> 2% of each run, Pallas kernels for 5% -> 5%
where the time goes in v6:
time: 78.7 us; the launch traced here: 77.9 us
  starting transfers between devices  40.1 us (51%)
  waiting for transfers between devices  28.5 us (36%)
  Pallas kernels  6.2 us (8%)
  other arithmetic  2.19 us (3%)
    ppermute x11, waiting for transfers between devices, across(): return lax.ppermute(a, axis, [(i, i ^ k) for i in range(count)])  15.4 us
    ppermute x11, starting transfers between devices, across(): return lax.ppermute(a, axis, [(i, i ^ k) for i in range(count)])  10.5 us
    ppermute x4, starting transfers between devices, stationary_shards(): spread.append(lax.ppermute(tokens, ('wide', 'narrow'), pairs))  8.76 us
    ppermute x3, waiting for transfers between devices, ahead(): return lax.ppermute(a, 'wide', [(i, (i + k) % count) for i in range(count)])  8.24 us
    ppermute x2, starting transfers between devices, stationary_shards(): lax.ppermute(spread[side * a], ('wide', 'narrow'), pairs)  6.38 us
    ppermute x2, starting transfers between devices, swap(): return lax.ppermute(a, ('wide', 'narrow'), pairs)  5.98 us
    ppermute x3, starting transfers between devices, ahead(): return lax.ppermute(a, 'wide', [(i, (i + k) % count) for i in range(count)])  4.89 us
    ppermute x2, waiting for transfers between devices, swap(): return lax.ppermute(a, ('wide', 'narrow'), pairs)  2.49 us
  transfers between devices with their start and end apart: 24, of which 13 were waited for; matrix products, arithmetic and copies ran while one was open for 2% of the time, Pallas kernels for 5%

profile of v6, /device:TPU:0, one launch (start us, length us, event | category | flops | bytes accessed | tf_op | source)
XLA Modules:
  0.0 77.9 jit_solution(15992936381218967775)
XLA Ops:
  0.0 4.0 %collective-permute-start.2 = (bf16[64,1024]{1,0:T(8,128)(2,1)}, bf16[64,1024]{1,0:T(8,128)(2,1)S(1)}, u32[]{:S(2)}, u32[]{:S(2)}) collective-permute-start(bf16[64,1024]{1,0:T(8,128)(2,1)} %param.13), channel_id=1, source_target_pairs={{0,8},{1,12},{2,10},{3,14},{4,9},{5,13},{6,11},{7,15},{8,0},{9,4},... | collective-permute-start | bytes 393224 | tf_op jit(solution)/shard_map/ppermute | solution.py:269
  4.0 1.6 %collective-permute-start = (bf16[64,1024]{1,0:T(8,128)(2,1)}, bf16[64,1024]{1,0:T(8,128)(2,1)S(1)}, u32[]{:S(2)}, u32[]{:S(2)}) collective-permute-start(bf16[64,1024]{1,0:T(8,128)(2,1)} %param.13), channel_id=1, source_target_pairs={{0,0},{1,4},{2,2},{3,6},{4,1},{5,5},{6,3},{7,7},{8,8},{9,12},{10,1... | collective-permute-start | bytes 393224 | tf_op jit(solution)/shard_map/ppermute | solution.py:269
  5.6 3.2 %collective-permute-start.4 = (bf16[64,1024]{1,0:T(8,128)(2,1)}, bf16[64,1024]{1,0:T(8,128)(2,1)S(1)}, u32[]{:S(2)}, u32[]{:S(2)}) collective-permute-start(bf16[64,1024]{1,0:T(8,128)(2,1)} %param.13), channel_id=1, source_target_pairs={{0,4},{1,0},{2,6},{3,2},{4,5},{5,1},{6,7},{7,3},{8,12},{9,8},{10,1... | collective-permute-start | bytes 393224 | tf_op jit(solution)/shard_map/ppermute | solution.py:269
  8.8 0.0 collective-permute-start.5
  8.8 1.1 %pad_maximum_fusion.refs_4_ = bf16[256,1024]{1,0:T(8,128)(2,1)S(1)} fusion(bf16[128,1024]{1,0:T(8,128)(2,1)} %bitcast.16, bf16[128,1024]{1,0:T(8,128)(2,1)} %bitcast.17), kind=kLoop, calls=%fused_computation | loop fusion | flops 1048576 | bytes 1048576 | tf_op jit(solution)/shard_map/concatenate | solution.py:281
  9.9 0.1 collective-permute-start.6
  10.0 1.4 %collective-permute-done.2.refs_2_ = bf16[64,1024]{1,0:T(8,128)(2,1)S(1)} collective-permute-done((bf16[64,1024]{1,0:T(8,128)(2,1)}, bf16[64,1024]{1,0:T(8,128)(2,1)S(1)}, u32[]{:S(2)}, u32[]{:S(2)}) %collective-permute-start.2) | collective-permute-done | bytes 131104 | tf_op jit(solution)/shard_map/ppermute | solution.py:269
  11.4 3.4 %collective-permute-start.3 = (bf16[64,1024]{1,0:T(8,128)(2,1)S(1)}, bf16[64,1024]{1,0:T(8,128)(2,1)S(1)}, u32[]{:S(2)}, u32[]{:S(2)}) collective-permute-start(bf16[64,1024]{1,0:T(8,128)(2,1)S(1)} %collective-permute-done.2.refs_2_), channel_id=1, source_target_pairs={{0,2},{1,3},{4,6},{5,7},{10,8},{11,9},{14,12},{15,13},{16,18},{17,... | collective-permute-start | bytes 393224 | tf_op jit(solution)/shard_map/ppermute | solution.py:277
  14.9 0.1 pad_add_fusion.place
  14.9 0.0 collective-permute-done.refs_0_
  15.0 0.1 collective-permute-start.13
  15.1 0.0 collective-permute-done.4.refs_1_
  15.1 3.0 %collective-permute-start.1 = (bf16[64,1024]{1,0:T(8,128)(2,1)S(1)}, bf16[64,1024]{1,0:T(8,128)(2,1)S(1)}, u32[]{:S(2)}, u32[]{:S(2)}) collective-permute-start(bf16[64,1024]{1,0:T(8,128)(2,1)S(1)} %collective-permute-done.refs_0_), channel_id=1, source_target_pairs={{0,2},{1,3},{4,6},{5,7},{10,8},{11,9},{14,12},{15,13},{16,18},{17,... | collective-permute-start | bytes 393224 | tf_op jit(solution)/shard_map/ppermute | solution.py:277
  18.1 0.0 collective-permute-done.5.refs_3_
  18.1 0.0 collective-permute-done.3
  18.1 2.2 %collective-permute-start.14 = (bf16[3,128,384]{2,1,0:T(8,128)(2,1)S(1)}, bf16[3,128,384]{2,1,0:T(8,128)(2,1)S(1)}, u32[]{:S(2)}, u32[]{:S(2)}) collective-permute-start(bf16[3,128,384]{2,1,0:T(8,128)(2,1)S(1)} %pad_maximum_fusion.1.refs_5_), channel_id=1, source_target_pairs={{0,8},{4,12},{8,0},{12,4},{16,28},{20,24},{24,20},{28,16},{1,9},{5... | collective-permute-start | bytes 884744 | tf_op jit(solution)/shard_map/ppermute | solution.py:323
  20.3 0.8 %collective-permute-done.1 = bf16[64,1024]{1,0:T(8,128)(2,1)S(1)} collective-permute-done((bf16[64,1024]{1,0:T(8,128)(2,1)S(1)}, bf16[64,1024]{1,0:T(8,128)(2,1)S(1)}, u32[]{:S(2)}, u32[]{:S(2)}) %collective-permute-start.1) | collective-permute-done | bytes 131104 | tf_op jit(solution)/shard_map/ppermute | solution.py:277
  21.2 0.0 collective-permute-done.6.refs_5_
  21.2 0.0 copy-start.7
  21.2 0.0 copy-start.1
  21.2 1.0 %shard_map.127 = (f32[128,256]{1,0:T(8,128)S(1)}, bf16[128,256]{1,0:T(8,128)(2,1)S(1)}) custom-call(s32[3]{0:T(128)S(1)} %pad_add_fusion.place, bf16[64,1024]{1,0:T(8,128)(2,1)S(1)} %collective-permute-done.refs_0_, bf16[64,1024]{1,0:T(8,128)(2,1)S(1)} %collective-permute-done.4.refs_1_, bf16[64,1024]{1,0:T(8,128)(2,1)S(1)} %collective-permute-done.2.refs_2_, ...), custom_call_target="tpu_custom_call" | custom-call | tf_op jit(solution)/shard_map/pallas_call | solution.py:284
  22.2 0.0 copy-start
  22.2 2.5 %collective-permute-start.8 = (bf16[128,256]{1,0:T(8,128)(2,1)S(1)}, bf16[128,256]{1,0:T(8,128)(2,1)S(1)}, u32[]{:S(2)}, u32[]{:S(2)}) collective-permute-start(bf16[128,256]{1,0:T(8,128)(2,1)S(1)} %get-tuple-element.25), channel_id=1, source_target_pairs={{0,2},{1,3},{2,0},{3,1},{4,6},{5,7},{6,4},{7,5},{8,10},{9,11},{10,... | collective-permute-start | bytes 196616 | tf_op jit(solution)/shard_map/ppermute | solution.py:257
  24.8 0.1 collective-permute-start.7
  24.9 2.1 %collective-permute-done.8 = bf16[128,256]{1,0:T(8,128)(2,1)S(1)} collective-permute-done((bf16[128,256]{1,0:T(8,128)(2,1)S(1)}, bf16[128,256]{1,0:T(8,128)(2,1)S(1)}, u32[]{:S(2)}, u32[]{:S(2)}) %collective-permute-start.8) | collective-permute-done | bytes 65568 | tf_op jit(solution)/shard_map/ppermute | solution.py:257
  27.0 0.1 collective-permute-start.9
  27.1 0.5 copy-done.9
  27.7 0.1 select_reduce_fusion.1
  27.8 0.6 collective-permute-done.9.refs_3_
  28.4 0.0 collective-permute-done.7.refs_1_
  28.4 1.4 %shard_map.128 = (f32[64,1024]{1,0:T(8,128)S(1)}, bf16[64,1024]{1,0:T(8,128)(2,1)S(1)}, bf16[64,1024]{1,0:T(8,128)(2,1)S(1)}, bf16[64,1024]{1,0:T(8,128)(2,1)S(1)}) custom-call(s32[3]{0:T(128)S(1)} %pad_add_fusion.place, bf16[128,1024]{1,0:T(8,128)(2,1)S(1)} %pad_maximum_fusion.2.refs_0_, bf16[128,1024]{1,0:T(8,128)(2,1)S(1)} %collective-permute-done.7.refs_1_, ...), custom_call_target="tpu_custom_call" | custom-call | tf_op jit(solution)/shard_map/pallas_call | solution.py:295
  29.8 1.1 %collective-permute-start.10 = (bf16[64,1024]{1,0:T(8,128)(2,1)S(1)}, bf16[64,1024]{1,0:T(8,128)(2,1)S(1)}, u32[]{:S(2)}, u32[]{:S(2)}) collective-permute-start(bf16[64,1024]{1,0:T(8,128)(2,1)S(1)} %get-tuple-element.29), channel_id=1, source_target_pairs={{0,4},{4,0},{8,12},{12,8},{1,5},{5,1},{9,13},{13,9},{2,6},{6,2},{1... | collective-permute-start | bytes 393224 | tf_op jit(solution)/shard_map/ppermute | solution.py:257
  30.9 1.6 %collective-permute-start.11 = (bf16[64,1024]{1,0:T(8,128)(2,1)S(1)}, bf16[64,1024]{1,0:T(8,128)(2,1)S(1)}, u32[]{:S(2)}, u32[]{:S(2)}) collective-permute-start(bf16[64,1024]{1,0:T(8,128)(2,1)S(1)} %get-tuple-element.30), channel_id=1, source_target_pairs={{0,8},{4,12},{8,0},{12,4},{1,9},{5,13},{9,1},{13,5},{2,10},{6,14},... | collective-permute-start | bytes 393224 | tf_op jit(solution)/shard_map/ppermute | solution.py:257
  32.4 1.8 %collective-permute-start.12 = (bf16[64,1024]{1,0:T(8,128)(2,1)S(1)}, bf16[64,1024]{1,0:T(8,128)(2,1)S(1)}, u32[]{:S(2)}, u32[]{:S(2)}) collective-permute-start(bf16[64,1024]{1,0:T(8,128)(2,1)S(1)} %get-tuple-element.31), channel_id=1, source_target_pairs={{0,12},{4,8},{8,4},{12,0},{1,13},{5,9},{9,5},{13,1},{2,14},{6,10},... | collective-permute-start | bytes 393224 | tf_op jit(solution)/shard_map/ppermute | solution.py:257
  34.2 0.1 collective-permute-done.14.refs_7_
  34.3 1.4 %collective-permute-start.15 = (bf16[3,128,384]{2,1,0:T(8,128)(2,1)S(1)}, bf16[3,128,384]{2,1,0:T(8,128)(2,1)S(1)}, u32[]{:S(2)}, u32[]{:S(2)}) collective-permute-start(bf16[3,128,384]{2,1,0:T(8,128)(2,1)S(1)} %collective-permute-done.14.refs_7_), channel_id=1, source_target_pairs={{0,16},{16,0},{1,17},{17,1},{2,18},{18,2},{3,19},{19,3},{4,20},{20... | collective-permute-start | bytes 884744 | tf_op jit(solution)/shard_map/ppermute | solution.py:324
  35.8 0.1 copy.16.refs_4_.weight
  35.9 0.0 collective-permute-done.13.refs_6_
  35.9 3.6 %collective-permute-done.10.refs_1_ = bf16[64,1024]{1,0:T(8,128)(2,1)S(1)} collective-permute-done((bf16[64,1024]{1,0:T(8,128)(2,1)S(1)}, bf16[64,1024]{1,0:T(8,128)(2,1)S(1)}, u32[]{:S(2)}, u32[]{:S(2)}) %collective-permute-start.10) | collective-permute-done | bytes 131104 | tf_op jit(solution)/shard_map/ppermute | solution.py:257
  39.5 4.3 %collective-permute-done.11.refs_2_ = bf16[64,1024]{1,0:T(8,128)(2,1)S(1)} collective-permute-done((bf16[64,1024]{1,0:T(8,128)(2,1)S(1)}, bf16[64,1024]{1,0:T(8,128)(2,1)S(1)}, u32[]{:S(2)}, u32[]{:S(2)}) %collective-permute-start.11) | collective-permute-done | bytes 131104 | tf_op jit(solution)/shard_map/ppermute | solution.py:257
  43.8 0.0 collective-permute-done.12.refs_3_
  43.8 1.6 %shard_map.129 = (f32[64,768]{1,0:T(8,128)S(1)}, f32[64,384]{1,0:T(8,128)S(1)}, f32[4,64,128]{2,1,0:T(8,128)S(1)}, bf16[4,64,256]{2,1,0:T(8,128)(2,1)S(1)}) custom-call(s32[3]{0:T(128)S(1)} %pad_add_fusion.place, f32[64,1024]{1,0:T(8,128)S(1)} %get-tuple-element.28.refs_0_, bf16[64,1024]{1,0:T(8,128)(2,1)S(1)} %collective-permute-done.10.refs_1_, ...), custom_call_target="tpu_custom_call" | custom-call | tf_op jit(solution)/shard_map/pallas_call | solution.py:336
  45.4 0.0 collective-permute-done.15.r
  45.4 0.0 copy-start.2
  45.4 1.0 %shard_map.130 = (bf16[64,384]{1,0:T(8,128)(2,1)S(1)}, f32[64,256]{1,0:T(8,128)S(1)}, bf16[64,256]{1,0:T(8,128)(2,1)S(1)}) custom-call(s32[3]{0:T(128)S(1)} %pad_add_fusion.place, f32[64,768]{1,0:T(8,128)S(1)} %get-tuple-element.33.base, f32[64,384]{1,0:T(8,128)S(1)} %get-tuple-element.34.acc, f32[4,64,128]{2,1,0:T(8,128)S(1)} %get-tuple-element.35.come, ...), custom_call_target="tpu_custom_call" | custom-call | tf_op jit(solution)/shard_map/pallas_call | solution.py:348
  46.4 0.1 collective-permute-start.16
  46.5 1.2 %collective-permute-done.16 = bf16[64,256]{1,0:T(8,128)(2,1)S(1)} collective-permute-done((bf16[64,256]{1,0:T(8,128)(2,1)S(1)}, bf16[64,256]{1,0:T(8,128)(2,1)S(1)}, u32[]{:S(2)}, u32[]{:S(2)}) %collective-permute-start.16) | collective-permute-done | bytes 32800 | tf_op jit(solution)/shard_map/ppermute | solution.py:257
  47.7 0.7 collective-permute-start.17
  48.4 0.0 copy-start.3
  48.4 5.3 %collective-permute-start.18 = (bf16[64,128]{1,0:T(8,128)(2,1)S(1)}, bf16[64,128]{1,0:T(8,128)(2,1)S(1)}, u32[]{:S(2)}, u32[]{:S(2)}) collective-permute-start(bf16[64,128]{1,0:T(8,128)(2,1)S(1)} %get-tuple-element.46), channel_id=1, source_target_pairs={{0,8},{1,12},{2,0},{3,4},{4,9},{5,13},{6,1},{7,5},{8,10},{9,14},{1... | collective-permute-start | bytes 49160 | tf_op jit(solution)/shard_map/ppermute | solution.py:254
  53.7 0.0 collective-permute-done.17
  53.7 2.5 %collective-permute-done.18 = bf16[64,128]{1,0:T(8,128)(2,1)S(1)} collective-permute-done((bf16[64,128]{1,0:T(8,128)(2,1)S(1)}, bf16[64,128]{1,0:T(8,128)(2,1)S(1)}, u32[]{:S(2)}, u32[]{:S(2)}) %collective-permute-start.18) | collective-permute-done | bytes 16416 | tf_op jit(solution)/shard_map/ppermute | solution.py:254
  56.3 3.0 %collective-permute-start.19 = (bf16[64,512]{1,0:T(8,128)(2,1)S(1)}, bf16[64,512]{1,0:T(8,128)(2,1)S(1)}, u32[]{:S(2)}, u32[]{:S(2)}) collective-permute-start(bf16[64,512]{1,0:T(8,128)(2,1)S(1)} %pad_maximum_fusion.5), channel_id=1, source_target_pairs={{0,2},{1,3},{2,0},{3,1},{4,6},{5,7},{6,4},{7,5},{8,10},{9,11},{10,... | collective-permute-start | bytes 196616 | tf_op jit(solution)/shard_map/ppermute | solution.py:257
  59.2 2.2 %collective-permute-done.19 = bf16[64,512]{1,0:T(8,128)(2,1)S(1)} collective-permute-done((bf16[64,512]{1,0:T(8,128)(2,1)S(1)}, bf16[64,512]{1,0:T(8,128)(2,1)S(1)}, u32[]{:S(2)}, u32[]{:S(2)}) %collective-permute-start.19) | collective-permute-done | bytes 65568 | tf_op jit(solution)/shard_map/ppermute | solution.py:257
  61.5 0.1 collective-permute-start.20
  61.6 1.3 %collective-permute-done.20.other = bf16[128,512]{1,0:T(8,128)(2,1)S(1)} collective-permute-done((bf16[128,512]{1,0:T(8,128)(2,1)S(1)}, bf16[128,512]{1,0:T(8,128)(2,1)S(1)}, u32[]{:S(2)}, u32[]{:S(2)}) %collective-permute-start.20) | collective-permute-done | bytes 131104 | tf_op jit(solution)/shard_map/ppermute | solution.py:257
  62.9 1.2 %shard_map.131 = (f32[64,1024]{1,0:T(8,128)S(1)}, bf16[64,1024]{1,0:T(8,128)(2,1)S(1)}, bf16[64,1024]{1,0:T(8,128)(2,1)S(1)}, bf16[64,1024]{1,0:T(8,128)(2,1)S(1)}) custom-call(s32[3]{0:T(128)S(1)} %pad_add_fusion.place, bf16[128,512]{1,0:T(8,128)(2,1)S(1)} %pad_maximum_fusion.3.mine, bf16[128,512]{1,0:T(8,128)(2,1)S(1)} %collective-permute-done.20.other, ...), custom_call_target="tpu_custom_call" | custom-call | tf_op jit(solution)/shard_map/pallas_call | solution.py:367
  64.1 0.9 %collective-permute-start.21 = (bf16[64,1024]{1,0:T(8,128)(2,1)S(1)}, bf16[64,1024]{1,0:T(8,128)(2,1)S(1)}, u32[]{:S(2)}, u32[]{:S(2)}) collective-permute-start(bf16[64,1024]{1,0:T(8,128)(2,1)S(1)} %get-tuple-element.42), channel_id=1, source_target_pairs={{0,4},{4,8},{8,12},{12,0},{1,5},{5,9},{9,13},{13,1},{2,6},{6,10},{... | collective-permute-start | bytes 393224 | tf_op jit(solution)/shard_map/ppermute | solution.py:260
  65.0 2.1 %collective-permute-start.22 = (bf16[64,1024]{1,0:T(8,128)(2,1)S(1)}, bf16[64,1024]{1,0:T(8,128)(2,1)S(1)}, u32[]{:S(2)}, u32[]{:S(2)}) collective-permute-start(bf16[64,1024]{1,0:T(8,128)(2,1)S(1)} %get-tuple-element.43), channel_id=1, source_target_pairs={{0,8},{4,12},{8,0},{12,4},{1,9},{5,13},{9,1},{13,5},{2,10},{6,14},... | collective-permute-start | bytes 393224 | tf_op jit(solution)/shard_map/ppermute | solution.py:260
  67.1 1.8 %collective-permute-start.23 = (bf16[64,1024]{1,0:T(8,128)(2,1)S(1)}, bf16[64,1024]{1,0:T(8,128)(2,1)S(1)}, u32[]{:S(2)}, u32[]{:S(2)}) collective-permute-start(bf16[64,1024]{1,0:T(8,128)(2,1)S(1)} %get-tuple-element.44), channel_id=1, source_target_pairs={{0,12},{4,0},{8,4},{12,8},{1,13},{5,1},{9,5},{13,9},{2,14},{6,2},{... | collective-permute-start | bytes 393224 | tf_op jit(solution)/shard_map/ppermute | solution.py:260
  69.0 3.4 %collective-permute-done.21 = bf16[64,1024]{1,0:T(8,128)(2,1)S(1)} collective-permute-done((bf16[64,1024]{1,0:T(8,128)(2,1)S(1)}, bf16[64,1024]{1,0:T(8,128)(2,1)S(1)}, u32[]{:S(2)}, u32[]{:S(2)}) %collective-permute-start.21) | collective-permute-done | bytes 131104 | tf_op jit(solution)/shard_map/ppermute | solution.py:260
  72.4 4.8 %collective-permute-done.22 = bf16[64,1024]{1,0:T(8,128)(2,1)S(1)} collective-permute-done((bf16[64,1024]{1,0:T(8,128)(2,1)S(1)}, bf16[64,1024]{1,0:T(8,128)(2,1)S(1)}, u32[]{:S(2)}, u32[]{:S(2)}) %collective-permute-start.22) | collective-permute-done | bytes 131104 | tf_op jit(solution)/shard_map/ppermute | solution.py:260
  77.2 0.0 collective-permute-done.23
  77.2 0.7 add_convert_fusion
  (28 shorter events, 0.2 us)
Async XLA Ops:
  0.0 11.4 %collective-permute-start.2 = (bf16[64,1024]{1,0:T(8,128)(2,1)}, bf16[64,1024]{1,0:T(8,128)(2,1)S(1)}, u32[]{:S(2)}, u32[]{:S(2)}) collective-permute-start(bf16[64,1024]{1,0:T(8,128)(2,1)} %param.13), channel_id=1, source_target_pairs={{0,8},{1,12},{2,10},{3,14},{4,9},{5,13},{6,11},{7,15},{8,0},{9,4},... | collective-permute-start | bytes 393224 | tf_op jit(solution)/shard_map/ppermute | solution.py:269
  4.0 10.9 %collective-permute-start = (bf16[64,1024]{1,0:T(8,128)(2,1)}, bf16[64,1024]{1,0:T(8,128)(2,1)S(1)}, u32[]{:S(2)}, u32[]{:S(2)}) collective-permute-start(bf16[64,1024]{1,0:T(8,128)(2,1)} %param.13), channel_id=1, source_target_pairs={{0,0},{1,4},{2,2},{3,6},{4,1},{5,5},{6,3},{7,7},{8,8},{9,12},{10,1... | collective-permute-start | bytes 393224 | tf_op jit(solution)/shard_map/ppermute | solution.py:269
  5.6 9.5 %collective-permute-start.4 = (bf16[64,1024]{1,0:T(8,128)(2,1)}, bf16[64,1024]{1,0:T(8,128)(2,1)S(1)}, u32[]{:S(2)}, u32[]{:S(2)}) collective-permute-start(bf16[64,1024]{1,0:T(8,128)(2,1)} %param.13), channel_id=1, source_target_pairs={{0,4},{1,0},{2,6},{3,2},{4,5},{5,1},{6,7},{7,3},{8,12},{9,8},{10,1... | collective-permute-start | bytes 393224 | tf_op jit(solution)/shard_map/ppermute | solution.py:269
  8.8 9.3 %collective-permute-start.5 = (bf16[64,1024]{1,0:T(8,128)(2,1)}, bf16[64,1024]{1,0:T(8,128)(2,1)S(1)}, u32[]{:S(2)}, u32[]{:S(2)}) collective-permute-start(bf16[64,1024]{1,0:T(8,128)(2,1)} %param.13), channel_id=1, source_target_pairs={{0,12},{1,8},{2,14},{3,10},{4,13},{5,9},{6,15},{7,11},{8,4},{9,0},... | collective-permute-start | bytes 393224 | tf_op jit(solution)/shard_map/ppermute | solution.py:269
  8.8 6.0 %copy-start.4 = (bf16[4,384,32]{1,2,0:T(8,128)(2,1)S(1)}, bf16[4,384,32]{1,2,0:T(8,128)(2,1)}, u32[]{:S(2)}) copy-start(bf16[4,384,32]{1,2,0:T(8,128)(2,1)} %param.24) | copy-start | bytes 294916
  8.8 6.0 %copy-start.5 = (bf16[4,32,384]{2,1,0:T(8,128)(2,1)S(1)}, bf16[4,32,384]{2,1,0:T(8,128)(2,1)}, u32[]{:S(2)}) copy-start(bf16[4,32,384]{2,1,0:T(8,128)(2,1)} %param.23) | copy-start | bytes 294916
  8.8 6.0 %copy-start.6 = (bf16[4,32,384]{2,1,0:T(8,128)(2,1)S(1)}, bf16[4,32,384]{2,1,0:T(8,128)(2,1)}, u32[]{:S(2)}) copy-start(bf16[4,32,384]{2,1,0:T(8,128)(2,1)} %param.21) | copy-start | bytes 294916
  9.9 11.3 %collective-permute-start.6 = (bf16[256,1024]{1,0:T(8,128)(2,1)S(1)}, bf16[256,1024]{1,0:T(8,128)(2,1)S(1)}, u32[]{:S(2)}, u32[]{:S(2)}) collective-permute-start(bf16[256,1024]{1,0:T(8,128)(2,1)S(1)} %pad_maximum_fusion.refs_4_), channel_id=1, source_target_pairs={{0,1},{1,0},{2,3},{3,2},{4,5},{5,4},{6,7},{7,6},{8,9},{9,8},{10,11... | collective-permute-start | bytes 1572872 | tf_op jit(solution)/shard_map/ppermute | solution.py:257
  11.4 6.7 %collective-permute-start.3 = (bf16[64,1024]{1,0:T(8,128)(2,1)S(1)}, bf16[64,1024]{1,0:T(8,128)(2,1)S(1)}, u32[]{:S(2)}, u32[]{:S(2)}) collective-permute-start(bf16[64,1024]{1,0:T(8,128)(2,1)S(1)} %collective-permute-done.2.refs_2_), channel_id=1, source_target_pairs={{0,2},{1,3},{4,6},{5,7},{10,8},{11,9},{14,12},{15,13},{16,18},{17,... | collective-permute-start | bytes 393224 | tf_op jit(solution)/shard_map/ppermute | solution.py:277
  15.0 20.9 %collective-permute-start.13 = (bf16[3,128,384]{2,1,0:T(8,128)(2,1)S(1)}, bf16[3,128,384]{2,1,0:T(8,128)(2,1)S(1)}, u32[]{:S(2)}, u32[]{:S(2)}) collective-permute-start(bf16[3,128,384]{2,1,0:T(8,128)(2,1)S(1)} %pad_maximum_fusion.1.refs_5_), channel_id=1, source_target_pairs={{0,4},{4,0},{8,12},{12,8},{1,5},{5,1},{9,13},{13,9},{2,6},{6,2},{1... | collective-permute-start | bytes 884744 | tf_op jit(solution)/shard_map/ppermute | solution.py:257
  15.1 6.0 %collective-permute-start.1 = (bf16[64,1024]{1,0:T(8,128)(2,1)S(1)}, bf16[64,1024]{1,0:T(8,128)(2,1)S(1)}, u32[]{:S(2)}, u32[]{:S(2)}) collective-permute-start(bf16[64,1024]{1,0:T(8,128)(2,1)S(1)} %collective-permute-done.refs_0_), channel_id=1, source_target_pairs={{0,2},{1,3},{4,6},{5,7},{10,8},{11,9},{14,12},{15,13},{16,18},{17,... | collective-permute-start | bytes 393224 | tf_op jit(solution)/shard_map/ppermute | solution.py:277
  18.1 16.2 %collective-permute-start.14 = (bf16[3,128,384]{2,1,0:T(8,128)(2,1)S(1)}, bf16[3,128,384]{2,1,0:T(8,128)(2,1)S(1)}, u32[]{:S(2)}, u32[]{:S(2)}) collective-permute-start(bf16[3,128,384]{2,1,0:T(8,128)(2,1)S(1)} %pad_maximum_fusion.1.refs_5_), channel_id=1, source_target_pairs={{0,8},{4,12},{8,0},{12,4},{16,28},{20,24},{24,20},{28,16},{1,9},{5... | collective-permute-start | bytes 884744 | tf_op jit(solution)/shard_map/ppermute | solution.py:323
  21.2 6.0 %copy-start.7 = (s32[64,8]{0,1:T(8,128)S(1)}, s32[64,8]{0,1:T(8,128)}, u32[]{:S(2)}) copy-start(s32[64,8]{0,1:T(8,128)} %param.14) | copy-start | bytes 6148
  21.2 7.2 %copy-start.1 = (bf16[1024,384]{1,0:T(8,128)(2,1)S(1)}, bf16[1024,384]{1,0:T(8,128)(2,1)}, u32[]{:S(2)}) copy-start(bf16[1024,384]{1,0:T(8,128)(2,1)} %refs_5_.1) | copy-start | bytes 2359300
  22.2 6.2 %copy-start = (bf16[1024,384]{1,0:T(8,128)(2,1)S(1)}, bf16[1024,384]{1,0:T(8,128)(2,1)}, u32[]{:S(2)}) copy-start(bf16[1024,384]{1,0:T(8,128)(2,1)} %refs_4_.1) | copy-start | bytes 2359300
  22.2 4.8 %collective-permute-start.8 = (bf16[128,256]{1,0:T(8,128)(2,1)S(1)}, bf16[128,256]{1,0:T(8,128)(2,1)S(1)}, u32[]{:S(2)}, u32[]{:S(2)}) collective-permute-start(bf16[128,256]{1,0:T(8,128)(2,1)S(1)} %get-tuple-element.25), channel_id=1, source_target_pairs={{0,2},{1,3},{2,0},{3,1},{4,6},{5,7},{6,4},{7,5},{8,10},{9,11},{10,... | collective-permute-start | bytes 196616 | tf_op jit(solution)/shard_map/ppermute | solution.py:257
  24.8 3.6 %collective-permute-start.7 = (bf16[128,1024]{1,0:T(8,128)(2,1)S(1)}, bf16[128,1024]{1,0:T(8,128)(2,1)S(1)}, u32[]{:S(2)}, u32[]{:S(2)}) collective-permute-start(bf16[128,1024]{1,0:T(8,128)(2,1)S(1)} %pad_maximum_fusion.2.refs_0_), channel_id=1, source_target_pairs={{0,1},{1,0},{2,3},{3,2},{4,5},{5,4},{6,7},{7,6},{8,9},{9,8},{10,11... | collective-permute-start | bytes 786440 | tf_op jit(solution)/shard_map/ppermute | solution.py:257
  27.0 0.7 copy-start.9
  27.0 1.3 %collective-permute-start.9 = (bf16[128,256]{1,0:T(8,128)(2,1)S(1)}, bf16[128,256]{1,0:T(8,128)(2,1)S(1)}, u32[]{:S(2)}, u32[]{:S(2)}) collective-permute-start(bf16[128,256]{1,0:T(8,128)(2,1)S(1)} %add_convert_fusion.1.refs_2_), channel_id=1, source_target_pairs={{0,1},{1,0},{2,3},{3,2},{4,5},{5,4},{6,7},{7,6},{8,9},{9,8},{10,11... | collective-permute-start | bytes 196616 | tf_op jit(solution)/shard_map/ppermute | solution.py:257
  29.8 9.7 %collective-permute-start.10 = (bf16[64,1024]{1,0:T(8,128)(2,1)S(1)}, bf16[64,1024]{1,0:T(8,128)(2,1)S(1)}, u32[]{:S(2)}, u32[]{:S(2)}) collective-permute-start(bf16[64,1024]{1,0:T(8,128)(2,1)S(1)} %get-tuple-element.29), channel_id=1, source_target_pairs={{0,4},{4,0},{8,12},{12,8},{1,5},{5,1},{9,13},{13,9},{2,6},{6,2},{1... | collective-permute-start | bytes 393224 | tf_op jit(solution)/shard_map/ppermute | solution.py:257
  30.9 12.9 %collective-permute-start.11 = (bf16[64,1024]{1,0:T(8,128)(2,1)S(1)}, bf16[64,1024]{1,0:T(8,128)(2,1)S(1)}, u32[]{:S(2)}, u32[]{:S(2)}) collective-permute-start(bf16[64,1024]{1,0:T(8,128)(2,1)S(1)} %get-tuple-element.30), channel_id=1, source_target_pairs={{0,8},{4,12},{8,0},{12,4},{1,9},{5,13},{9,1},{13,5},{2,10},{6,14},... | collective-permute-start | bytes 393224 | tf_op jit(solution)/shard_map/ppermute | solution.py:257
  32.4 11.3 %collective-permute-start.12 = (bf16[64,1024]{1,0:T(8,128)(2,1)S(1)}, bf16[64,1024]{1,0:T(8,128)(2,1)S(1)}, u32[]{:S(2)}, u32[]{:S(2)}) collective-permute-start(bf16[64,1024]{1,0:T(8,128)(2,1)S(1)} %get-tuple-element.31), channel_id=1, source_target_pairs={{0,12},{4,8},{8,4},{12,0},{1,13},{5,9},{9,5},{13,1},{2,14},{6,10},... | collective-permute-start | bytes 393224 | tf_op jit(solution)/shard_map/ppermute | solution.py:257
  34.3 1.4 %copy-start.8 = (f32[64,8]{0,1:T(8,128)S(1)}, f32[64,8]{0,1:T(8,128)}, u32[]{:S(2)}) copy-start(f32[64,8]{0,1:T(8,128)} %param.15) | copy-start | bytes 6148
  34.3 11.1 %collective-permute-start.15 = (bf16[3,128,384]{2,1,0:T(8,128)(2,1)S(1)}, bf16[3,128,384]{2,1,0:T(8,128)(2,1)S(1)}, u32[]{:S(2)}, u32[]{:S(2)}) collective-permute-start(bf16[3,128,384]{2,1,0:T(8,128)(2,1)S(1)} %collective-permute-done.14.refs_7_), channel_id=1, source_target_pairs={{0,16},{16,0},{1,17},{17,1},{2,18},{18,2},{3,19},{19,3},{4,20},{20... | collective-permute-start | bytes 884744 | tf_op jit(solution)/shard_map/ppermute | solution.py:324
  45.4 17.5 %copy-start.2 = (bf16[384,1024]{1,0:T(8,128)(2,1)S(1)}, bf16[384,1024]{1,0:T(8,128)(2,1)}, u32[]{:S(2)}) copy-start(bf16[384,1024]{1,0:T(8,128)(2,1)} %w.1) | copy-start | bytes 2359300
  46.4 1.3 %collective-permute-start.16 = (bf16[64,256]{1,0:T(8,128)(2,1)S(1)}, bf16[64,256]{1,0:T(8,128)(2,1)S(1)}, u32[]{:S(2)}, u32[]{:S(2)}) collective-permute-start(bf16[64,256]{1,0:T(8,128)(2,1)S(1)} %get-tuple-element.40), channel_id=1, source_target_pairs={{0,1},{1,0},{2,3},{3,2},{4,5},{5,4},{6,7},{7,6},{8,9},{9,8},{10,11... | collective-permute-start | bytes 98312 | tf_op jit(solution)/shard_map/ppermute | solution.py:257
  47.7 6.0 %collective-permute-start.17 = (bf16[64,512]{1,0:T(8,128)(2,1)S(1)}, bf16[64,512]{1,0:T(8,128)(2,1)S(1)}, u32[]{:S(2)}, u32[]{:S(2)}) collective-permute-start(bf16[64,512]{1,0:T(8,128)(2,1)S(1)} %pad_maximum_fusion.4), channel_id=1, source_target_pairs={{0,0},{1,4},{2,8},{3,12},{4,1},{5,5},{6,9},{7,13},{8,2},{9,6},{10,... | collective-permute-start | bytes 196616 | tf_op jit(solution)/shard_map/ppermute | solution.py:254
  48.4 14.5 %copy-start.3 = (bf16[4,32,1024]{2,1,0:T(8,128)(2,1)S(1)}, bf16[4,32,1024]{2,1,0:T(8,128)(2,1)}, u32[]{:S(2)}) copy-start(bf16[4,32,1024]{2,1,0:T(8,128)(2,1)} %param.25) | copy-start | bytes 786436
  48.4 7.8 %collective-permute-start.18 = (bf16[64,128]{1,0:T(8,128)(2,1)S(1)}, bf16[64,128]{1,0:T(8,128)(2,1)S(1)}, u32[]{:S(2)}, u32[]{:S(2)}) collective-permute-start(bf16[64,128]{1,0:T(8,128)(2,1)S(1)} %get-tuple-element.46), channel_id=1, source_target_pairs={{0,8},{1,12},{2,0},{3,4},{4,9},{5,13},{6,1},{7,5},{8,10},{9,14},{1... | collective-permute-start | bytes 49160 | tf_op jit(solution)/shard_map/ppermute | solution.py:254
  56.3 5.2 %collective-permute-start.19 = (bf16[64,512]{1,0:T(8,128)(2,1)S(1)}, bf16[64,512]{1,0:T(8,128)(2,1)S(1)}, u32[]{:S(2)}, u32[]{:S(2)}) collective-permute-start(bf16[64,512]{1,0:T(8,128)(2,1)S(1)} %pad_maximum_fusion.5), channel_id=1, source_target_pairs={{0,2},{1,3},{2,0},{3,1},{4,6},{5,7},{6,4},{7,5},{8,10},{9,11},{10,... | collective-permute-start | bytes 196616 | tf_op jit(solution)/shard_map/ppermute | solution.py:257
  61.5 1.4 %collective-permute-start.20 = (bf16[128,512]{1,0:T(8,128)(2,1)S(1)}, bf16[128,512]{1,0:T(8,128)(2,1)S(1)}, u32[]{:S(2)}, u32[]{:S(2)}) collective-permute-start(bf16[128,512]{1,0:T(8,128)(2,1)S(1)} %pad_maximum_fusion.3.mine), channel_id=1, source_target_pairs={{0,1},{1,0},{2,3},{3,2},{4,5},{5,4},{6,7},{7,6},{8,9},{9,8},{10,11... | collective-permute-start | bytes 393224 | tf_op jit(solution)/shard_map/ppermute | solution.py:257
  64.1 8.3 %collective-permute-start.21 = (bf16[64,1024]{1,0:T(8,128)(2,1)S(1)}, bf16[64,1024]{1,0:T(8,128)(2,1)S(1)}, u32[]{:S(2)}, u32[]{:S(2)}) collective-permute-start(bf16[64,1024]{1,0:T(8,128)(2,1)S(1)} %get-tuple-element.42), channel_id=1, source_target_pairs={{0,4},{4,8},{8,12},{12,0},{1,5},{5,9},{9,13},{13,1},{2,6},{6,10},{... | collective-permute-start | bytes 393224 | tf_op jit(solution)/shard_map/ppermute | solution.py:260
  65.0 12.2 %collective-permute-start.22 = (bf16[64,1024]{1,0:T(8,128)(2,1)S(1)}, bf16[64,1024]{1,0:T(8,128)(2,1)S(1)}, u32[]{:S(2)}, u32[]{:S(2)}) collective-permute-start(bf16[64,1024]{1,0:T(8,128)(2,1)S(1)} %get-tuple-element.43), channel_id=1, source_target_pairs={{0,8},{4,12},{8,0},{12,4},{1,9},{5,13},{9,1},{13,5},{2,10},{6,14},... | collective-permute-start | bytes 393224 | tf_op jit(solution)/shard_map/ppermute | solution.py:260
  67.1 10.1 %collective-permute-start.23 = (bf16[64,1024]{1,0:T(8,128)(2,1)S(1)}, bf16[64,1024]{1,0:T(8,128)(2,1)S(1)}, u32[]{:S(2)}, u32[]{:S(2)}) collective-permute-start(bf16[64,1024]{1,0:T(8,128)(2,1)S(1)} %get-tuple-element.44), channel_id=1, source_target_pairs={{0,12},{4,0},{8,4},{12,8},{1,13},{5,1},{9,5},{13,9},{2,14},{6,2},{... | collective-permute-start | bytes 393224 | tf_op jit(solution)/shard_map/ppermute | solution.py:260

commit v7 on v6

--- a/solution.py
+++ b/solution.py
@@ -201,11 +201,11 @@
             outs[e][:, b * rank_cols : (b + 1) * rank_cols] = hl[side * b + e].astype(outs[e].dtype)
 
 
-def down_kernel(count, side, place, mine, other, w, rd, *refs):
-    outs, total = refs[:count], refs[count]
+def down_kernel(count, side, place, *refs):
+    blocks, (w, rd), outs, total = refs[:count], refs[count : count + 2], refs[count + 2 : -1], refs[-1]
     rows = outs[0].shape[0]
     inner = w.shape[0]
-    hs = jnp.concatenate([mine[...], other[...]], axis=0)
+    hs = jnp.concatenate([b[...] for b in blocks], axis=0)
     total[...] = jnp.dot(hs[:, :inner], w[...], preferred_element_type=F32)
     total[...] += jnp.dot(hs[:, inner:], rd[...], preferred_element_type=F32)
     for k in range(count):
@@ -363,15 +363,16 @@
     first = swap(jnp.concatenate([hsum, part[0]], axis=1))
     low_sum = first[:, inner:].astype(F32) + sum(swap(part[b], side * b).astype(F32) for b in range(1, side))
     hs = jnp.concatenate([first[:, :inner], low_sum.astype(BF16)], axis=1)
-    hs = jnp.concatenate([hs, across(hs, "narrow", side)], axis=0)
+    hs = [hs, across(hs, "narrow", side)]
+    hs = hs + [across(h, "narrow", 1) for h in hs]
     outs = pl.pallas_call(
         functools.partial(down_kernel, count, side),
         out_shape=[jax.ShapeDtypeStruct((rows, features), F32 if k == 0 else BF16) for k in range(count)],
-        in_specs=[SMEM] + [VMEM] * 4,
+        in_specs=[SMEM] + [VMEM] * (count + 2),
         out_specs=[VMEM] * count,
         scratch_shapes=[pltpu.VMEM((count * rows, features), F32)],
         compiler_params=PARAMS,
-    )(places, hs, across(hs, "narrow", 1), base_down, down_right.reshape(rank_cols, features))
+    )(places, *hs, base_down, down_right.reshape(rank_cols, features))
     return sum([outs[0]] + [ahead(outs[k], k).astype(F32) for k in range(1, count)]).astype(BF16)
 
 

time: 78.7 us -> 78.7 us (level)
    ppermute x11 -> x12, waiting for transfers between devices: 15.4 us -> 15.3 us  [across(): return lax.ppermute(a, axis, [(i, i ^ k) for i in range(count)])]
    ppermute x11 -> x12, starting transfers between devices: 10.5 us -> 10.4 us  [across(): return lax.ppermute(a, axis, [(i, i ^ k) for i in range(count)])]
  transfers between devices with their start and end apart: 24 -> 25, of which waited for: 13 -> 13; matrix products, arithmetic and copies ran while one was open for 2% -> 2% of each run, Pallas kernels for 5% -> 5%
where the time goes in v7:
time: 78.7 us; the launch traced here: 77.9 us
  starting transfers between devices  40.2 us (51%)
  waiting for transfers between devices  28.4 us (36%)
  Pallas kernels  6.2 us (8%)
  other arithmetic  2.18 us (3%)
    ppermute x12, waiting for transfers between devices, across(): return lax.ppermute(a, axis, [(i, i ^ k) for i in range(count)])  15.3 us
    ppermute x12, starting transfers between devices, across(): return lax.ppermute(a, axis, [(i, i ^ k) for i in range(count)])  10.4 us
    ppermute x4, starting transfers between devices, stationary_shards(): spread.append(lax.ppermute(tokens, ('wide', 'narrow'), pairs))  8.76 us
    ppermute x3, waiting for transfers between devices, ahead(): return lax.ppermute(a, 'wide', [(i, (i + k) % count) for i in range(count)])  8.23 us
    ppermute x2, starting transfers between devices, stationary_shards(): lax.ppermute(spread[side * a], ('wide', 'narrow'), pairs)  6.38 us
    ppermute x2, starting transfers between devices, swap(): return lax.ppermute(a, ('wide', 'narrow'), pairs)  6.11 us
    ppermute x3, starting transfers between devices, ahead(): return lax.ppermute(a, 'wide', [(i, (i + k) % count) for i in range(count)])  4.9 us
    ppermute x2, waiting for transfers between devices, swap(): return lax.ppermute(a, ('wide', 'narrow'), pairs)  2.49 us
  transfers between devices with their start and end apart: 25, of which 13 were waited for; matrix products, arithmetic and copies ran while one was open for 2% of the time, Pallas kernels for 5%

profile of v7, /device:TPU:0, one launch (start us, length us, event | category | flops | bytes accessed | tf_op | source)
XLA Modules:
  0.0 77.9 jit_solution(18303579216490803221)
XLA Ops:
  0.0 4.0 %collective-permute-start.2 = (bf16[64,1024]{1,0:T(8,128)(2,1)}, bf16[64,1024]{1,0:T(8,128)(2,1)S(1)}, u32[]{:S(2)}, u32[]{:S(2)}) collective-permute-start(bf16[64,1024]{1,0:T(8,128)(2,1)} %param.13), channel_id=1, source_target_pairs={{0,8},{1,12},{2,10},{3,14},{4,9},{5,13},{6,11},{7,15},{8,0},{9,4},... | collective-permute-start | bytes 393224 | tf_op jit(solution)/shard_map/ppermute | solution.py:269
  4.0 1.6 %collective-permute-start = (bf16[64,1024]{1,0:T(8,128)(2,1)}, bf16[64,1024]{1,0:T(8,128)(2,1)S(1)}, u32[]{:S(2)}, u32[]{:S(2)}) collective-permute-start(bf16[64,1024]{1,0:T(8,128)(2,1)} %param.13), channel_id=1, source_target_pairs={{0,0},{1,4},{2,2},{3,6},{4,1},{5,5},{6,3},{7,7},{8,8},{9,12},{10,1... | collective-permute-start | bytes 393224 | tf_op jit(solution)/shard_map/ppermute | solution.py:269
  5.6 3.2 %collective-permute-start.4 = (bf16[64,1024]{1,0:T(8,128)(2,1)}, bf16[64,1024]{1,0:T(8,128)(2,1)S(1)}, u32[]{:S(2)}, u32[]{:S(2)}) collective-permute-start(bf16[64,1024]{1,0:T(8,128)(2,1)} %param.13), channel_id=1, source_target_pairs={{0,4},{1,0},{2,6},{3,2},{4,5},{5,1},{6,7},{7,3},{8,12},{9,8},{10,1... | collective-permute-start | bytes 393224 | tf_op jit(solution)/shard_map/ppermute | solution.py:269
  8.8 0.0 collective-permute-start.5
  8.8 1.1 %pad_maximum_fusion.refs_4_ = bf16[256,1024]{1,0:T(8,128)(2,1)S(1)} fusion(bf16[128,1024]{1,0:T(8,128)(2,1)} %bitcast.16, bf16[128,1024]{1,0:T(8,128)(2,1)} %bitcast.17), kind=kLoop, calls=%fused_computation | loop fusion | flops 1048576 | bytes 1048576 | tf_op jit(solution)/shard_map/concatenate | solution.py:281
  9.9 0.1 collective-permute-start.6
  10.0 1.4 %collective-permute-done.2.refs_2_ = bf16[64,1024]{1,0:T(8,128)(2,1)S(1)} collective-permute-done((bf16[64,1024]{1,0:T(8,128)(2,1)}, bf16[64,1024]{1,0:T(8,128)(2,1)S(1)}, u32[]{:S(2)}, u32[]{:S(2)}) %collective-permute-start.2) | collective-permute-done | bytes 131104 | tf_op jit(solution)/shard_map/ppermute | solution.py:269
  11.4 3.4 %collective-permute-start.3 = (bf16[64,1024]{1,0:T(8,128)(2,1)S(1)}, bf16[64,1024]{1,0:T(8,128)(2,1)S(1)}, u32[]{:S(2)}, u32[]{:S(2)}) collective-permute-start(bf16[64,1024]{1,0:T(8,128)(2,1)S(1)} %collective-permute-done.2.refs_2_), channel_id=1, source_target_pairs={{0,2},{1,3},{4,6},{5,7},{10,8},{11,9},{14,12},{15,13},{16,18},{17,... | collective-permute-start | bytes 393224 | tf_op jit(solution)/shard_map/ppermute | solution.py:277
  14.9 0.1 pad_add_fusion.place
  14.9 0.0 collective-permute-done.refs_0_
  15.0 0.1 collective-permute-start.13
  15.1 0.0 collective-permute-done.4.refs_1_
  15.1 3.0 %collective-permute-start.1 = (bf16[64,1024]{1,0:T(8,128)(2,1)S(1)}, bf16[64,1024]{1,0:T(8,128)(2,1)S(1)}, u32[]{:S(2)}, u32[]{:S(2)}) collective-permute-start(bf16[64,1024]{1,0:T(8,128)(2,1)S(1)} %collective-permute-done.refs_0_), channel_id=1, source_target_pairs={{0,2},{1,3},{4,6},{5,7},{10,8},{11,9},{14,12},{15,13},{16,18},{17,... | collective-permute-start | bytes 393224 | tf_op jit(solution)/shard_map/ppermute | solution.py:277
  18.1 0.0 collective-permute-done.5.refs_3_
  18.1 0.0 collective-permute-done.3
  18.1 2.2 %collective-permute-start.14 = (bf16[3,128,384]{2,1,0:T(8,128)(2,1)S(1)}, bf16[3,128,384]{2,1,0:T(8,128)(2,1)S(1)}, u32[]{:S(2)}, u32[]{:S(2)}) collective-permute-start(bf16[3,128,384]{2,1,0:T(8,128)(2,1)S(1)} %pad_maximum_fusion.1.refs_5_), channel_id=1, source_target_pairs={{0,8},{4,12},{8,0},{12,4},{16,28},{20,24},{24,20},{28,16},{1,9},{5... | collective-permute-start | bytes 884744 | tf_op jit(solution)/shard_map/ppermute | solution.py:323
  20.3 0.8 %collective-permute-done.1 = bf16[64,1024]{1,0:T(8,128)(2,1)S(1)} collective-permute-done((bf16[64,1024]{1,0:T(8,128)(2,1)S(1)}, bf16[64,1024]{1,0:T(8,128)(2,1)S(1)}, u32[]{:S(2)}, u32[]{:S(2)}) %collective-permute-start.1) | collective-permute-done | bytes 131104 | tf_op jit(solution)/shard_map/ppermute | solution.py:277
  21.2 0.0 collective-permute-done.6.refs_5_
  21.2 0.0 copy-start.7
  21.2 0.0 copy-start.1
  21.2 1.0 %shard_map.127 = (f32[128,256]{1,0:T(8,128)S(1)}, bf16[128,256]{1,0:T(8,128)(2,1)S(1)}) custom-call(s32[3]{0:T(128)S(1)} %pad_add_fusion.place, bf16[64,1024]{1,0:T(8,128)(2,1)S(1)} %collective-permute-done.refs_0_, bf16[64,1024]{1,0:T(8,128)(2,1)S(1)} %collective-permute-done.4.refs_1_, bf16[64,1024]{1,0:T(8,128)(2,1)S(1)} %collective-permute-done.2.refs_2_, ...), custom_call_target="tpu_custom_call" | custom-call | tf_op jit(solution)/shard_map/pallas_call | solution.py:284
  22.2 0.0 copy-start
  22.2 2.5 %collective-permute-start.8 = (bf16[128,256]{1,0:T(8,128)(2,1)S(1)}, bf16[128,256]{1,0:T(8,128)(2,1)S(1)}, u32[]{:S(2)}, u32[]{:S(2)}) collective-permute-start(bf16[128,256]{1,0:T(8,128)(2,1)S(1)} %get-tuple-element.25), channel_id=1, source_target_pairs={{0,2},{1,3},{2,0},{3,1},{4,6},{5,7},{6,4},{7,5},{8,10},{9,11},{10,... | collective-permute-start | bytes 196616 | tf_op jit(solution)/shard_map/ppermute | solution.py:257
  24.8 0.1 collective-permute-start.7
  24.9 2.1 %collective-permute-done.8 = bf16[128,256]{1,0:T(8,128)(2,1)S(1)} collective-permute-done((bf16[128,256]{1,0:T(8,128)(2,1)S(1)}, bf16[128,256]{1,0:T(8,128)(2,1)S(1)}, u32[]{:S(2)}, u32[]{:S(2)}) %collective-permute-start.8) | collective-permute-done | bytes 65568 | tf_op jit(solution)/shard_map/ppermute | solution.py:257
  27.0 0.1 collective-permute-start.9
  27.1 0.5 copy-done.9
  27.7 0.1 select_reduce_fusion.1
  27.8 0.6 collective-permute-done.9.refs_3_
  28.4 0.0 collective-permute-done.7.refs_1_
  28.4 1.4 %shard_map.128 = (f32[64,1024]{1,0:T(8,128)S(1)}, bf16[64,1024]{1,0:T(8,128)(2,1)S(1)}, bf16[64,1024]{1,0:T(8,128)(2,1)S(1)}, bf16[64,1024]{1,0:T(8,128)(2,1)S(1)}) custom-call(s32[3]{0:T(128)S(1)} %pad_add_fusion.place, bf16[128,1024]{1,0:T(8,128)(2,1)S(1)} %pad_maximum_fusion.2.refs_0_, bf16[128,1024]{1,0:T(8,128)(2,1)S(1)} %collective-permute-done.7.refs_1_, ...), custom_call_target="tpu_custom_call" | custom-call | tf_op jit(solution)/shard_map/pallas_call | solution.py:295
  29.8 1.1 %collective-permute-start.10 = (bf16[64,1024]{1,0:T(8,128)(2,1)S(1)}, bf16[64,1024]{1,0:T(8,128)(2,1)S(1)}, u32[]{:S(2)}, u32[]{:S(2)}) collective-permute-start(bf16[64,1024]{1,0:T(8,128)(2,1)S(1)} %get-tuple-element.29), channel_id=1, source_target_pairs={{0,4},{4,0},{8,12},{12,8},{1,5},{5,1},{9,13},{13,9},{2,6},{6,2},{1... | collective-permute-start | bytes 393224 | tf_op jit(solution)/shard_map/ppermute | solution.py:257
  30.9 1.6 %collective-permute-start.11 = (bf16[64,1024]{1,0:T(8,128)(2,1)S(1)}, bf16[64,1024]{1,0:T(8,128)(2,1)S(1)}, u32[]{:S(2)}, u32[]{:S(2)}) collective-permute-start(bf16[64,1024]{1,0:T(8,128)(2,1)S(1)} %get-tuple-element.30), channel_id=1, source_target_pairs={{0,8},{4,12},{8,0},{12,4},{1,9},{5,13},{9,1},{13,5},{2,10},{6,14},... | collective-permute-start | bytes 393224 | tf_op jit(solution)/shard_map/ppermute | solution.py:257
  32.4 1.8 %collective-permute-start.12 = (bf16[64,1024]{1,0:T(8,128)(2,1)S(1)}, bf16[64,1024]{1,0:T(8,128)(2,1)S(1)}, u32[]{:S(2)}, u32[]{:S(2)}) collective-permute-start(bf16[64,1024]{1,0:T(8,128)(2,1)S(1)} %get-tuple-element.31), channel_id=1, source_target_pairs={{0,12},{4,8},{8,4},{12,0},{1,13},{5,9},{9,5},{13,1},{2,14},{6,10},... | collective-permute-start | bytes 393224 | tf_op jit(solution)/shard_map/ppermute | solution.py:257
  34.2 0.1 collective-permute-done.14.refs_7_
  34.3 1.4 %collective-permute-start.15 = (bf16[3,128,384]{2,1,0:T(8,128)(2,1)S(1)}, bf16[3,128,384]{2,1,0:T(8,128)(2,1)S(1)}, u32[]{:S(2)}, u32[]{:S(2)}) collective-permute-start(bf16[3,128,384]{2,1,0:T(8,128)(2,1)S(1)} %collective-permute-done.14.refs_7_), channel_id=1, source_target_pairs={{0,16},{16,0},{1,17},{17,1},{2,18},{18,2},{3,19},{19,3},{4,20},{20... | collective-permute-start | bytes 884744 | tf_op jit(solution)/shard_map/ppermute | solution.py:324
  35.8 0.1 copy.16.refs_4_.weight
  35.9 0.0 collective-permute-done.13.refs_6_
  35.9 3.6 %collective-permute-done.10.refs_1_ = bf16[64,1024]{1,0:T(8,128)(2,1)S(1)} collective-permute-done((bf16[64,1024]{1,0:T(8,128)(2,1)S(1)}, bf16[64,1024]{1,0:T(8,128)(2,1)S(1)}, u32[]{:S(2)}, u32[]{:S(2)}) %collective-permute-start.10) | collective-permute-done | bytes 131104 | tf_op jit(solution)/shard_map/ppermute | solution.py:257
  39.5 4.3 %collective-permute-done.11.refs_2_ = bf16[64,1024]{1,0:T(8,128)(2,1)S(1)} collective-permute-done((bf16[64,1024]{1,0:T(8,128)(2,1)S(1)}, bf16[64,1024]{1,0:T(8,128)(2,1)S(1)}, u32[]{:S(2)}, u32[]{:S(2)}) %collective-permute-start.11) | collective-permute-done | bytes 131104 | tf_op jit(solution)/shard_map/ppermute | solution.py:257
  43.8 0.0 collective-permute-done.12.refs_3_
  43.8 1.6 %shard_map.129 = (f32[64,768]{1,0:T(8,128)S(1)}, f32[64,384]{1,0:T(8,128)S(1)}, f32[4,64,128]{2,1,0:T(8,128)S(1)}, bf16[4,64,256]{2,1,0:T(8,128)(2,1)S(1)}) custom-call(s32[3]{0:T(128)S(1)} %pad_add_fusion.place, f32[64,1024]{1,0:T(8,128)S(1)} %get-tuple-element.28.refs_0_, bf16[64,1024]{1,0:T(8,128)(2,1)S(1)} %collective-permute-done.10.refs_1_, ...), custom_call_target="tpu_custom_call" | custom-call | tf_op jit(solution)/shard_map/pallas_call | solution.py:336
  45.4 0.0 copy-start.2
  45.4 1.0 %shard_map.130 = (bf16[64,384]{1,0:T(8,128)(2,1)S(1)}, f32[64,256]{1,0:T(8,128)S(1)}, bf16[64,256]{1,0:T(8,128)(2,1)S(1)}) custom-call(s32[3]{0:T(128)S(1)} %pad_add_fusion.place, f32[64,768]{1,0:T(8,128)S(1)} %get-tuple-element.33.base, f32[64,384]{1,0:T(8,128)S(1)} %get-tuple-element.34.acc, f32[4,64,128]{2,1,0:T(8,128)S(1)} %get-tuple-element.35.come, ...), custom_call_target="tpu_custom_call" | custom-call | tf_op jit(solution)/shard_map/pallas_call | solution.py:348
  46.4 0.1 collective-permute-start.16
  46.5 1.2 %collective-permute-done.16 = bf16[64,256]{1,0:T(8,128)(2,1)S(1)} collective-permute-done((bf16[64,256]{1,0:T(8,128)(2,1)S(1)}, bf16[64,256]{1,0:T(8,128)(2,1)S(1)}, u32[]{:S(2)}, u32[]{:S(2)}) %collective-permute-start.16) | collective-permute-done | bytes 32800 | tf_op jit(solution)/shard_map/ppermute | solution.py:257
  47.7 0.0 copy-start.3
  47.7 0.8 %collective-permute-start.17 = (bf16[64,512]{1,0:T(8,128)(2,1)S(1)}, bf16[64,512]{1,0:T(8,128)(2,1)S(1)}, u32[]{:S(2)}, u32[]{:S(2)}) collective-permute-start(bf16[64,512]{1,0:T(8,128)(2,1)S(1)} %pad_maximum_fusion.3), channel_id=1, source_target_pairs={{0,0},{1,4},{2,8},{3,12},{4,1},{5,5},{6,9},{7,13},{8,2},{9,6},{10,... | collective-permute-start | bytes 196616 | tf_op jit(solution)/shard_map/ppermute | solution.py:254
  48.5 5.3 %collective-permute-start.18 = (bf16[64,128]{1,0:T(8,128)(2,1)S(1)}, bf16[64,128]{1,0:T(8,128)(2,1)S(1)}, u32[]{:S(2)}, u32[]{:S(2)}) collective-permute-start(bf16[64,128]{1,0:T(8,128)(2,1)S(1)} %get-tuple-element.46), channel_id=1, source_target_pairs={{0,8},{1,12},{2,0},{3,4},{4,9},{5,13},{6,1},{7,5},{8,10},{9,14},{1... | collective-permute-start | bytes 49160 | tf_op jit(solution)/shard_map/ppermute | solution.py:254
  53.9 0.0 collective-permute-done.17
  53.9 2.5 %collective-permute-done.18 = bf16[64,128]{1,0:T(8,128)(2,1)S(1)} collective-permute-done((bf16[64,128]{1,0:T(8,128)(2,1)S(1)}, bf16[64,128]{1,0:T(8,128)(2,1)S(1)}, u32[]{:S(2)}, u32[]{:S(2)}) %collective-permute-start.18) | collective-permute-done | bytes 16416 | tf_op jit(solution)/shard_map/ppermute | solution.py:254
  56.4 3.0 %collective-permute-start.19 = (bf16[64,512]{1,0:T(8,128)(2,1)S(1)}, bf16[64,512]{1,0:T(8,128)(2,1)S(1)}, u32[]{:S(2)}, u32[]{:S(2)}) collective-permute-start(bf16[64,512]{1,0:T(8,128)(2,1)S(1)} %pad_maximum_fusion.4.refs_0_), channel_id=1, source_target_pairs={{0,2},{1,3},{2,0},{3,1},{4,6},{5,7},{6,4},{7,5},{8,10},{9,11},{10,... | collective-permute-start | bytes 196616 | tf_op jit(solution)/shard_map/ppermute | solution.py:257
  59.4 2.2 %collective-permute-done.19.refs_1_ = bf16[64,512]{1,0:T(8,128)(2,1)S(1)} collective-permute-done((bf16[64,512]{1,0:T(8,128)(2,1)S(1)}, bf16[64,512]{1,0:T(8,128)(2,1)S(1)}, u32[]{:S(2)}, u32[]{:S(2)}) %collective-permute-start.19) | collective-permute-done | bytes 65568 | tf_op jit(solution)/shard_map/ppermute | solution.py:257
  61.6 0.0 collective-permute-start.21
  61.6 0.0 collective-permute-done.20.refs_2_
  61.6 1.2 %collective-permute-done.21.refs_3_ = bf16[64,512]{1,0:T(8,128)(2,1)S(1)} collective-permute-done((bf16[64,512]{1,0:T(8,128)(2,1)S(1)}, bf16[64,512]{1,0:T(8,128)(2,1)S(1)}, u32[]{:S(2)}, u32[]{:S(2)}) %collective-permute-start.21) | collective-permute-done | bytes 65568 | tf_op jit(solution)/shard_map/ppermute | solution.py:257
  62.9 1.2 %shard_map.131 = (f32[64,1024]{1,0:T(8,128)S(1)}, bf16[64,1024]{1,0:T(8,128)(2,1)S(1)}, bf16[64,1024]{1,0:T(8,128)(2,1)S(1)}, bf16[64,1024]{1,0:T(8,128)(2,1)S(1)}) custom-call(s32[3]{0:T(128)S(1)} %pad_add_fusion.place, bf16[64,512]{1,0:T(8,128)(2,1)S(1)} %pad_maximum_fusion.4.refs_0_, bf16[64,512]{1,0:T(8,128)(2,1)S(1)} %collective-permute-done.19.refs_1_, ...), custom_call_target="tpu_custom_call" | custom-call | tf_op jit(solution)/shard_map/pallas_call | solution.py:368
  64.0 1.0 %collective-permute-start.22 = (bf16[64,1024]{1,0:T(8,128)(2,1)S(1)}, bf16[64,1024]{1,0:T(8,128)(2,1)S(1)}, u32[]{:S(2)}, u32[]{:S(2)}) collective-permute-start(bf16[64,1024]{1,0:T(8,128)(2,1)S(1)} %get-tuple-element.42), channel_id=1, source_target_pairs={{0,4},{4,8},{8,12},{12,0},{1,5},{5,9},{9,13},{13,1},{2,6},{6,10},{... | collective-permute-start | bytes 393224 | tf_op jit(solution)/shard_map/ppermute | solution.py:260
  65.0 2.1 %collective-permute-start.23 = (bf16[64,1024]{1,0:T(8,128)(2,1)S(1)}, bf16[64,1024]{1,0:T(8,128)(2,1)S(1)}, u32[]{:S(2)}, u32[]{:S(2)}) collective-permute-start(bf16[64,1024]{1,0:T(8,128)(2,1)S(1)} %get-tuple-element.43), channel_id=1, source_target_pairs={{0,8},{4,12},{8,0},{12,4},{1,9},{5,13},{9,1},{13,5},{2,10},{6,14},... | collective-permute-start | bytes 393224 | tf_op jit(solution)/shard_map/ppermute | solution.py:260
  67.1 1.9 %collective-permute-start.24 = (bf16[64,1024]{1,0:T(8,128)(2,1)S(1)}, bf16[64,1024]{1,0:T(8,128)(2,1)S(1)}, u32[]{:S(2)}, u32[]{:S(2)}) collective-permute-start(bf16[64,1024]{1,0:T(8,128)(2,1)S(1)} %get-tuple-element.44), channel_id=1, source_target_pairs={{0,12},{4,0},{8,4},{12,8},{1,13},{5,1},{9,5},{13,9},{2,14},{6,2},{... | collective-permute-start | bytes 393224 | tf_op jit(solution)/shard_map/ppermute | solution.py:260
  68.9 3.4 %collective-permute-done.22 = bf16[64,1024]{1,0:T(8,128)(2,1)S(1)} collective-permute-done((bf16[64,1024]{1,0:T(8,128)(2,1)S(1)}, bf16[64,1024]{1,0:T(8,128)(2,1)S(1)}, u32[]{:S(2)}, u32[]{:S(2)}) %collective-permute-start.22) | collective-permute-done | bytes 131104 | tf_op jit(solution)/shard_map/ppermute | solution.py:260
  72.3 4.8 %collective-permute-done.23 = bf16[64,1024]{1,0:T(8,128)(2,1)S(1)} collective-permute-done((bf16[64,1024]{1,0:T(8,128)(2,1)S(1)}, bf16[64,1024]{1,0:T(8,128)(2,1)S(1)}, u32[]{:S(2)}, u32[]{:S(2)}) %collective-permute-start.23) | collective-permute-done | bytes 131104 | tf_op jit(solution)/shard_map/ppermute | solution.py:260
  77.2 0.0 collective-permute-done.24
  77.2 0.7 add_convert_fusion
  (29 shorter events, 0.2 us)
Async XLA Ops:
  0.0 11.4 %collective-permute-start.2 = (bf16[64,1024]{1,0:T(8,128)(2,1)}, bf16[64,1024]{1,0:T(8,128)(2,1)S(1)}, u32[]{:S(2)}, u32[]{:S(2)}) collective-permute-start(bf16[64,1024]{1,0:T(8,128)(2,1)} %param.13), channel_id=1, source_target_pairs={{0,8},{1,12},{2,10},{3,14},{4,9},{5,13},{6,11},{7,15},{8,0},{9,4},... | collective-permute-start | bytes 393224 | tf_op jit(solution)/shard_map/ppermute | solution.py:269
  4.0 10.9 %collective-permute-start = (bf16[64,1024]{1,0:T(8,128)(2,1)}, bf16[64,1024]{1,0:T(8,128)(2,1)S(1)}, u32[]{:S(2)}, u32[]{:S(2)}) collective-permute-start(bf16[64,1024]{1,0:T(8,128)(2,1)} %param.13), channel_id=1, source_target_pairs={{0,0},{1,4},{2,2},{3,6},{4,1},{5,5},{6,3},{7,7},{8,8},{9,12},{10,1... | collective-permute-start | bytes 393224 | tf_op jit(solution)/shard_map/ppermute | solution.py:269
  5.6 9.5 %collective-permute-start.4 = (bf16[64,1024]{1,0:T(8,128)(2,1)}, bf16[64,1024]{1,0:T(8,128)(2,1)S(1)}, u32[]{:S(2)}, u32[]{:S(2)}) collective-permute-start(bf16[64,1024]{1,0:T(8,128)(2,1)} %param.13), channel_id=1, source_target_pairs={{0,4},{1,0},{2,6},{3,2},{4,5},{5,1},{6,7},{7,3},{8,12},{9,8},{10,1... | collective-permute-start | bytes 393224 | tf_op jit(solution)/shard_map/ppermute | solution.py:269
  8.8 9.3 %collective-permute-start.5 = (bf16[64,1024]{1,0:T(8,128)(2,1)}, bf16[64,1024]{1,0:T(8,128)(2,1)S(1)}, u32[]{:S(2)}, u32[]{:S(2)}) collective-permute-start(bf16[64,1024]{1,0:T(8,128)(2,1)} %param.13), channel_id=1, source_target_pairs={{0,12},{1,8},{2,14},{3,10},{4,13},{5,9},{6,15},{7,11},{8,4},{9,0},... | collective-permute-start | bytes 393224 | tf_op jit(solution)/shard_map/ppermute | solution.py:269
  8.8 6.0 %copy-start.4 = (bf16[4,384,32]{1,2,0:T(8,128)(2,1)S(1)}, bf16[4,384,32]{1,2,0:T(8,128)(2,1)}, u32[]{:S(2)}) copy-start(bf16[4,384,32]{1,2,0:T(8,128)(2,1)} %param.24) | copy-start | bytes 294916
  8.8 6.0 %copy-start.5 = (bf16[4,32,384]{2,1,0:T(8,128)(2,1)S(1)}, bf16[4,32,384]{2,1,0:T(8,128)(2,1)}, u32[]{:S(2)}) copy-start(bf16[4,32,384]{2,1,0:T(8,128)(2,1)} %param.23) | copy-start | bytes 294916
  8.8 6.0 %copy-start.6 = (bf16[4,32,384]{2,1,0:T(8,128)(2,1)S(1)}, bf16[4,32,384]{2,1,0:T(8,128)(2,1)}, u32[]{:S(2)}) copy-start(bf16[4,32,384]{2,1,0:T(8,128)(2,1)} %param.21) | copy-start | bytes 294916
  9.9 11.3 %collective-permute-start.6 = (bf16[256,1024]{1,0:T(8,128)(2,1)S(1)}, bf16[256,1024]{1,0:T(8,128)(2,1)S(1)}, u32[]{:S(2)}, u32[]{:S(2)}) collective-permute-start(bf16[256,1024]{1,0:T(8,128)(2,1)S(1)} %pad_maximum_fusion.refs_4_), channel_id=1, source_target_pairs={{0,1},{1,0},{2,3},{3,2},{4,5},{5,4},{6,7},{7,6},{8,9},{9,8},{10,11... | collective-permute-start | bytes 1572872 | tf_op jit(solution)/shard_map/ppermute | solution.py:257
  11.4 6.7 %collective-permute-start.3 = (bf16[64,1024]{1,0:T(8,128)(2,1)S(1)}, bf16[64,1024]{1,0:T(8,128)(2,1)S(1)}, u32[]{:S(2)}, u32[]{:S(2)}) collective-permute-start(bf16[64,1024]{1,0:T(8,128)(2,1)S(1)} %collective-permute-done.2.refs_2_), channel_id=1, source_target_pairs={{0,2},{1,3},{4,6},{5,7},{10,8},{11,9},{14,12},{15,13},{16,18},{17,... | collective-permute-start | bytes 393224 | tf_op jit(solution)/shard_map/ppermute | solution.py:277
  15.0 20.9 %collective-permute-start.13 = (bf16[3,128,384]{2,1,0:T(8,128)(2,1)S(1)}, bf16[3,128,384]{2,1,0:T(8,128)(2,1)S(1)}, u32[]{:S(2)}, u32[]{:S(2)}) collective-permute-start(bf16[3,128,384]{2,1,0:T(8,128)(2,1)S(1)} %pad_maximum_fusion.1.refs_5_), channel_id=1, source_target_pairs={{0,4},{4,0},{8,12},{12,8},{1,5},{5,1},{9,13},{13,9},{2,6},{6,2},{1... | collective-permute-start | bytes 884744 | tf_op jit(solution)/shard_map/ppermute | solution.py:257
  15.1 6.0 %collective-permute-start.1 = (bf16[64,1024]{1,0:T(8,128)(2,1)S(1)}, bf16[64,1024]{1,0:T(8,128)(2,1)S(1)}, u32[]{:S(2)}, u32[]{:S(2)}) collective-permute-start(bf16[64,1024]{1,0:T(8,128)(2,1)S(1)} %collective-permute-done.refs_0_), channel_id=1, source_target_pairs={{0,2},{1,3},{4,6},{5,7},{10,8},{11,9},{14,12},{15,13},{16,18},{17,... | collective-permute-start | bytes 393224 | tf_op jit(solution)/shard_map/ppermute | solution.py:277
  18.1 16.2 %collective-permute-start.14 = (bf16[3,128,384]{2,1,0:T(8,128)(2,1)S(1)}, bf16[3,128,384]{2,1,0:T(8,128)(2,1)S(1)}, u32[]{:S(2)}, u32[]{:S(2)}) collective-permute-start(bf16[3,128,384]{2,1,0:T(8,128)(2,1)S(1)} %pad_maximum_fusion.1.refs_5_), channel_id=1, source_target_pairs={{0,8},{4,12},{8,0},{12,4},{16,28},{20,24},{24,20},{28,16},{1,9},{5... | collective-permute-start | bytes 884744 | tf_op jit(solution)/shard_map/ppermute | solution.py:323
  21.2 6.0 %copy-start.7 = (s32[64,8]{0,1:T(8,128)S(1)}, s32[64,8]{0,1:T(8,128)}, u32[]{:S(2)}) copy-start(s32[64,8]{0,1:T(8,128)} %param.14) | copy-start | bytes 6148
  21.2 7.2 %copy-start.1 = (bf16[1024,384]{1,0:T(8,128)(2,1)S(1)}, bf16[1024,384]{1,0:T(8,128)(2,1)}, u32[]{:S(2)}) copy-start(bf16[1024,384]{1,0:T(8,128)(2,1)} %refs_5_.1) | copy-start | bytes 2359300
  22.2 6.2 %copy-start = (bf16[1024,384]{1,0:T(8,128)(2,1)S(1)}, bf16[1024,384]{1,0:T(8,128)(2,1)}, u32[]{:S(2)}) copy-start(bf16[1024,384]{1,0:T(8,128)(2,1)} %refs_4_.2) | copy-start | bytes 2359300
  22.2 4.8 %collective-permute-start.8 = (bf16[128,256]{1,0:T(8,128)(2,1)S(1)}, bf16[128,256]{1,0:T(8,128)(2,1)S(1)}, u32[]{:S(2)}, u32[]{:S(2)}) collective-permute-start(bf16[128,256]{1,0:T(8,128)(2,1)S(1)} %get-tuple-element.25), channel_id=1, source_target_pairs={{0,2},{1,3},{2,0},{3,1},{4,6},{5,7},{6,4},{7,5},{8,10},{9,11},{10,... | collective-permute-start | bytes 196616 | tf_op jit(solution)/shard_map/ppermute | solution.py:257
  24.8 3.6 %collective-permute-start.7 = (bf16[128,1024]{1,0:T(8,128)(2,1)S(1)}, bf16[128,1024]{1,0:T(8,128)(2,1)S(1)}, u32[]{:S(2)}, u32[]{:S(2)}) collective-permute-start(bf16[128,1024]{1,0:T(8,128)(2,1)S(1)} %pad_maximum_fusion.2.refs_0_), channel_id=1, source_target_pairs={{0,1},{1,0},{2,3},{3,2},{4,5},{5,4},{6,7},{7,6},{8,9},{9,8},{10,11... | collective-permute-start | bytes 786440 | tf_op jit(solution)/shard_map/ppermute | solution.py:257
  27.0 0.7 copy-start.9
  27.0 1.3 %collective-permute-start.9 = (bf16[128,256]{1,0:T(8,128)(2,1)S(1)}, bf16[128,256]{1,0:T(8,128)(2,1)S(1)}, u32[]{:S(2)}, u32[]{:S(2)}) collective-permute-start(bf16[128,256]{1,0:T(8,128)(2,1)S(1)} %add_convert_fusion.1.refs_2_), channel_id=1, source_target_pairs={{0,1},{1,0},{2,3},{3,2},{4,5},{5,4},{6,7},{7,6},{8,9},{9,8},{10,11... | collective-permute-start | bytes 196616 | tf_op jit(solution)/shard_map/ppermute | solution.py:257
  29.8 9.7 %collective-permute-start.10 = (bf16[64,1024]{1,0:T(8,128)(2,1)S(1)}, bf16[64,1024]{1,0:T(8,128)(2,1)S(1)}, u32[]{:S(2)}, u32[]{:S(2)}) collective-permute-start(bf16[64,1024]{1,0:T(8,128)(2,1)S(1)} %get-tuple-element.29), channel_id=1, source_target_pairs={{0,4},{4,0},{8,12},{12,8},{1,5},{5,1},{9,13},{13,9},{2,6},{6,2},{1... | collective-permute-start | bytes 393224 | tf_op jit(solution)/shard_map/ppermute | solution.py:257
  30.9 12.9 %collective-permute-start.11 = (bf16[64,1024]{1,0:T(8,128)(2,1)S(1)}, bf16[64,1024]{1,0:T(8,128)(2,1)S(1)}, u32[]{:S(2)}, u32[]{:S(2)}) collective-permute-start(bf16[64,1024]{1,0:T(8,128)(2,1)S(1)} %get-tuple-element.30), channel_id=1, source_target_pairs={{0,8},{4,12},{8,0},{12,4},{1,9},{5,13},{9,1},{13,5},{2,10},{6,14},... | collective-permute-start | bytes 393224 | tf_op jit(solution)/shard_map/ppermute | solution.py:257
  32.4 11.3 %collective-permute-start.12 = (bf16[64,1024]{1,0:T(8,128)(2,1)S(1)}, bf16[64,1024]{1,0:T(8,128)(2,1)S(1)}, u32[]{:S(2)}, u32[]{:S(2)}) collective-permute-start(bf16[64,1024]{1,0:T(8,128)(2,1)S(1)} %get-tuple-element.31), channel_id=1, source_target_pairs={{0,12},{4,8},{8,4},{12,0},{1,13},{5,9},{9,5},{13,1},{2,14},{6,10},... | collective-permute-start | bytes 393224 | tf_op jit(solution)/shard_map/ppermute | solution.py:257
  34.3 1.4 %copy-start.8 = (f32[64,8]{0,1:T(8,128)S(1)}, f32[64,8]{0,1:T(8,128)}, u32[]{:S(2)}) copy-start(f32[64,8]{0,1:T(8,128)} %param.15) | copy-start | bytes 6148
  34.3 11.1 %collective-permute-start.15 = (bf16[3,128,384]{2,1,0:T(8,128)(2,1)S(1)}, bf16[3,128,384]{2,1,0:T(8,128)(2,1)S(1)}, u32[]{:S(2)}, u32[]{:S(2)}) collective-permute-start(bf16[3,128,384]{2,1,0:T(8,128)(2,1)S(1)} %collective-permute-done.14.refs_7_), channel_id=1, source_target_pairs={{0,16},{16,0},{1,17},{17,1},{2,18},{18,2},{3,19},{19,3},{4,20},{20... | collective-permute-start | bytes 884744 | tf_op jit(solution)/shard_map/ppermute | solution.py:324
  45.4 17.5 %copy-start.2 = (bf16[384,1024]{1,0:T(8,128)(2,1)S(1)}, bf16[384,1024]{1,0:T(8,128)(2,1)}, u32[]{:S(2)}) copy-start(bf16[384,1024]{1,0:T(8,128)(2,1)} %refs_4_.3) | copy-start | bytes 2359300
  46.4 1.3 %collective-permute-start.16 = (bf16[64,256]{1,0:T(8,128)(2,1)S(1)}, bf16[64,256]{1,0:T(8,128)(2,1)S(1)}, u32[]{:S(2)}, u32[]{:S(2)}) collective-permute-start(bf16[64,256]{1,0:T(8,128)(2,1)S(1)} %get-tuple-element.40), channel_id=1, source_target_pairs={{0,1},{1,0},{2,3},{3,2},{4,5},{5,4},{6,7},{7,6},{8,9},{9,8},{10,11... | collective-permute-start | bytes 98312 | tf_op jit(solution)/shard_map/ppermute | solution.py:257
  47.7 15.2 %copy-start.3 = (bf16[4,32,1024]{2,1,0:T(8,128)(2,1)S(1)}, bf16[4,32,1024]{2,1,0:T(8,128)(2,1)}, u32[]{:S(2)}) copy-start(bf16[4,32,1024]{2,1,0:T(8,128)(2,1)} %param.25) | copy-start | bytes 786436
  47.7 6.1 %collective-permute-start.17 = (bf16[64,512]{1,0:T(8,128)(2,1)S(1)}, bf16[64,512]{1,0:T(8,128)(2,1)S(1)}, u32[]{:S(2)}, u32[]{:S(2)}) collective-permute-start(bf16[64,512]{1,0:T(8,128)(2,1)S(1)} %pad_maximum_fusion.3), channel_id=1, source_target_pairs={{0,0},{1,4},{2,8},{3,12},{4,1},{5,5},{6,9},{7,13},{8,2},{9,6},{10,... | collective-permute-start | bytes 196616 | tf_op jit(solution)/shard_map/ppermute | solution.py:254
  48.5 7.8 %collective-permute-start.18 = (bf16[64,128]{1,0:T(8,128)(2,1)S(1)}, bf16[64,128]{1,0:T(8,128)(2,1)S(1)}, u32[]{:S(2)}, u32[]{:S(2)}) collective-permute-start(bf16[64,128]{1,0:T(8,128)(2,1)S(1)} %get-tuple-element.46), channel_id=1, source_target_pairs={{0,8},{1,12},{2,0},{3,4},{4,9},{5,13},{6,1},{7,5},{8,10},{9,14},{1... | collective-permute-start | bytes 49160 | tf_op jit(solution)/shard_map/ppermute | solution.py:254
  56.4 5.2 %collective-permute-start.19 = (bf16[64,512]{1,0:T(8,128)(2,1)S(1)}, bf16[64,512]{1,0:T(8,128)(2,1)S(1)}, u32[]{:S(2)}, u32[]{:S(2)}) collective-permute-start(bf16[64,512]{1,0:T(8,128)(2,1)S(1)} %pad_maximum_fusion.4.refs_0_), channel_id=1, source_target_pairs={{0,2},{1,3},{2,0},{3,1},{4,6},{5,7},{6,4},{7,5},{8,10},{9,11},{10,... | collective-permute-start | bytes 196616 | tf_op jit(solution)/shard_map/ppermute | solution.py:257
  59.4 2.3 %collective-permute-start.20 = (bf16[64,512]{1,0:T(8,128)(2,1)S(1)}, bf16[64,512]{1,0:T(8,128)(2,1)S(1)}, u32[]{:S(2)}, u32[]{:S(2)}) collective-permute-start(bf16[64,512]{1,0:T(8,128)(2,1)S(1)} %pad_maximum_fusion.4.refs_0_), channel_id=1, source_target_pairs={{0,1},{1,0},{2,3},{3,2},{4,5},{5,4},{6,7},{7,6},{8,9},{9,8},{10,11... | collective-permute-start | bytes 196616 | tf_op jit(solution)/shard_map/ppermute | solution.py:257
  61.6 1.3 %collective-permute-start.21 = (bf16[64,512]{1,0:T(8,128)(2,1)S(1)}, bf16[64,512]{1,0:T(8,128)(2,1)S(1)}, u32[]{:S(2)}, u32[]{:S(2)}) collective-permute-start(bf16[64,512]{1,0:T(8,128)(2,1)S(1)} %collective-permute-done.19.refs_1_), channel_id=1, source_target_pairs={{0,1},{1,0},{2,3},{3,2},{4,5},{5,4},{6,7},{7,6},{8,9},{9,8},{10,11... | collective-permute-start | bytes 196616 | tf_op jit(solution)/shard_map/ppermute | solution.py:257
  64.0 8.3 %collective-permute-start.22 = (bf16[64,1024]{1,0:T(8,128)(2,1)S(1)}, bf16[64,1024]{1,0:T(8,128)(2,1)S(1)}, u32[]{:S(2)}, u32[]{:S(2)}) collective-permute-start(bf16[64,1024]{1,0:T(8,128)(2,1)S(1)} %get-tuple-element.42), channel_id=1, source_target_pairs={{0,4},{4,8},{8,12},{12,0},{1,5},{5,9},{9,13},{13,1},{2,6},{6,10},{... | collective-permute-start | bytes 393224 | tf_op jit(solution)/shard_map/ppermute | solution.py:260
  65.0 12.2 %collective-permute-start.23 = (bf16[64,1024]{1,0:T(8,128)(2,1)S(1)}, bf16[64,1024]{1,0:T(8,128)(2,1)S(1)}, u32[]{:S(2)}, u32[]{:S(2)}) collective-permute-start(bf16[64,1024]{1,0:T(8,128)(2,1)S(1)} %get-tuple-element.43), channel_id=1, source_target_pairs={{0,8},{4,12},{8,0},{12,4},{1,9},{5,13},{9,1},{13,5},{2,10},{6,14},... | collective-permute-start | bytes 393224 | tf_op jit(solution)/shard_map/ppermute | solution.py:260
  67.1 10.1 %collective-permute-start.24 = (bf16[64,1024]{1,0:T(8,128)(2,1)S(1)}, bf16[64,1024]{1,0:T(8,128)(2,1)S(1)}, u32[]{:S(2)}, u32[]{:S(2)}) collective-permute-start(bf16[64,1024]{1,0:T(8,128)(2,1)S(1)} %get-tuple-element.44), channel_id=1, source_target_pairs={{0,12},{4,0},{8,4},{12,8},{1,13},{5,1},{9,5},{13,9},{2,14},{6,2},{... | collective-permute-start | bytes 393224 | tf_op jit(solution)/shard_map/ppermute | solution.py:260
